TPU v7x, 128 devices: a whole 4x4x4 slice. The times are simulated.
128 devices in a mesh: section: 2 (over core), fsdp: 8 (over z, y_lo), dp: 8 (over x, y_hi).
Axes of the slice: x: 4, y: 4 (y_hi: 2, y_lo: 2; y = y_hi * 2 + y_lo), z: 4, core: 2. Of those that a mesh axis runs over, the one named last changes fastest.
Arguments:
- boundary: bfloat16 [2, 2, 8, 1024, 960], P('section', None, 'dp', 'fsdp'), may hold values from -6 to 6
- lengths: int32 [8, 2, 4], P('dp'), may hold values from 0 to 1024, as said below
- query_weight: bfloat16 [2, 960, 960], P('section', 'fsdp'), may hold values from -0.1875 to 0.1875
- key_matrix: bfloat16 [2, 960, 320], P('section', 'fsdp'), may hold values from -0.1875 to 0.1875
- value_matrix: bfloat16 [2, 960, 320], P('section', 'fsdp'), may hold values from -0.1875 to 0.1875
- output_weight: bfloat16 [2, 960, 960], P('section', 'fsdp'), may hold values from -0.75 to 0.75
- gate_weight: bfloat16 [2, 960, 2560], P('section', 'fsdp'), may hold values from -0.1875 to 0.1875
- up_weight: bfloat16 [2, 960, 2560], P('section', 'fsdp'), may hold values from -0.1875 to 0.1875
- down_weight: bfloat16 [2, 2560, 960], P('section', 'fsdp'), may hold values from -0.125 to 0.125
- first_gain: bfloat16 [2, 960], P('section', 'fsdp'), may hold values from 0.099609375 to 1.8984375
- second_gain: bfloat16 [2, 960], P('section', 'fsdp'), may hold values from 0.099609375 to 1.8984375
Outputs:
- boundary_out: bfloat16 [2, 2, 8, 1024, 960], P('section', None, 'dp', 'fsdp')
- query_grad: float32 [2, 960, 960], P('section', 'fsdp')
- key_grad: float32 [2, 960, 320], P('section', 'fsdp')
- value_grad: float32 [2, 960, 320], P('section', 'fsdp')
- output_grad: float32 [2, 960, 960], P('section', 'fsdp')
- gate_grad: float32 [2, 960, 2560], P('section', 'fsdp')
- up_grad: float32 [2, 960, 2560], P('section', 'fsdp')
- down_grad: float32 [2, 2560, 960], P('section', 'fsdp')
- first_gain_grad: float32 [2, 960], P('section', 'fsdp')
- second_gain_grad: float32 [2, 960], P('section', 'fsdp')
Inputs may be any that keep to these rules, and one draw needn't show every extreme that they name: For each group and micro-batch the 4 lengths sum to at most 1024; rows beyond the sum are padding; a length may be 0.
All inputs are finite; a program needn't handle non-finite values.
Results may differ from a plain program's by a relative error of at most 0.025.
Values may be sent and summed in bfloat16 or wider, within the bound.
No kernel may reach another device: no remote copies, remote signals or barrier semaphores. Data moves between devices by JAX's collectives and lax.ppermute only.
A program may use at most 192 MiB of HBM per device.

v0:
```python
from functools import partial

import jax
import jax.numpy as jnp
from jax import lax
from jax.sharding import PartitionSpec as P

QUERY_HEADS = 15
KEY_VALUE_HEADS = 5
HEAD_SIZE = 64


EPS = 1e-05
SCALE = 0.125
MASKED = -1e30


def for_sending(value):

    def short(part):
        return part.astype(jnp.bfloat16) if part.dtype == jnp.float32 else part

    return jax.tree.map(short, value)


def shifted(block, axis, distance):
    devices = range(lax.axis_size(axis))
    route = [(i - distance, i) for i in devices if i - distance in devices]
    return lax.ppermute(block, axis, route)


def segment_rows(seq_lengths, row_index):
    seq_ends = jnp.cumsum(seq_lengths)
    starts = seq_ends - seq_lengths
    segment = jnp.sum((row_index[:, None] >= seq_ends[None, :]).astype(jnp.int32), axis=1)
    slot_ids = jnp.arange(seq_lengths.shape[0], dtype=jnp.int32)
    row_start = jnp.sum(
        jnp.where(segment[:, None] == slot_ids[None, :], starts[None, :], 0), axis=1
    )
    return (segment, row_index - row_start)


def rotary_tables(position):
    frequency = 10000.0 ** (-2.0 * jnp.arange(HEAD_SIZE // 2, dtype=jnp.float32) / HEAD_SIZE)
    angles = position.astype(jnp.float32)[:, None] * frequency[None, :]
    return (jnp.cos(angles)[:, None, :], jnp.sin(angles)[:, None, :])


def rotary_embedding(vector, cosine_table, sine_portion):
    first_half = vector[..., : HEAD_SIZE // 2]
    second_half = vector[..., HEAD_SIZE // 2 :]
    return jnp.concatenate(
        [
            first_half * cosine_table - second_half * sine_portion,
            second_half * cosine_table + first_half * sine_portion,
        ],
        axis=-1,
    )


def rotary_embedding_backward(grad, cosine_table, sine_portion):
    first_half = grad[..., : HEAD_SIZE // 2]
    second_half = grad[..., HEAD_SIZE // 2 :]
    return jnp.concatenate(
        [
            first_half * cosine_table + second_half * sine_portion,
            second_half * cosine_table - first_half * sine_portion,
        ],
        axis=-1,
    )


def rms_scale(values):
    return lax.rsqrt(jnp.mean(values * values, axis=-1, keepdims=True) + EPS)


def outer_sum(left, right):
    return lax.dot_general(
        left, right, (((0,), (0,)), ((), ())), preferred_element_type=jnp.float32
    )


def backward_product(grad, weight):
    return lax.dot_general(
        grad, weight, (((1,), (1,)), ((), ())), preferred_element_type=jnp.float32
    )


def select_tree(flag, when_true, when_false):
    return jax.tree.map(partial(jnp.where, flag), when_true, when_false)


def forward_layer(inputs, gathered, cosine_table, sine_portion, allowed):
    (
        w_query,
        key_projection_weight,
        value_projection_weight,
        output_projection_weight,
        w_gate,
        w_up,
        w_down,
        gain_one,
        gain_two,
    ) = gathered
    count_of_rows = inputs.shape[0]
    inv_one = rms_scale(inputs)
    normalized_input = (inputs * inv_one * gain_one.astype(jnp.float32)).astype(jnp.bfloat16)
    query_rows = jnp.dot(normalized_input, w_query, preferred_element_type=jnp.float32).reshape(
        count_of_rows, QUERY_HEADS, HEAD_SIZE
    )
    key_portion = jnp.dot(
        normalized_input, key_projection_weight, preferred_element_type=jnp.float32
    ).reshape(count_of_rows, KEY_VALUE_HEADS, HEAD_SIZE)
    value_part = jnp.dot(
        normalized_input, value_projection_weight, preferred_element_type=jnp.float32
    ).astype(jnp.bfloat16)
    query_rows = (
        rotary_embedding(query_rows, cosine_table, sine_portion)
        .astype(jnp.bfloat16)
        .reshape(count_of_rows, KEY_VALUE_HEADS, QUERY_HEADS // KEY_VALUE_HEADS, HEAD_SIZE)
    )
    key_portion = (
        rotary_embedding(key_portion, cosine_table, sine_portion)
        .astype(jnp.bfloat16)
        .reshape(count_of_rows, KEY_VALUE_HEADS * HEAD_SIZE)
    )
    key_row_block, value_row_block = (
        lax.all_gather(key_portion, "fsdp", axis=0, tiled=True),
        lax.all_gather(value_part, "fsdp", axis=0, tiled=True),
    )
    key_row_block = key_row_block.reshape(-1, KEY_VALUE_HEADS, HEAD_SIZE)
    value_row_block = value_row_block.reshape(-1, KEY_VALUE_HEADS, HEAD_SIZE)
    scores = (
        jnp.einsum("qghd,kgd->ghqk", query_rows, key_row_block, preferred_element_type=jnp.float32)
        * SCALE
    )
    scores = jnp.where(allowed, scores, MASKED)
    row_max = jnp.max(scores, axis=-1, keepdims=True)
    exponent = jnp.exp(scores - row_max)
    total = jnp.sum(exponent, axis=-1, keepdims=True)
    attention = (exponent / total).astype(jnp.bfloat16)
    log_total = row_max + jnp.log(total)
    mixture = jnp.einsum(
        "ghqk,kgd->qghd", attention, value_row_block, preferred_element_type=jnp.float32
    )
    mixture = mixture.astype(jnp.bfloat16).reshape(count_of_rows, QUERY_HEADS * HEAD_SIZE)
    middle = inputs + jnp.dot(mixture, output_projection_weight, preferred_element_type=jnp.float32)
    inv_two = rms_scale(middle)
    normed_two = (middle * inv_two * gain_two.astype(jnp.float32)).astype(jnp.bfloat16)
    gate_pre = jnp.dot(normed_two, w_gate, preferred_element_type=jnp.float32)
    up_pre = jnp.dot(normed_two, w_up, preferred_element_type=jnp.float32)
    hidden = (jax.nn.silu(gate_pre) * up_pre).astype(jnp.bfloat16)
    result = middle + jnp.dot(hidden, w_down, preferred_element_type=jnp.float32)
    stored = (
        inputs,
        inv_one,
        normalized_input,
        query_rows,
        key_row_block,
        value_row_block,
        log_total,
        mixture,
        middle,
        inv_two,
        normed_two,
        gate_pre,
        up_pre,
        hidden,
    )
    return (result, stored)


def backward_layer(grad_out, gathered, stored, cosine_table, sine_portion, allowed):
    (
        w_query,
        key_projection_weight,
        value_projection_weight,
        output_projection_weight,
        w_gate,
        w_up,
        w_down,
        gain_one,
        gain_two,
    ) = gathered
    (
        inputs,
        inv_one,
        normalized_input,
        query_rows,
        key_row_block,
        value_row_block,
        log_total,
        mixture,
        middle,
        inv_two,
        normed_two,
        gate_pre,
        up_pre,
        hidden,
    ) = stored
    count_of_rows = grad_out.shape[0]
    grad_low = grad_out.astype(jnp.bfloat16)
    grad_w_down = outer_sum(hidden, grad_low)
    grad_hidden = backward_product(grad_low, w_down)
    sigmoid_gate = jax.nn.sigmoid(gate_pre)
    grad_gate = (
        grad_hidden * up_pre * sigmoid_gate * (1.0 + gate_pre * (1.0 - sigmoid_gate))
    ).astype(jnp.bfloat16)
    grad_up = (grad_hidden * gate_pre * sigmoid_gate).astype(jnp.bfloat16)
    grad_w_gate = outer_sum(normed_two, grad_gate)
    grad_w_up = outer_sum(normed_two, grad_up)
    grad_normed_two = backward_product(grad_gate, w_gate) + backward_product(grad_up, w_up)
    unit_two = middle * inv_two
    grad_gain_two = jnp.sum(grad_normed_two * unit_two, axis=0)
    scaled_two = grad_normed_two * gain_two.astype(jnp.float32)
    grad_mid = grad_out + inv_two * (
        scaled_two - unit_two * jnp.mean(scaled_two * unit_two, axis=-1, keepdims=True)
    )
    middle_lower_gradient = grad_mid.astype(jnp.bfloat16)
    grad_w_output = outer_sum(mixture, middle_lower_gradient)
    grad_mixture = (
        backward_product(middle_lower_gradient, output_projection_weight)
        .astype(jnp.bfloat16)
        .reshape(count_of_rows, KEY_VALUE_HEADS, QUERY_HEADS // KEY_VALUE_HEADS, HEAD_SIZE)
    )
    scores = (
        jnp.einsum("qghd,kgd->ghqk", query_rows, key_row_block, preferred_element_type=jnp.float32)
        * SCALE
    )
    scores = jnp.where(allowed, scores, MASKED)
    attention_full = jnp.exp(scores - log_total)
    attention = attention_full.astype(jnp.bfloat16)
    value_gradient = jnp.einsum(
        "ghqk,qghd->kgd", attention, grad_mixture, preferred_element_type=jnp.float32
    )
    grad_attention = jnp.einsum(
        "qghd,kgd->ghqk", grad_mixture, value_row_block, preferred_element_type=jnp.float32
    )
    row_dots = jnp.sum(attention_full * grad_attention, axis=-1, keepdims=True)
    grad_scores = (attention_full * (grad_attention - row_dots)).astype(jnp.bfloat16)
    grad_queries = (
        jnp.einsum("ghqk,kgd->qghd", grad_scores, key_row_block, preferred_element_type=jnp.float32)
        * SCALE
    )
    key_gradient = (
        jnp.einsum("ghqk,qghd->kgd", grad_scores, query_rows, preferred_element_type=jnp.float32)
        * SCALE
    )
    key_gradient, value_gradient = (
        lax.psum_scatter(
            key_gradient.reshape(-1, KEY_VALUE_HEADS * HEAD_SIZE).astype(jnp.bfloat16),
            "fsdp",
            scatter_dimension=0,
            tiled=True,
        ).astype(jnp.float32),
        lax.psum_scatter(
            value_gradient.reshape(-1, KEY_VALUE_HEADS * HEAD_SIZE).astype(jnp.bfloat16),
            "fsdp",
            scatter_dimension=0,
            tiled=True,
        ).astype(jnp.float32),
    )
    grad_queries = rotary_embedding_backward(
        grad_queries.reshape(count_of_rows, QUERY_HEADS, HEAD_SIZE), cosine_table, sine_portion
    )
    grad_queries = grad_queries.reshape(count_of_rows, QUERY_HEADS * HEAD_SIZE).astype(jnp.bfloat16)
    key_gradient = rotary_embedding_backward(
        key_gradient.reshape(count_of_rows, KEY_VALUE_HEADS, HEAD_SIZE), cosine_table, sine_portion
    )
    key_gradient = key_gradient.reshape(count_of_rows, KEY_VALUE_HEADS * HEAD_SIZE).astype(
        jnp.bfloat16
    )
    value_gradient = value_gradient.astype(jnp.bfloat16)
    grad_w_query = outer_sum(normalized_input, grad_queries)
    grad_w_key = outer_sum(normalized_input, key_gradient)
    grad_w_value = outer_sum(normalized_input, value_gradient)
    grad_normed = (
        backward_product(grad_queries, w_query)
        + backward_product(key_gradient, key_projection_weight)
        + backward_product(value_gradient, value_projection_weight)
    )
    unit_one = inputs * inv_one
    grad_gain_one = jnp.sum(grad_normed * unit_one, axis=0)
    scaled_one = grad_normed * gain_one.astype(jnp.float32)
    grad_in = grad_mid + inv_one * (
        scaled_one - unit_one * jnp.mean(scaled_one * unit_one, axis=-1, keepdims=True)
    )
    weight_grads = (
        grad_w_query,
        grad_w_key,
        grad_w_value,
        grad_w_output,
        grad_w_gate,
        grad_w_up,
        grad_w_down,
        grad_gain_one,
        grad_gain_two,
    )
    return (grad_in, weight_grads)


def per_device(
    boundary,
    lengths,
    query_weight,
    key_matrix,
    value_matrix,
    output_weight,
    gate_weight,
    up_weight,
    down_weight,
    first_gain,
    second_gain,
):
    shards = tuple(
        (
            item[0]
            for item in (
                query_weight,
                key_matrix,
                value_matrix,
                output_weight,
                gate_weight,
                up_weight,
                down_weight,
                first_gain,
                second_gain,
            )
        )
    )
    section_index = lax.axis_index("section")
    is_first = section_index == 0
    own_slab = boundary[0, :, 0]
    micro_count = own_slab.shape[0]
    rows_dev = own_slab.shape[1]
    full_rows = rows_dev * lax.axis_size("fsdp")
    shard_index = lax.axis_index("fsdp")
    seq_lengths = lengths[0]
    own_rows = shard_index * rows_dev + jnp.arange(rows_dev, dtype=jnp.int32)
    all_rows = jnp.arange(full_rows, dtype=jnp.int32)

    def geometry(micro_index):
        chosen_lengths = seq_lengths[micro_index]
        segment_mine, position_mine = segment_rows(chosen_lengths, own_rows)
        segment_all, unused_position = segment_rows(chosen_lengths, all_rows)
        allowed = (segment_mine[:, None] == segment_all[None, :]) & (
            own_rows[:, None] >= all_rows[None, :]
        )
        cosine_table, sine_portion = rotary_tables(position_mine)
        live_rows = (segment_mine < seq_lengths.shape[1]).astype(jnp.float32)
        return (cosine_table, sine_portion, allowed, live_rows)

    gathered = jax.tree.map(
        lambda part, own: part.astype(own.dtype),
        lax.all_gather(for_sending(shards), "fsdp", axis=0, tiled=True),
        shards,
    )
    received = jnp.zeros((rows_dev, own_slab.shape[2]), jnp.bfloat16)
    stored_all = []
    finals = []
    for moment in range(micro_count + 1):
        micro_index = jnp.clip(moment - section_index, 0, micro_count - 1)
        cosine_table, sine_portion, allowed, live_rows = geometry(micro_index)
        start_rows = jnp.where(is_first, own_slab[min(moment, micro_count - 1)], received)
        result, stored_now = forward_layer(
            start_rows.astype(jnp.float32), gathered, cosine_table, sine_portion, allowed
        )
        stored_all.append(stored_now)
        finals.append(result.astype(jnp.bfloat16))
        if moment < micro_count:
            received = shifted(finals[-1], "section", 1)
    returned = jnp.zeros((rows_dev, own_slab.shape[2]), jnp.bfloat16)
    totals = None
    input_grads = []
    for moment in range(micro_count + 1):
        micro_raw = moment - 1 + section_index
        micro_index = jnp.clip(micro_raw, 0, micro_count - 1)
        is_valid = ((micro_raw >= 0) & (micro_raw < micro_count)).astype(jnp.float32)
        cosine_table, sine_portion, allowed, live_rows = geometry(micro_index)
        stored_now = select_tree(
            is_first, stored_all[max(moment - 1, 0)], stored_all[min(moment + 1, micro_count)]
        )
        cotangent = own_slab[min(moment, micro_count - 1)].astype(jnp.float32) * live_rows[:, None]
        incoming = jnp.where(is_first, returned.astype(jnp.float32), cotangent) * is_valid
        grad_in, weight_grads = backward_layer(
            incoming, gathered, stored_now, cosine_table, sine_portion, allowed
        )
        totals = weight_grads if totals is None else jax.tree.map(jnp.add, totals, weight_grads)
        input_grads.append(grad_in.astype(jnp.bfloat16))
        if moment < micro_count:
            returned = shifted(input_grads[-1], "section", -1)
    spread_part = lax.psum_scatter(totals, ("fsdp", "dp"), scatter_dimension=0, tiled=True)
    summed = jax.tree.map(
        lambda part, own: part.astype(own.dtype),
        lax.all_gather(for_sending(spread_part), "dp", axis=0, tiled=True),
        spread_part,
    )
    ends_out = jnp.where(is_first, jnp.stack(input_grads[1:]), jnp.stack(finals[1:]))
    boundary_out = ends_out[None, :, None]
    return (
        boundary_out,
        summed[0][None],
        summed[1][None],
        summed[2][None],
        summed[3][None],
        summed[4][None],
        summed[5][None],
        summed[6][None],
        summed[7][None],
        summed[8][None],
    )


def solution(mesh):
    placed = (
        P("section", None, "dp", "fsdp", None),
        P("dp", None, None),
        P("section", "fsdp", None),
        P("section", "fsdp", None),
        P("section", "fsdp", None),
        P("section", "fsdp", None),
        P("section", "fsdp", None),
        P("section", "fsdp", None),
        P("section", "fsdp", None),
        P("section", "fsdp"),
        P("section", "fsdp"),
    )
    return jax.shard_map(
        per_device,
        mesh=mesh,
        in_specs=placed,
        out_specs=(
            P("section", None, "dp", "fsdp", None),
            P("section", "fsdp", None),
            P("section", "fsdp", None),
            P("section", "fsdp", None),
            P("section", "fsdp", None),
            P("section", "fsdp", None),
            P("section", "fsdp", None),
            P("section", "fsdp", None),
            P("section", "fsdp"),
            P("section", "fsdp"),
        ),
        check_vma=False,
    )
```

profile of v0, /device:TPU:0, one launch (start us, length us, event | category | flops | bytes accessed | tf_op | source)
XLA Modules:
  0.0 2468.8 jit_solution(2060355228606749427)
XLA Ops:
  11.7 59.5 %all-gather.1 = bf16[1,960,320]{2,0,1:T(2,128)(2,1)} all-gather(bf16[1,120,320]{2,0,1:T(2,128)(2,1)S(1)} %copy.88), channel_id=3, replica_groups=mesh['section'=2,'fsdp'=8,'dp'=8] {'fsdp'}, dimensions={1}, use_global_device_ids=true | all-gather | bytes 691200 | tf_op jit(solution)/shard_map/all_gather | solution.py:355
  74.3 48.7 %all-gather.2 = bf16[1,960,320]{2,0,1:T(2,128)(2,1)} all-gather(bf16[1,120,320]{2,0,1:T(2,128)(2,1)S(1)} %copy.90), channel_id=4, replica_groups=mesh['section'=2,'fsdp'=8,'dp'=8] {'fsdp'}, dimensions={1}, use_global_device_ids=true | all-gather | bytes 691200 | tf_op jit(solution)/shard_map/all_gather | solution.py:355
  157.2 32.0 %all_gather.74 = bf16[1024,320]{0,1:T(8,128)(2,1)S(1)} all-gather(bf16[128,320]{0,1:T(8,128)(2,1)S(1)} %convolution_convert_fusion.2), channel_id=1, replica_groups=mesh['section'=2,'fsdp'=8,'dp'=8] {'fsdp'}, dimensions={0}, use_global_device_ids=true | all-gather | bytes 737280 | tf_op jit(solution)/shard_map/all_gather | solution.py:129
  189.2 32.2 %all_gather.76 = bf16[1024,320]{0,1:T(8,128)(2,1)S(1)} all-gather(bf16[128,320]{0,1:T(8,128)(2,1)S(1)} %bitcast.793), channel_id=1, replica_groups=mesh['section'=2,'fsdp'=8,'dp'=8] {'fsdp'}, dimensions={0}, use_global_device_ids=true | all-gather | bytes 737280 | tf_op jit(solution)/shard_map/all_gather | solution.py:128
  235.9 39.7 %all-gather.25.cloned.1.call-done = bf16[1,960,2560]{2,1,0:T(8,128)(2,1)} async-done(((bf16[1,120,2560]{2,1,0:T(8,128)(2,1)}), bf16[1,960,2560]{2,1,0:T(8,128)(2,1)}) %all-gather.25.cloned.1.call-update) | async-done | bytes 4915216 | tf_op jit(solution)/shard_map/all_gather | solution.py:355
  278.9 101.5 %all-gather.27.cloned.1.call-done = bf16[1,960,2560]{2,1,0:T(8,128)(2,1)} async-done(((bf16[1,120,2560]{2,1,0:T(8,128)(2,1)}), bf16[1,960,2560]{2,1,0:T(8,128)(2,1)}) %all-gather.27.cloned.1.call-update) | async-done | bytes 4915216 | tf_op jit(solution)/shard_map/all_gather | solution.py:355
  384.9 107.4 %all-gather.29.cloned.1.call-done = bf16[1,2560,960]{2,1,0:T(8,128)(2,1)} async-done(((bf16[1,320,960]{2,1,0:T(8,128)(2,1)}), bf16[1,2560,960]{2,1,0:T(8,128)(2,1)}) %all-gather.29.cloned.1.call-update) | async-done | bytes 4915216 | tf_op jit(solution)/shard_map/all_gather | solution.py:355
  504.0 27.6 %all_gather.83 = bf16[1024,320]{0,1:T(8,128)(2,1)S(1)} all-gather(bf16[128,320]{0,1:T(8,128)(2,1)S(1)} %convolution_convert_fusion.1), channel_id=1, replica_groups=mesh['section'=2,'fsdp'=8,'dp'=8] {'fsdp'}, dimensions={0}, use_global_device_ids=true | all-gather | bytes 737280 | tf_op jit(solution)/shard_map/all_gather | solution.py:129
  531.7 28.1 %all_gather.84 = bf16[1024,320]{0,1:T(8,128)(2,1)S(1)} all-gather(bf16[128,320]{0,1:T(8,128)(2,1)S(1)} %bitcast.794), channel_id=1, replica_groups=mesh['section'=2,'fsdp'=8,'dp'=8] {'fsdp'}, dimensions={0}, use_global_device_ids=true | all-gather | bytes 737280 | tf_op jit(solution)/shard_map/all_gather | solution.py:128
  614.6 20.8 reduce-scatter.34.cloned.1.call-done
  637.3 39.6 %reduce-scatter.36.cloned.1.call-done = bf16[128,320]{1,0:T(8,128)(2,1)} async-done(((bf16[1024,320]{1,0:T(8,128)(2,1)}), bf16[128,320]{1,0:T(8,128)(2,1)}) %reduce-scatter.36.cloned.1.call-update) | async-done | bytes 81936
  687.6 27.3 %all_gather.85 = bf16[1024,320]{0,1:T(8,128)(2,1)S(1)} all-gather(bf16[128,320]{0,1:T(8,128)(2,1)S(1)} %convolution_convert_fusion), channel_id=1, replica_groups=mesh['section'=2,'fsdp'=8,'dp'=8] {'fsdp'}, dimensions={0}, use_global_device_ids=true | all-gather | bytes 737280 | tf_op jit(solution)/shard_map/all_gather | solution.py:129
  715.0 26.6 %all_gather.86 = bf16[1024,320]{0,1:T(8,128)(2,1)S(1)} all-gather(bf16[128,320]{0,1:T(8,128)(2,1)S(1)} %bitcast.795), channel_id=1, replica_groups=mesh['section'=2,'fsdp'=8,'dp'=8] {'fsdp'}, dimensions={0}, use_global_device_ids=true | all-gather | bytes 737280 | tf_op jit(solution)/shard_map/all_gather | solution.py:128
  791.7 29.0 %reduce-scatter.38.cloned.1.call-done = bf16[128,320]{1,0:T(8,128)(2,1)} async-done(((bf16[1024,320]{1,0:T(8,128)(2,1)}), bf16[128,320]{1,0:T(8,128)(2,1)}) %reduce-scatter.38.cloned.1.call-update) | async-done | bytes 81936
  826.2 36.0 %reduce-scatter.40.cloned.1.call-done = bf16[128,320]{1,0:T(8,128)(2,1)} async-done(((bf16[1024,320]{1,0:T(8,128)(2,1)}), bf16[128,320]{1,0:T(8,128)(2,1)}) %reduce-scatter.40.cloned.1.call-update) | async-done | bytes 81936
  989.2 911.5 %fusion.345 = (f32[16,960]{1,0:T(8,128)S(1)}, f32[16,320]{1,0:T(8,128)S(1)}, f32[16,320]{1,0:T(8,128)S(1)}, f32[16,960]{1,0:T(8,128)S(1)}, f32[16,2560]{1,0:T(8,128)}, /*index=5*/f32[16,2560]{1,0:T(8,128)S(1)}) fusion(f32[960,960]{1,0:T(8,128)} %add_add_fusion.4, f32[960,320]{1,0:T(8,128)} %add_add_fusion.6, f32[960,320]{1,0:T(8,128)} %add_add_fusion.5, ...), kind=kCustom, calls=%all-reduce-scatter.6 | all-reduce-scatter fusion | flops 7864321 | bytes 29983232
  1927.8 175.8 %all-reduce.18 = (bf16[960]{0:T(1024)(128)(2,1)S(1)}, bf16[960]{0:T(1024)(128)(2,1)S(1)}) all-reduce(f32[960]{0:T(1024)S(1)} %add_add_fusion.8, f32[960]{0:T(1024)S(1)} %add_add_fusion.7), channel_id=24, replica_groups=mesh['section'=2,'fsdp'=8,'dp'=8] {'fsdp','dp'}, use_global_device_ids=true, to_apply=%region_61.62.clone | all-reduce | flops 1920 | bytes 11520
  2146.9 34.3 %all-gather.10 = bf16[8,15,320]{2,1,0:T(8,128)(2,1)S(1)} all-gather(bf16[1,15,320]{2,1,0:T(8,128)(2,1)S(1)} %fusion.303), channel_id=1, replica_groups=mesh['section'=2,'fsdp'=8,'dp'=8] {'dp'}, dimensions={0}, use_global_device_ids=true | all-gather | bytes 86400 | tf_op jit(solution)/shard_map/all_gather | solution.py:395
  2195.0 34.3 %all-gather.11 = bf16[8,15,320]{2,1,0:T(8,128)(2,1)S(1)} all-gather(bf16[1,15,320]{2,1,0:T(8,128)(2,1)S(1)} %fusion.304), channel_id=1, replica_groups=mesh['section'=2,'fsdp'=8,'dp'=8] {'dp'}, dimensions={0}, use_global_device_ids=true | all-gather | bytes 86400 | tf_op jit(solution)/shard_map/all_gather | solution.py:395
  2243.3 34.6 %all-gather.9 = bf16[8,15,960]{2,1,0:T(8,128)(2,1)S(1)} all-gather(bf16[1,15,960]{2,1,0:T(8,128)(2,1)S(1)} %fusion.301), channel_id=1, replica_groups=mesh['section'=2,'fsdp'=8,'dp'=8] {'dp'}, dimensions={0}, use_global_device_ids=true | all-gather | bytes 259200 | tf_op jit(solution)/shard_map/all_gather | solution.py:395
  2302.5 37.8 %all-gather.12 = bf16[8,15,960]{2,1,0:T(8,128)(2,1)S(1)} all-gather(bf16[1,15,960]{2,1,0:T(8,128)(2,1)S(1)} %fusion.302), channel_id=1, replica_groups=mesh['section'=2,'fsdp'=8,'dp'=8] {'dp'}, dimensions={0}, use_global_device_ids=true | all-gather | bytes 259200 | tf_op jit(solution)/shard_map/all_gather | solution.py:395
  2350.7 35.4 %all-gather.13 = bf16[8,15,2560]{2,1,0:T(8,128)(2,1)S(1)} all-gather(bf16[1,15,2560]{2,1,0:T(8,128)(2,1)S(1)} %fusion.295), channel_id=1, replica_groups=mesh['section'=2,'fsdp'=8,'dp'=8] {'dp'}, dimensions={0}, use_global_device_ids=true | all-gather | bytes 691200 | tf_op jit(solution)/shard_map/all_gather | solution.py:395
  2388.2 35.1 %all-gather.14 = bf16[8,15,2560]{2,1,0:T(8,128)(2,1)S(1)} all-gather(bf16[1,15,2560]{2,1,0:T(8,128)(2,1)S(1)} %fusion.296), channel_id=1, replica_groups=mesh['section'=2,'fsdp'=8,'dp'=8] {'dp'}, dimensions={0}, use_global_device_ids=true | all-gather | bytes 691200 | tf_op jit(solution)/shard_map/all_gather | solution.py:395
  2425.4 35.1 %all_gather.93 = bf16[320,960]{1,0:T(8,128)(2,1)S(1)} all-gather(bf16[40,960]{1,0:T(8,128)(2,1)S(1)} %convert_element_type.571), channel_id=1, replica_groups=mesh['section'=2,'fsdp'=8,'dp'=8] {'dp'}, dimensions={0}, use_global_device_ids=true | all-gather | bytes 691200 | tf_op jit(solution)/shard_map/all_gather | solution.py:395
  (721 shorter events, 458.4 us)
Async XLA Ops:
  7.2 214.2 %all-gather.21.cloned.1.call-start = ((), (), s32[]{:S(2)}) async-start(), calls=%async_computation.8 | async-start | bytes 2211840 | tf_op jit(solution)/shard_map/all_gather | solution.py:355
  8.0 225.2 %all-gather.23.cloned.1.call-start = ((), (), s32[]{:S(2)}) async-start(), calls=%async_computation.9 | async-start | bytes 2211840 | tf_op jit(solution)/shard_map/all_gather | solution.py:355
  8.7 267.0 %all-gather.25.cloned.1.call-start = ((), (), s32[]{:S(2)}) async-start(), calls=%async_computation.10 | async-start | bytes 5529600 | tf_op jit(solution)/shard_map/all_gather | solution.py:355
  9.4 371.0 %all-gather.27.cloned.1.call-start = ((), (), s32[]{:S(2)}) async-start(), calls=%async_computation.11 | async-start | bytes 5529600 | tf_op jit(solution)/shard_map/all_gather | solution.py:355
  10.0 482.3 %all-gather.29.cloned.1.call-start = ((), (), s32[]{:S(2)}) async-start(), calls=%async_computation.12 | async-start | bytes 5898240 | tf_op jit(solution)/shard_map/all_gather | solution.py:355
  10.6 624.8 %reduce-scatter.34.cloned.1.call-start = ((), (), s32[]{:S(2)}) async-start(), calls=%async_computation.13 | async-start | bytes 884736
  596.7 80.2 %reduce-scatter.36.cloned.1.call-start = ((), (), s32[]{:S(2)}) async-start(), calls=%async_computation.14 | async-start | bytes 884736
  605.8 214.9 %reduce-scatter.38.cloned.1.call-start = ((), (), s32[]{:S(2)}) async-start(), calls=%async_computation.15 | async-start | bytes 884736
  611.2 69.0 %collective-permute-start.2 = (bf16[128,960]{0,1:T(8,128)(2,1)}, bf16[128,960]{0,1:T(8,128)(2,1)}, u32[]{:S(2)}, u32[]{:S(2)}) collective-permute-start(bf16[128,960]{0,1:T(8,128)(2,1)} %fusion.175), channel_id=1, source_target_pairs={{0,64},{1,65},{2,66},{3,67},{4,68},{5,69},{6,70},{7,71},{8,72},{9,... | collective-permute-start | bytes 737288 | tf_op jit(solution)/shard_map/ppermute | solution.py:29
  779.1 83.1 %reduce-scatter.40.cloned.1.call-start = ((), (), s32[]{:S(2)}) async-start(), calls=%async_computation.16 | async-start | bytes 884736
  787.7 193.8 %reduce-scatter.42.cloned.1.call-start = ((), (), s32[]{:S(2)}) async-start(), calls=%async_computation.17 | async-start | bytes 884736
  893.2 93.0 %reduce-scatter.44.cloned.1.call-start = ((), (), s32[]{:S(2)}) async-start(), calls=%async_computation.18 | async-start | bytes 884736
  907.3 1517.2 %reduce-scatter.32.cloned.1.call-start = ((), (), s32[]{:S(2)}) async-start(), calls=%async_computation.7 | async-start | bytes 10649600 | tf_op jit(solution)/shard_map/reduce_scatter | solution.py:392
  1901.9 231.2 %collective-permute-start.10 = (bf16[16,320]{1,0:T(8,128)(2,1)}, bf16[16,320]{1,0:T(8,128)(2,1)}, u32[]{:S(2)}, u32[]{:S(2)}) collective-permute-start(bf16[16,320]{1,0:T(8,128)(2,1)} %convert.204), channel_id=1, source_target_pairs={{0,3},{1,4},{2,5},{3,6},{4,7},{5,8},{6,9},{7,10},{8,11},{9,12},{10... | collective-permute-start | bytes 30728
  1909.6 227.3 %collective-permute-start.9 = (bf16[16,320]{1,0:T(8,128)(2,1)}, bf16[16,320]{1,0:T(8,128)(2,1)}, u32[]{:S(2)}, u32[]{:S(2)}) collective-permute-start(bf16[16,320]{1,0:T(8,128)(2,1)} %convert.204), channel_id=1, source_target_pairs={{0,2},{1,3},{2,4},{3,5},{4,6},{5,7},{6,8},{7,9},{8,10},{9,11},{10,... | collective-permute-start | bytes 30728
  1911.4 229.2 %collective-permute-start.8 = (bf16[16,320]{1,0:T(8,128)(2,1)}, bf16[16,320]{1,0:T(8,128)(2,1)}, u32[]{:S(2)}, u32[]{:S(2)}) collective-permute-start(bf16[16,320]{1,0:T(8,128)(2,1)} %convert.204), channel_id=1, source_target_pairs={{0,1},{1,2},{2,3},{3,4},{4,5},{5,6},{6,7},{7,8},{8,9},{9,10},{10,1... | collective-permute-start | bytes 30728
  1916.2 215.5 %collective-permute-start.11 = (bf16[15,320]{1,0:T(8,128)(2,1)}, bf16[15,320]{1,0:T(8,128)(2,1)}, u32[]{:S(2)}, u32[]{:S(2)}) collective-permute-start(bf16[15,320]{1,0:T(8,128)(2,1)} %slice.135), channel_id=1, source_target_pairs={{0,4},{1,5},{2,6},{3,7},{4,8},{5,9},{6,10},{7,11},{8,12},{9,13},{1... | collective-permute-start | bytes 28808
  1918.3 265.1 %collective-permute-start.14 = (bf16[16,320]{1,0:T(8,128)(2,1)}, bf16[16,320]{1,0:T(8,128)(2,1)}, u32[]{:S(2)}, u32[]{:S(2)}) collective-permute-start(bf16[16,320]{1,0:T(8,128)(2,1)} %convert.203), channel_id=1, source_target_pairs={{0,3},{1,4},{2,5},{3,6},{4,7},{5,8},{6,9},{7,10},{8,11},{9,12},{10... | collective-permute-start | bytes 30728
  2136.8 94.6 %collective-permute-start.6 = (bf16[16,960]{1,0:T(8,128)(2,1)S(1)}, bf16[16,960]{1,0:T(8,128)(2,1)S(1)}, u32[]{:S(2)}, u32[]{:S(2)}) collective-permute-start(bf16[16,960]{1,0:T(8,128)(2,1)S(1)} %convert.202), channel_id=1, source_target_pairs={{0,3},{1,4},{2,5},{3,6},{4,7},{5,8},{6,9},{7,10},{8,11},{9,12},{10... | collective-permute-start | bytes 92168
  2192.3 87.8 %collective-permute-start.18 = (bf16[16,960]{1,0:T(8,128)(2,1)S(1)}, bf16[16,960]{1,0:T(8,128)(2,1)S(1)}, u32[]{:S(2)}, u32[]{:S(2)}) collective-permute-start(bf16[16,960]{1,0:T(8,128)(2,1)S(1)} %convert.201), channel_id=1, source_target_pairs={{0,3},{1,4},{2,5},{3,6},{4,7},{5,8},{6,9},{7,10},{8,11},{9,12},{10... | collective-permute-start | bytes 92168
  2241.4 101.3 %collective-permute-start.22 = (bf16[16,2560]{1,0:T(8,128)(2,1)S(1)}, bf16[16,2560]{1,0:T(8,128)(2,1)S(1)}, u32[]{:S(2)}, u32[]{:S(2)}) collective-permute-start(bf16[16,2560]{1,0:T(8,128)(2,1)S(1)} %convert.200), channel_id=1, source_target_pairs={{0,3},{1,4},{2,5},{3,6},{4,7},{5,8},{6,9},{7,10},{8,11},{9,12},{10... | collective-permute-start | bytes 245768
  2278.8 65.2 %collective-permute-start.21 = (bf16[16,2560]{1,0:T(8,128)(2,1)S(1)}, bf16[16,2560]{1,0:T(8,128)(2,1)S(1)}, u32[]{:S(2)}, u32[]{:S(2)}) collective-permute-start(bf16[16,2560]{1,0:T(8,128)(2,1)S(1)} %convert.200), channel_id=1, source_target_pairs={{0,2},{1,3},{2,4},{3,5},{4,6},{5,7},{6,8},{7,9},{8,10},{9,11},{10,... | collective-permute-start | bytes 245768
  2280.1 69.7 %collective-permute-start.20 = (bf16[16,2560]{1,0:T(8,128)(2,1)S(1)}, bf16[16,2560]{1,0:T(8,128)(2,1)S(1)}, u32[]{:S(2)}, u32[]{:S(2)}) collective-permute-start(bf16[16,2560]{1,0:T(8,128)(2,1)S(1)} %convert.200), channel_id=1, source_target_pairs={{0,1},{1,2},{2,3},{3,4},{4,5},{5,6},{6,7},{7,8},{8,9},{9,10},{10,1... | collective-permute-start | bytes 245768
  2290.0 97.3 %collective-permute-start.26 = (bf16[16,2560]{1,0:T(8,128)(2,1)S(1)}, bf16[16,2560]{1,0:T(8,128)(2,1)S(1)}, u32[]{:S(2)}, u32[]{:S(2)}) collective-permute-start(bf16[16,2560]{1,0:T(8,128)(2,1)S(1)} %convert.199), channel_id=1, source_target_pairs={{0,3},{1,4},{2,5},{3,6},{4,7},{5,8},{6,9},{7,10},{8,11},{9,12},{10... | collective-permute-start | bytes 245768
  (210 other events, 7991.2 us)
Sparse Core Ops, SparseCore 0:
  9.7 80.8 all-gather.20
  92.3 57.8 all-gather.22
  151.8 123.8 all-gather.24
  277.2 103.2 all-gather.26
  382.0 110.2 all-gather.28
  596.8 38.5 reduce-scatter.33
  638.5 38.3 reduce-scatter.35
  779.3 41.3 reduce-scatter.37
  823.8 38.4 reduce-scatter.39
  893.3 39.6 reduce-scatter.41
  936.0 38.4 reduce-scatter.43
  976.8 507.7 reduce-scatter.31
where the time goes:
time: 2480 us; the launch traced here: 2470 us
  blocking collectives  1660 us (67%)
  waiting for transfers between devices  379 us (15%)
  matrix products  215 us (9%)
  starting transfers between devices  95.3 us (4%)
  local copies, waits for them, and re-layouts  65.8 us (3%)
  other arithmetic  36.6 us (1%)
    unnamed x4, blocking collectives  1130 us
    all_gather x5, waiting for transfers between devices, per_device(): lax.all_gather(for_sending(shards), 'fsdp', axis=0, tiled=True)  249 us
    all_gather x7, blocking collectives, per_device(): lax.all_gather(for_sending(spread_part), 'dp', axis=0, tiled=True)  247 us
    unnamed x42, waiting for transfers between devices  129 us
    all_gather x2, blocking collectives, per_device(): lax.all_gather(for_sending(shards), 'fsdp', axis=0, tiled=True)  108 us
    unnamed x30, starting transfers between devices  87.2 us
    all_gather x3, blocking collectives, forward_layer(): lax.all_gather(value_part, 'fsdp', axis=0, tiled=True)  87 us
    all_gather x3, blocking collectives, forward_layer(): lax.all_gather(key_portion, 'fsdp', axis=0, tiled=True)  86.8 us
  transfers between devices with their start and end apart: 40, of which 9 were waited for; matrix products, arithmetic and copies ran while one was open for 45% of the time, Pallas kernels for 0%

commit v1 on v0

v1 whole, which is shorter than its diff:
```python
import jax
import jax.numpy as jnp
from jax import lax
from jax.sharding import PartitionSpec as P

QUERY_HEADS = 15
KEY_VALUE_HEADS = 5
HEAD_SIZE = 64


EPS = 1e-05
SCALE = 0.125
MASKED = -1e30


BF16 = jnp.bfloat16
F32 = jnp.float32
WIDTH = 960
PART = 120
PADDED = 128
SPREAD = 1024
UNIT = 1280
FF_PART = 320
FF_QUARTER = 80
DOWN_COLS = 512
DOWN_SKIP = 64
ROW_QUARTER = 32
KV_WIDTH = KEY_VALUE_HEADS * HEAD_SIZE
DISTANCES = (0, -1, 1, 2)


def segment_rows(seq_lengths, row_index):
    seq_ends = jnp.cumsum(seq_lengths)
    starts = seq_ends - seq_lengths
    segment = jnp.sum((row_index[:, None] >= seq_ends[None, :]).astype(jnp.int32), axis=1)
    slot_ids = jnp.arange(seq_lengths.shape[0], dtype=jnp.int32)
    row_start = jnp.sum(
        jnp.where(segment[:, None] == slot_ids[None, :], starts[None, :], 0), axis=1
    )
    return (segment, row_index - row_start)


def rotary_tables(position):
    frequency = 10000.0 ** (-2.0 * jnp.arange(HEAD_SIZE // 2, dtype=jnp.float32) / HEAD_SIZE)
    angles = position.astype(jnp.float32)[:, None] * frequency[None, :]
    return (jnp.cos(angles)[:, None, :], jnp.sin(angles)[:, None, :])


def rotary_embedding(vector, cosine_table, sine_portion):
    first_half = vector[..., : HEAD_SIZE // 2]
    second_half = vector[..., HEAD_SIZE // 2 :]
    return jnp.concatenate(
        [
            first_half * cosine_table - second_half * sine_portion,
            second_half * cosine_table + first_half * sine_portion,
        ],
        axis=-1,
    )


def rotary_embedding_backward(grad, cosine_table, sine_portion):
    first_half = grad[..., : HEAD_SIZE // 2]
    second_half = grad[..., HEAD_SIZE // 2 :]
    return jnp.concatenate(
        [
            first_half * cosine_table + second_half * sine_portion,
            second_half * cosine_table - first_half * sine_portion,
        ],
        axis=-1,
    )


def rms_scale(values):
    return lax.rsqrt(jnp.mean(values * values, axis=-1, keepdims=True) + EPS)


def outer_sum(left, right):
    return lax.dot_general(
        left, right, (((0,), (0,)), ((), ())), preferred_element_type=jnp.float32
    )


def backward_product(grad, weight):
    return lax.dot_general(
        grad, weight, (((1,), (1,)), ((), ())), preferred_element_type=jnp.float32
    )


def z_step(value, step):
    return lax.ppermute(value, "fsdp", [(i, (i + 2 * step) % 8) for i in range(8)])


def x_step(value, step):
    return lax.ppermute(value, "dp", [(i, (i + 2 * step) % 8) for i in range(8)])


def y_near(value):
    return lax.ppermute(value, "fsdp", [(i, i ^ 1) for i in range(8)])


def y_far(value):
    return lax.ppermute(value, "dp", [(i, i ^ 1) for i in range(8)])


def sibling(value):
    return lax.ppermute(value, "section", [(0, 1), (1, 0)])


def ring_gather(step, way, block):
    before = step(block, 1)
    after = step(block, -1)
    far = step(before if way == 1 else after, way)
    return [block, before, after, far]


def ring_sum(step, way, chunk):
    relayed = step(chunk(2).astype(BF16), way)
    other = step(chunk(-way).astype(BF16), -way)
    nearer = (chunk(way).astype(F32) + relayed.astype(F32)).astype(BF16)
    return chunk(0).astype(F32) + other.astype(F32) + step(nearer, way).astype(F32)


def direct_sum(step, chunk):
    total = chunk(0).astype(F32)
    for distance in (1, -1, 2):
        total = total + step(chunk(distance).astype(BF16), distance).astype(F32)
    return total


class Place:
    def __init__(self):
        self.section = lax.axis_index("section")
        self.shard = lax.axis_index("fsdp")
        dp = lax.axis_index("dp")
        self.z, self.y = self.shard // 2, self.shard % 2
        self.x = dp // 2
        self.first = self.section == 0
        self.near_shards = jnp.stack(
            [(self.z + d) % 4 * 2 + (self.y + near) % 2 for d in DISTANCES for near in (0, 1)]
        )
        row = lax.broadcasted_iota(jnp.int32, (WIDTH, SPREAD), 0)
        column = jnp.arange(SPREAD, dtype=jnp.int32)
        self.z_shard = jnp.repeat(self.near_shards, PADDED)
        self.by_z = (
            (row // PART == self.z_shard[None]) & (row % PART == (column % PADDED)[None])
        ).astype(BF16)
        quarters = jnp.repeat(jnp.stack([(self.x + d) % 4 for d in DISTANCES]), SPREAD // 4)
        shards = jnp.tile(jnp.repeat(self.near_shards, ROW_QUARTER), 4)
        inner = quarters * ROW_QUARTER + column % ROW_QUARTER
        self.by_x = ((row // PART == shards[None]) & (row % PART == inner[None])).astype(BF16)

    def role(self, zero, one):
        return jnp.where(self.first, zero, one)

    def roles(self, mine, other):
        return (jnp.where(self.first, mine, other), jnp.where(self.first, other, mine))


def spread(value, places):
    return jnp.dot(value, places, preferred_element_type=F32).astype(BF16)


def unspread(value, places):
    high = lax.reduce_precision(value, 8, 7)
    both = jnp.concatenate([high.astype(BF16), (value - high).astype(BF16)], axis=1)
    return backward_product(both, jnp.concatenate([places, places], axis=1))


def product(left, right):
    return jnp.dot(left, right, preferred_element_type=F32)


def gate(value, *others):
    late = False
    for other in others:
        corner = other[(0,) * other.ndim]
        late = late | (corner != corner)
    return jax.tree.map(lambda part: jnp.where(late, jnp.zeros_like(part), part), value)


def gather_first(place, own):
    pair = jnp.concatenate([own, y_near(own)], axis=0)
    blocks = ring_gather(z_step, 1, pair)
    mine = jnp.concatenate(blocks, axis=0)
    return (mine, sibling(mine), blocks[-1])


def gather_down(place, own):
    other = y_near(own)
    low, high = (jnp.where(place.y == 0, own, other), jnp.where(place.y == 0, other, own))
    pair = jnp.concatenate([low, high], axis=0)
    blocks = ring_gather(z_step, -1, pair)
    mine = jnp.concatenate(blocks, axis=0)
    return (mine, sibling(mine), blocks[-1])


def gather_column(place, own):
    quarter = lax.dynamic_slice_in_dim(own, place.x * ROW_QUARTER, ROW_QUARTER, 0)
    pair = jnp.concatenate([quarter, y_near(quarter)], axis=0)
    return ring_gather(z_step, -1, pair)


def gather_wide(column):
    before = x_step(column, 1)
    after = x_step(column, -1)
    half = column.shape[0] // 2
    far = [x_step(before[:half], 1), x_step(after[half:], -1)]
    mine = jnp.concatenate([column, before, after] + far, axis=0)
    return (mine, sibling(mine), far[0])


def layer_weights(place, column, first, down):
    one = gather_first(place, first)
    two = gather_wide(column)
    low = gather_down(place, down)
    gains = one[0].reshape(8, PADDED, UNIT)[:, PART : PART + 2, :PADDED]
    gains = backward_product(gains.transpose(1, 0, 2).reshape(2, SPREAD), place.by_z)
    return (one, two, low, gains[:1], gains[1:])


def gather_rows(own):
    pair = jnp.concatenate([own, y_near(own)], axis=0)
    return jnp.concatenate(ring_gather(z_step, 1, pair), axis=0)


def scatter_rows(partial):
    parts = partial.reshape(4, -1, partial.shape[1])
    pair = ring_sum(z_step, -1, lambda distance: parts[DISTANCES.index(distance)])
    rows = pair.shape[0] // 2
    return pair[:rows] + y_near(pair[rows:].astype(BF16)).astype(F32)


def down_columns(place, hidden):
    size = 2 * FF_PART
    return jnp.concatenate(
        [
            lax.dynamic_slice_in_dim(hidden, (place.z + d) % 4 * size, size, 1)
            for d in DISTANCES
        ],
        axis=1,
    )


def forward_layer(place, inputs, weights, cosine_table, sine_portion, allowed):
    one, two, low, gain_one, gain_two = weights
    count_of_rows = inputs.shape[0]
    inv_one = rms_scale(inputs)
    normed_one = spread((inputs * inv_one * gain_one).astype(BF16), place.by_z)
    query_key, value_part = place.roles(product(normed_one, one[0]), product(normed_one, one[1]))
    value_part = value_part[:, WIDTH:].astype(BF16)
    turned = rotary_embedding(
        query_key.reshape(count_of_rows, QUERY_HEADS + KEY_VALUE_HEADS, HEAD_SIZE),
        cosine_table,
        sine_portion,
    ).astype(BF16)
    query_rows = turned[:, :QUERY_HEADS].reshape(
        count_of_rows, KEY_VALUE_HEADS, QUERY_HEADS // KEY_VALUE_HEADS, HEAD_SIZE
    )
    key_portion = turned[:, QUERY_HEADS:].reshape(count_of_rows, KV_WIDTH)
    key_value = gather_rows(jnp.concatenate([key_portion, value_part], axis=1))
    key_row_block = key_value[:, :KV_WIDTH].reshape(-1, KEY_VALUE_HEADS, HEAD_SIZE)
    value_row_block = key_value[:, KV_WIDTH:].reshape(-1, KEY_VALUE_HEADS, HEAD_SIZE)
    scores = (
        jnp.einsum("qghd,kgd->ghqk", query_rows, key_row_block, preferred_element_type=F32)
        * SCALE
    )
    scores = jnp.where(allowed, scores, MASKED)
    row_max = jnp.max(scores, axis=-1, keepdims=True)
    exponent = jnp.exp(scores - row_max)
    total = jnp.sum(exponent, axis=-1, keepdims=True)
    attention = (exponent / total).astype(BF16)
    log_total = row_max + jnp.log(total)
    mixture = jnp.einsum(
        "ghqk,kgd->qghd", attention, value_row_block, preferred_element_type=F32
    )
    mixture = spread(
        mixture.astype(BF16).reshape(count_of_rows, QUERY_HEADS * HEAD_SIZE), place.by_z
    )
    unused, projected = place.roles(product(mixture, one[0]), product(mixture, one[1]))
    middle = inputs + projected[:, :WIDTH]
    inv_two = rms_scale(middle)
    normed_two = spread((middle * inv_two * gain_two).astype(BF16), place.by_x)
    gate_pre, up_pre = place.roles(product(normed_two, two[0]), product(normed_two, two[1]))
    hidden = down_columns(place, (jax.nn.silu(gate_pre) * up_pre).astype(BF16))
    left, right = place.roles(product(hidden, low[0]), product(hidden, low[1]))
    result = middle + jnp.concatenate([left, right[:, DOWN_SKIP:]], axis=1)
    stored = (
        inputs,
        inv_one,
        normed_one,
        query_rows,
        key_row_block,
        value_row_block,
        log_total,
        mixture,
        middle,
        inv_two,
        normed_two,
        gate_pre,
        up_pre,
        hidden,
    )
    return (result, stored)


def with_sibling(own, sent):
    return jnp.concatenate([own, sibling(sent)], axis=0)


def norm_backward(grad, unit, inverse, gain):
    scaled = grad * gain
    return inverse * (scaled - unit * jnp.mean(scaled * unit, axis=-1, keepdims=True))


def partial_chunks(left, right):
    size = left.shape[1] // 4

    def chunk(distance):
        at = DISTANCES.index(distance)
        return outer_sum(left[:, at * size : (at + 1) * size], right).astype(BF16)

    return chunk


def by_quarter(place, block, rows):
    quarters = block.reshape(4, rows, block.shape[-1])

    def quarter(distance):
        return lax.dynamic_index_in_dim(quarters, (place.x + distance) % 4, 0, keepdims=False)

    return quarter


def reduce_first(left, right):
    return ring_sum(z_step, 1, partial_chunks(left, right))


def reduce_down(place, left, right):
    pair = ring_sum(z_step, -1, partial_chunks(left, right)).astype(BF16)
    pair = pair.reshape(2, PADDED, UNIT)
    return jnp.concatenate(
        [
            lax.dynamic_index_in_dim(pair, place.y, 0, keepdims=False),
            lax.dynamic_index_in_dim(pair, 1 - place.y, 0, keepdims=False),
        ],
        axis=0,
    ).astype(F32)


def reduce_wide(left, right):
    chunk = partial_chunks(left, right)
    half = SPREAD // 8
    from_before = x_step(outer_sum(left[:, -2 * half : -half], right).astype(BF16), 1)
    from_after = x_step(outer_sum(left[:, -half:], right).astype(BF16), -1)
    after = chunk(1).astype(F32) + jnp.pad(from_before, ((0, half), (0, 0))).astype(F32)
    before = chunk(-1).astype(F32) + jnp.pad(from_after, ((half, 0), (0, 0))).astype(F32)
    column = (
        chunk(0).astype(F32)
        + x_step(after.astype(BF16), 1).astype(F32)
        + x_step(before.astype(BF16), -1).astype(F32)
    )
    parts = column.reshape(4, 2 * ROW_QUARTER, 2 * UNIT)
    pair = ring_sum(z_step, 1, lambda distance: parts[DISTANCES.index(distance)])
    quarter = pair[:ROW_QUARTER] + y_near(pair[ROW_QUARTER:].astype(BF16)).astype(F32)
    return ((from_before, from_after), column, quarter)


def quarter_of(place, pair):
    block = pair[:PADDED] + y_near(pair[PADDED:].astype(BF16)).astype(F32)
    return direct_sum(x_step, by_quarter(place, block, ROW_QUARTER))


def finish(place, quarter):
    low = quarter.astype(BF16)
    piece = (low.astype(F32) + y_far(low).astype(F32)).astype(BF16)
    whole = jnp.zeros((4,) + piece.shape, BF16)
    for distance in DISTANCES:
        block = step_from(piece, distance)
        whole = lax.dynamic_update_slice_in_dim(
            whole, block[None], (place.x + distance) % 4, 0
        )
    return whole.reshape(-1, piece.shape[-1])


def step_from(piece, distance):
    return piece if distance == 0 else x_step(piece, -distance)


def backward_layer(
    place, grad_out, weights, stored, waits, cosine_table, sine_portion, allowed
):
    one, two, low, gain_one, gain_two = weights
    (
        inputs,
        inv_one,
        normed_one,
        query_rows,
        key_row_block,
        value_row_block,
        log_total,
        mixture,
        middle,
        inv_two,
        normed_two,
        gate_pre,
        up_pre,
        hidden,
    ) = stored
    count_of_rows = grad_out.shape[0]
    grad_low = grad_out.astype(BF16)
    left_low = grad_low[:, :DOWN_COLS]
    right_low = grad_low[:, WIDTH - DOWN_COLS :]
    right_once = jnp.where(jnp.arange(DOWN_COLS)[None] < DOWN_SKIP, 0, right_low)
    mine_low, other_low = place.roles(left_low, right_once)
    hidden_grads = backward_product(mine_low, low[0]) + backward_product(other_low, low[1])
    size = 2 * FF_PART
    hidden_grad = jnp.zeros_like(hidden_grads)
    for at, distance in enumerate(DISTANCES):
        hidden_grad = lax.dynamic_update_slice_in_dim(
            hidden_grad,
            hidden_grads[:, at * size : (at + 1) * size],
            (place.z + distance) % 4 * size,
            1,
        )
    sigmoid_gate = jax.nn.sigmoid(gate_pre)
    grad_gate = (
        hidden_grad * up_pre * sigmoid_gate * (1.0 + gate_pre * (1.0 - sigmoid_gate))
    ).astype(BF16)
    grad_up = (hidden_grad * gate_pre * sigmoid_gate).astype(BF16)
    mine, other = place.roles(grad_gate, grad_up)
    spread_two = backward_product(mine, two[0]) + backward_product(other, two[1])
    left_rows = with_sibling(*2 * (jnp.concatenate([hidden, normed_two], axis=1),))
    right_rows = with_sibling(
        jnp.concatenate([place.role(left_low, right_low), mine], axis=1),
        jnp.concatenate([place.role(right_low, left_low), other], axis=1),
    )
    down = reduce_down(place, left_rows[:, : 2 * UNIT], right_rows[:, :DOWN_COLS])
    wide = reduce_wide(left_rows[:, 2 * UNIT :], right_rows[:, DOWN_COLS:])
    grad_normed_two = unspread(spread_two, place.by_x)
    unit_two = middle * inv_two
    grad_gain_two = jnp.sum(grad_normed_two * unit_two, axis=0)
    grad_normed_two = gate(grad_normed_two, *waits[0])
    grad_mid = grad_out + norm_backward(grad_normed_two, unit_two, inv_two, gain_two)
    none_narrow = jnp.zeros((count_of_rows, KV_WIDTH), BF16)
    output_side = jnp.concatenate([grad_mid.astype(BF16), none_narrow], axis=1)
    none = jnp.zeros_like(output_side)
    mine, other = place.roles(none, output_side)
    grad_mixture = (
        unspread(backward_product(mine, one[0]) + backward_product(other, one[1]), place.by_z)
        .astype(BF16)
        .reshape(count_of_rows, KEY_VALUE_HEADS, QUERY_HEADS // KEY_VALUE_HEADS, HEAD_SIZE)
    )
    scores = (
        jnp.einsum("qghd,kgd->ghqk", query_rows, key_row_block, preferred_element_type=F32)
        * SCALE
    )
    scores = jnp.where(allowed, scores, MASKED)
    attention_full = jnp.exp(scores - log_total)
    attention = attention_full.astype(BF16)
    value_gradient = jnp.einsum(
        "ghqk,qghd->kgd", attention, grad_mixture, preferred_element_type=F32
    )
    grad_attention = jnp.einsum(
        "qghd,kgd->ghqk", grad_mixture, value_row_block, preferred_element_type=F32
    )
    row_dots = jnp.sum(attention_full * grad_attention, axis=-1, keepdims=True)
    grad_scores = (attention_full * (grad_attention - row_dots)).astype(BF16)
    key_gradient = (
        jnp.einsum("ghqk,qghd->kgd", grad_scores, query_rows, preferred_element_type=F32)
        * SCALE
    )
    far, column, wide = wide
    key_gradient = gate(key_gradient, *waits[1], *far)
    key_value = scatter_rows(
        jnp.concatenate(
            [key_gradient.reshape(-1, KV_WIDTH), value_gradient.reshape(-1, KV_WIDTH)], axis=1
        ).astype(BF16)
    )
    grad_queries = (
        jnp.einsum("ghqk,kgd->qghd", grad_scores, key_row_block, preferred_element_type=F32)
        * SCALE
    )
    key_gradient, value_low = (key_value[:, :KV_WIDTH], key_value[:, KV_WIDTH:].astype(BF16))
    grad_query_key = rotary_embedding_backward(
        jnp.concatenate(
            [
                grad_queries.reshape(count_of_rows, QUERY_HEADS, HEAD_SIZE),
                key_gradient.reshape(count_of_rows, KEY_VALUE_HEADS, HEAD_SIZE),
            ],
            axis=1,
        ),
        cosine_table,
        sine_portion,
    )
    grad_query_key = grad_query_key.reshape(count_of_rows, UNIT).astype(BF16)
    value_side = jnp.concatenate([jnp.zeros((count_of_rows, WIDTH), BF16), value_low], axis=1)
    mine, other = place.roles(grad_query_key, value_side)
    grad_normed = unspread(
        backward_product(mine, one[0]) + backward_product(other, one[1]), place.by_z
    )
    unit_one = inputs * inv_one
    grad_gain_one = jnp.sum(grad_normed * unit_one, axis=0)
    grad_in = grad_mid + norm_backward(grad_normed, unit_one, inv_one, gain_one)
    gain_rows = jnp.stack([grad_gain_one.reshape(8, PART), grad_gain_two.reshape(8, PART)], axis=1)
    gain_rows = jnp.pad(gain_rows.reshape(16, PART).astype(BF16), ((0, 0), (0, UNIT - PART)))
    number = jnp.arange(16, dtype=jnp.int32)[:, None]
    inner = (jnp.arange(SPREAD, dtype=jnp.int32) % PADDED)[None]
    gain_place = (number // 2 == place.z_shard[None]) & (PART + number % 2 == inner)
    left_rows = with_sibling(
        jnp.concatenate([place.role(normed_one, mixture), normed_one], axis=1),
        jnp.concatenate([place.role(mixture, normed_one), normed_one], axis=1),
    )
    right_rows = with_sibling(
        jnp.concatenate([place.role(grad_query_key, output_side), place.role(none, value_side)], 1),
        jnp.concatenate([place.role(output_side, grad_query_key), place.role(value_side, none)], 1),
    )
    left_rows = gate(left_rows, *waits[2])
    left_rows = jnp.concatenate(
        [left_rows[:, :SPREAD], left_rows[:, SPREAD:], gain_place.astype(BF16)], axis=0
    )
    right_rows = jnp.concatenate([right_rows[:, :UNIT], right_rows[:, UNIT:], gain_rows], axis=0)
    return (
        gate(grad_in, down, column),
        (reduce_first(left_rows, right_rows), down, wide),
    )


def per_device(
    boundary,
    lengths,
    query_weight,
    key_matrix,
    value_matrix,
    output_weight,
    gate_weight,
    up_weight,
    down_weight,
    first_gain,
    second_gain,
):
    place = Place()
    first = place.first
    slab = boundary[0, :, 0]
    rows_dev = slab.shape[1]
    exchanged = sibling(jnp.where(first, slab[1], slab[0]))
    inputs = jnp.where(first, slab[0], exchanged).astype(F32)
    cotangent = jnp.where(first, exchanged, slab[1]).astype(F32)

    gains = jnp.pad(
        jnp.concatenate([first_gain, second_gain], axis=0), ((0, 6), (0, UNIT - PART))
    )
    role_packs = (
        (
            jnp.concatenate(
                [jnp.concatenate([query_weight[0], key_matrix[0]], axis=1), gains], axis=0
            ),
            jnp.pad(gate_weight[0], ((0, PADDED - PART), (0, 0))),
            down_weight[0, :, :DOWN_COLS],
        ),
        (
            jnp.concatenate(
                [jnp.concatenate([output_weight[0], value_matrix[0]], axis=1), gains], axis=0
            ),
            jnp.pad(up_weight[0], ((0, PADDED - PART), (0, 0))),
            down_weight[0, :, WIDTH - DOWN_COLS :],
        ),
    )
    layer_packs = ([], [])
    for zero, one in zip(*role_packs):
        kept = jnp.where(first, zero, one)
        other = sibling(jnp.where(first, one, zero))
        layer_packs[0].append(jnp.where(first, kept, other))
        layer_packs[1].append(jnp.where(first, other, kept))
    first_pack, wide_pack, down_pack = layer_packs[0]
    blocks = gather_column(place, wide_pack)
    column = jnp.concatenate(blocks, axis=0)
    weights_first = layer_weights(place, column, first_pack, gate(down_pack, blocks[3]))
    first_pack, wide_pack, down_pack = layer_packs[1]
    blocks = gather_column(place, gate(wide_pack, blocks[3]))

    seq_lengths = jnp.where(first, lengths[0, 0], lengths[0, 1])
    inner = jnp.arange(rows_dev, dtype=jnp.int32)
    own_rows = place.shard * rows_dev + inner
    all_rows = (place.near_shards[:, None] * rows_dev + inner[None]).reshape(-1)
    segment_mine, position_mine = segment_rows(seq_lengths, own_rows)
    segment_all, unused_position = segment_rows(seq_lengths, all_rows)
    allowed = (segment_mine[:, None] == segment_all[None, :]) & (
        own_rows[:, None] >= all_rows[None, :]
    )
    cosine_table, sine_portion = rotary_tables(position_mine)
    live_rows = (segment_mine < seq_lengths.shape[0]).astype(F32)

    geometry = (cosine_table, sine_portion, allowed)
    middle, stored_first = forward_layer(place, inputs, weights_first, *geometry)
    blocks[0], first_pack, down_pack = gate(
        (blocks[0], first_pack, down_pack), stored_first[4]
    )
    column = jnp.concatenate(blocks, axis=0)
    weights_second = layer_weights(place, column, first_pack, down_pack)
    middle = middle.astype(BF16).astype(F32)
    result, stored_second = forward_layer(place, middle, weights_second, *geometry)
    grad, pending = backward_layer(
        place, cotangent * live_rows[:, None], weights_second, stored_second, ((), (), ()), *geometry
    )
    pair, down, wide = pending
    wide = jnp.concatenate([quarter_of(place, down), wide], axis=1)
    low = quarter_of(place, pair)
    early_second, late_second = (finish(place, wide), finish(place, low))
    waits = ((pair,), (wide, low), (early_second, late_second))
    grad = grad.astype(BF16).astype(F32)
    grad, remaining = backward_layer(
        place, grad, weights_first, stored_first, waits, *geometry
    )

    ends = (grad.astype(BF16), result.astype(BF16))
    received = sibling(jnp.where(first, ends[1], ends[0]))
    boundary_out = jnp.where(
        first, jnp.stack([ends[0], received]), jnp.stack([received, ends[1]])
    )[None, :, None]

    pair, down, wide = remaining
    early_first = finish(place, jnp.concatenate([quarter_of(place, down), wide], axis=1))
    late_first = finish(place, quarter_of(place, pair))
    sums = []
    for for_first, for_second in ((early_first, early_second), (late_first, late_second)):
        own = jnp.where(first, for_first, for_second)
        other = sibling(jnp.where(first, for_second, for_first))
        sums.append([value.astype(F32) for value in place.roles(own, other)])
    down_left, down_right = [value[:, :UNIT].reshape(FF_PART, DOWN_COLS) for value in sums[0]]
    gate_sum, up_sum = [value[:, UNIT:] for value in sums[0]]
    query_key, output_value = sums[1]
    gain_sums = query_key[PART : PART + 2, :PART] + output_value[PART : PART + 2, :PART]
    return (
        boundary_out,
        query_key[None, :PART, :WIDTH],
        query_key[None, :PART, WIDTH:],
        output_value[None, :PART, WIDTH:],
        output_value[None, :PART, :WIDTH],
        gate_sum[None, :PART],
        up_sum[None, :PART],
        jnp.concatenate([down_left, down_right[:, DOWN_SKIP:]], axis=1)[None],
        gain_sums[:1],
        gain_sums[1:],
    )


def solution(mesh):
    placed = (
        P("section", None, "dp", "fsdp", None),
        P("dp", None, None),
        P("section", "fsdp", None),
        P("section", "fsdp", None),
        P("section", "fsdp", None),
        P("section", "fsdp", None),
        P("section", "fsdp", None),
        P("section", "fsdp", None),
        P("section", "fsdp", None),
        P("section", "fsdp"),
        P("section", "fsdp"),
    )
    return jax.shard_map(
        per_device,
        mesh=mesh,
        in_specs=placed,
        out_specs=(
            P("section", None, "dp", "fsdp", None),
            P("section", "fsdp", None),
            P("section", "fsdp", None),
            P("section", "fsdp", None),
            P("section", "fsdp", None),
            P("section", "fsdp", None),
            P("section", "fsdp", None),
            P("section", "fsdp", None),
            P("section", "fsdp"),
            P("section", "fsdp"),
        ),
        check_vma=False,
    )
```

time: 2480 us -> 814 us (0.33)
  blocking collectives: 1660 us -> 0 us
  waiting for transfers between devices: 379 us -> 292 us
  matrix products: 215 us -> 141 us
  other arithmetic: 36.6 us -> 95.2 us
  starting transfers between devices: 95.3 us -> 147 us
  local copies, waits for them, and re-layouts: 65.8 us -> 102 us
    unnamed x4 -> x0, blocking collectives: 1130 us -> none
    all_gather x15 -> x0, blocking collectives: 529 us -> none  [the longest x7 247 us: per_device(): lax.all_gather(for_sending(spread_part), 'dp', axis=0, tiled=True)]
    ppermute x4 -> x129, waiting for transfers between devices: 1.74 us -> 292 us  [the longest x48 145 us: z_step(): lax.ppermute(value, 'fsdp', [(i, (i + 2 * step) % 8) for i in range(8)])]
    all_gather x5 -> x0, waiting for transfers between devices: 249 us -> none  [per_device(): lax.all_gather(for_sending(shards), 'fsdp', axis=0, tiled=True)]
    ppermute x4 -> x129, starting transfers between devices: 7.64 us -> 147 us  [the longest x48 58.2 us: z_step(): lax.ppermute(value, 'fsdp', [(i, (i + 2 * step) % 8) for i in range(8)])]
    unnamed x42 -> x0, waiting for transfers between devices: 129 us -> none
    unnamed x30 -> x0, starting transfers between devices: 87.2 us -> none
    dot_general x21 -> x26, matrix products: 77.3 us -> 37.1 us  [outer_sum(): lax.dot_general(left, right, (((0,), (0,)), ((), ())), preferred_element_...]
  transfers between devices with their start and end apart: 40 -> 129, of which waited for: 9 -> 58; matrix products, arithmetic and copies ran while one was open for 45% -> 37% of each run, Pallas kernels for 0% -> 0%
where the time goes in v1:
time: 814 us; the launch traced here: 802 us
  waiting for transfers between devices  292 us (36%)
  starting transfers between devices  147 us (18%)
  matrix products  141 us (17%)
  local copies, waits for them, and re-layouts  102 us (13%)
  other arithmetic  95.2 us (12%)
  between operations  24.3 us (3%)
    ppermute x48, waiting for transfers between devices, z_step(): lax.ppermute(value, 'fsdp', [(i, (i + 2 * step) % 8) for i in range(8)])  145 us
    ppermute x40, waiting for transfers between devices, x_step(): lax.ppermute(value, 'dp', [(i, (i + 2 * step) % 8) for i in range(8)])  103 us
    ppermute x48, starting transfers between devices, z_step(): lax.ppermute(value, 'fsdp', [(i, (i + 2 * step) % 8) for i in range(8)])  58.2 us
    ppermute x40, starting transfers between devices, x_step(): lax.ppermute(value, 'dp', [(i, (i + 2 * step) % 8) for i in range(8)])  54.5 us
    dot_general x24, matrix products, backward_product(): lax.dot_general(grad, weight, (((1,), (1,)), ((), ())), preferred_element...  41.7 us
    unnamed x416, local copies, waits for them, and re-layouts  39 us
    dot_general x26, matrix products, outer_sum(): lax.dot_general(left, right, (((0,), (0,)), ((), ())), preferred_element_...  37.1 us
    ppermute x16, waiting for transfers between devices, y_near(): return lax.ppermute(value, 'fsdp', [(i, i ^ 1) for i in range(8)])  32.5 us
  transfers between devices with their start and end apart: 129, of which 58 were waited for; matrix products, arithmetic and copies ran while one was open for 37% of the time, Pallas kernels for 0%

profile of v1, /device:TPU:0, one launch (start us, length us, event | category | flops | bytes accessed | tf_op | source)
XLA Modules:
  0.0 802.1 jit_solution(16967492124066439642)
XLA Ops:
  19.9 6.4 collective-permute-done.2
  39.1 12.1 %collective-permute-done.14 = bf16[64,2560]{1,0:T(8,128)(2,1)S(1)} collective-permute-done((bf16[64,2560]{1,0:T(8,128)(2,1)S(1)}, bf16[64,2560]{1,0:T(8,128)(2,1)S(1)}, u32[]{:S(2)}, u32[]{:S(2)}) %collective-permute-start.14) | collective-permute-done | bytes 327712 | tf_op jit(solution)/shard_map/ppermute | solution.py:90
  54.9 15.7 %collective-permute-done.5 = bf16[256,1280]{1,0:T(8,128)(2,1)S(1)} collective-permute-done((bf16[256,1280]{1,0:T(8,128)(2,1)S(1)}, bf16[256,1280]{1,0:T(8,128)(2,1)S(1)}, u32[]{:S(2)}, u32[]{:S(2)}) %collective-permute-start.5) | collective-permute-done | bytes 655392 | tf_op jit(solution)/shard_map/ppermute | solution.py:90
  82.1 21.3 %collective-permute-done.16 = bf16[256,2560]{1,0:T(8,128)(2,1)S(1)} collective-permute-done((bf16[256,2560]{1,0:T(8,128)(2,1)S(1)}, bf16[256,2560]{1,0:T(8,128)(2,1)S(1)}, u32[]{:S(2)}, u32[]{:S(2)}) %collective-permute-start.16) | collective-permute-done | bytes 1310752 | tf_op jit(solution)/shard_map/ppermute | solution.py:94
  189.4 13.1 %collective-permute-done.40 = bf16[64,2560]{1,0:T(8,128)(2,1)S(1)} collective-permute-done((bf16[64,2560]{1,0:T(8,128)(2,1)}, bf16[64,2560]{1,0:T(8,128)(2,1)S(1)}, u32[]{:S(2)}, u32[]{:S(2)}) %collective-permute-start.40) | collective-permute-done | bytes 327712 | tf_op jit(solution)/shard_map/ppermute | solution.py:90
  210.5 9.8 %collective-permute-done.49 = bf16[640,512]{1,0:T(8,128)(2,1)S(1)} collective-permute-done((bf16[640,512]{1,0:T(8,128)(2,1)S(1)}, bf16[640,512]{1,0:T(8,128)(2,1)S(1)}, u32[]{:S(2)}, u32[]{:S(2)}) %collective-permute-start.49) | collective-permute-done | bytes 655392 | tf_op jit(solution)/shard_map/ppermute | solution.py:90
  224.9 9.4 %collective-permute-done.30 = bf16[256,1280]{1,0:T(8,128)(2,1)S(1)} collective-permute-done((bf16[256,1280]{1,0:T(8,128)(2,1)S(1)}, bf16[256,1280]{1,0:T(8,128)(2,1)S(1)}, u32[]{:S(2)}, u32[]{:S(2)}) %collective-permute-start.30) | collective-permute-done | bytes 655392 | tf_op jit(solution)/shard_map/ppermute | solution.py:90
  235.9 9.2 %collective-permute-done.26 = bf16[640,512]{1,0:T(8,128)(2,1)S(1)} collective-permute-done((bf16[640,512]{1,0:T(8,128)(2,1)S(1)}, bf16[640,512]{1,0:T(8,128)(2,1)S(1)}, u32[]{:S(2)}, u32[]{:S(2)}) %collective-permute-start.26) | collective-permute-done | bytes 655392 | tf_op jit(solution)/shard_map/ppermute | solution.py:90
  248.3 9.7 %collective-permute-done.50 = bf16[640,512]{1,0:T(8,128)(2,1)S(1)} collective-permute-done((bf16[640,512]{1,0:T(8,128)(2,1)S(1)}, bf16[640,512]{1,0:T(8,128)(2,1)S(1)}, u32[]{:S(2)}, u32[]{:S(2)}) %collective-permute-start.50) | collective-permute-done | bytes 655392 | tf_op jit(solution)/shard_map/ppermute | solution.py:90
  265.3 12.7 %collective-permute-done.43 = bf16[128,2560]{1,0:T(8,128)(2,1)S(1)} collective-permute-done((bf16[128,2560]{1,0:T(8,128)(2,1)S(1)}, bf16[128,2560]{1,0:T(8,128)(2,1)S(1)}, u32[]{:S(2)}, u32[]{:S(2)}) %collective-permute-start.43) | collective-permute-done | bytes 655392 | tf_op jit(solution)/shard_map/ppermute | solution.py:94
  280.7 5.1 multiply_convert_fusion.5
  314.9 5.6 collective-permute-done.34
  320.8 9.2 %collective-permute-done.36 = bf16[256,640]{1,0:T(8,128)(2,1)S(1)} collective-permute-done((bf16[256,640]{1,0:T(8,128)(2,1)S(1)}, bf16[256,640]{1,0:T(8,128)(2,1)S(1)}, u32[]{:S(2)}, u32[]{:S(2)}) %collective-permute-start.36) | collective-permute-done | bytes 327712 | tf_op jit(solution)/shard_map/ppermute | solution.py:90
  379.7 7.3 fusion.5
  409.0 6.4 collective-permute-done.56
  520.9 7.1 collective-permute-done.92
  542.3 8.0 %collective-permute-done.95 = bf16[32,3840]{1,0:T(8,128)(2,1)S(1)} collective-permute-done((bf16[32,3840]{1,0:T(8,128)(2,1)S(1)}, bf16[32,3840]{1,0:T(8,128)(2,1)S(1)}, u32[]{:S(2)}, u32[]{:S(2)}) %collective-permute-start.95) | collective-permute-done | bytes 245792 | tf_op jit(solution)/shard_map/ppermute | solution.py:94
  550.4 6.5 collective-permute-done.96
  556.9 7.7 collective-permute-done.97
  592.9 5.4 fusion
  598.3 7.1 fusion.2
  639.7 9.5 %collective-permute-done.100 = bf16[32,1280]{1,0:T(8,128)(2,1)S(1)} collective-permute-done((bf16[32,1280]{1,0:T(8,128)(2,1)S(1)}, bf16[32,1280]{1,0:T(8,128)(2,1)S(1)}, u32[]{:S(2)}, u32[]{:S(2)}) %collective-permute-start.100) | collective-permute-done | bytes 81952 | tf_op jit(solution)/shard_map/ppermute | solution.py:94
  721.0 6.6 collective-permute-done.122
  753.9 8.2 %collective-permute-done.106 = bf16[256,1280]{1,0:T(8,128)(2,1)S(1)} collective-permute-done((bf16[256,1280]{1,0:T(8,128)(2,1)S(1)}, bf16[256,1280]{1,0:T(8,128)(2,1)S(1)}, u32[]{:S(2)}, u32[]{:S(2)}) %collective-permute-start.106) | collective-permute-done | bytes 655392 | tf_op jit(solution)/shard_map/ppermute | solution.py:90
  (1007 shorter events, 558.6 us)
Async XLA Ops:
  5.6 147.1 %collective-permute-start.22 = (bf16[320,512]{1,0:T(8,128)(2,1)}, bf16[320,512]{1,0:T(8,128)(2,1)}, u32[]{:S(2)}, u32[]{:S(2)}) collective-permute-start(bf16[320,512]{1,0:T(8,128)(2,1)} %select_bitcast_fusion), channel_id=1, source_target_pairs={{0,64},{64,0},{1,65},{65,1},{2,66},{66,2},{3,67},{67,3},{4,68},{68... | collective-permute-start | bytes 983048 | tf_op jit(solution)/shard_map/ppermute | solution.py:106
  70.7 38.1 %collective-permute-start.6 = (bf16[1024,1280]{1,0:T(8,128)(2,1)S(1)}, bf16[1024,1280]{1,0:T(8,128)(2,1)S(1)}, u32[]{:S(2)}, u32[]{:S(2)}) collective-permute-start(bf16[1024,1280]{1,0:T(8,128)(2,1)S(1)} %constant_dynamic-update-slice_fusion), channel_id=1, source_target_pairs={{0,64},{64,0},{1,65},{65,1},{2,66},{66,2},{3,67},{67,3},{4,68},{68... | collective-permute-start | bytes 7864328 | tf_op jit(solution)/shard_map/ppermute | solution.py:106
  78.5 69.0 %collective-permute-start.37 = (bf16[32,2560]{1,0:T(8,128)(2,1)}, bf16[32,2560]{1,0:T(8,128)(2,1)}, u32[]{:S(2)}, u32[]{:S(2)}) collective-permute-start(bf16[32,2560]{1,0:T(8,128)(2,1)} %select_select_fusion.1), channel_id=1, source_target_pairs={{0,8},{8,0},{16,24},{24,16},{32,40},{40,32},{48,56},{56,48},{1,9},... | collective-permute-start | bytes 491528 | tf_op jit(solution)/shard_map/ppermute | solution.py:98
  127.5 153.2 %collective-permute-start.20 = (bf16[1024,2560]{1,0:T(8,128)(2,1)}, bf16[1024,2560]{1,0:T(8,128)(2,1)}, u32[]{:S(2)}, u32[]{:S(2)}) collective-permute-start(bf16[1024,2560]{1,0:T(8,128)(2,1)} %constant_dynamic-update-slice_fusion.15), channel_id=1, source_target_pairs={{0,64},{64,0},{1,65},{65,1},{2,66},{66,2},{3,67},{67,3},{4,68},{68... | collective-permute-start | bytes 15728648 | tf_op jit(solution)/shard_map/ppermute | solution.py:106
  209.5 35.6 %collective-permute-start.26 = (bf16[640,512]{1,0:T(8,128)(2,1)S(1)}, bf16[640,512]{1,0:T(8,128)(2,1)S(1)}, u32[]{:S(2)}, u32[]{:S(2)}) collective-permute-start(bf16[640,512]{1,0:T(8,128)(2,1)S(1)} %collective-permute-done.25), channel_id=1, source_target_pairs={{0,48},{8,56},{16,0},{24,8},{32,16},{40,24},{48,32},{56,40},{1,49}... | collective-permute-start | bytes 1966088 | tf_op jit(solution)/shard_map/ppermute | solution.py:90
  224.8 34.8 %collective-permute-start.41 = (bf16[256,2560]{1,0:T(8,128)(2,1)S(1)}, bf16[256,2560]{1,0:T(8,128)(2,1)S(1)}, u32[]{:S(2)}, u32[]{:S(2)}) collective-permute-start(bf16[256,2560]{1,0:T(8,128)(2,1)S(1)} %pad_maximum_fusion.6), channel_id=1, source_target_pairs={{0,2},{1,3},{2,4},{3,5},{4,6},{5,7},{6,0},{7,1},{8,10},{9,11},{10,... | collective-permute-start | bytes 3932168 | tf_op jit(solution)/shard_map/ppermute | solution.py:94
  248.2 37.9 %collective-permute-start.27 = (bf16[2560,512]{1,0:T(8,128)(2,1)S(1)}, bf16[2560,512]{1,0:T(8,128)(2,1)S(1)}, u32[]{:S(2)}, u32[]{:S(2)}) collective-permute-start(bf16[2560,512]{1,0:T(8,128)(2,1)S(1)} %constant_dynamic-update-slice_fusion.29), channel_id=1, source_target_pairs={{0,64},{64,0},{1,65},{65,1},{2,66},{66,2},{3,67},{67,3},{4,68},{68... | collective-permute-start | bytes 7864328 | tf_op jit(solution)/shard_map/ppermute | solution.py:106
  258.0 35.0 %collective-permute-start.32 = (bf16[1024,1280]{1,0:T(8,128)(2,1)S(1)}, bf16[1024,1280]{1,0:T(8,128)(2,1)S(1)}, u32[]{:S(2)}, u32[]{:S(2)}) collective-permute-start(bf16[1024,1280]{1,0:T(8,128)(2,1)S(1)} %constant_dynamic-update-slice_fusion.34), channel_id=1, source_target_pairs={{0,64},{64,0},{1,65},{65,1},{2,66},{66,2},{3,67},{67,3},{4,68},{68... | collective-permute-start | bytes 7864328 | tf_op jit(solution)/shard_map/ppermute | solution.py:106
  279.8 69.8 %collective-permute-start.45 = (bf16[1024,2560]{1,0:T(8,128)(2,1)}, bf16[1024,2560]{1,0:T(8,128)(2,1)}, u32[]{:S(2)}, u32[]{:S(2)}) collective-permute-start(bf16[1024,2560]{1,0:T(8,128)(2,1)} %constant_dynamic-update-slice_fusion.44), channel_id=1, source_target_pairs={{0,64},{64,0},{1,65},{65,1},{2,66},{66,2},{3,67},{67,3},{4,68},{68... | collective-permute-start | bytes 15728648 | tf_op jit(solution)/shard_map/ppermute | solution.py:106
  355.5 41.0 %collective-permute-start.52 = (bf16[128,3072]{1,0:T(8,128)(2,1)}, bf16[128,3072]{1,0:T(8,128)(2,1)}, u32[]{:S(2)}, u32[]{:S(2)}) collective-permute-start(bf16[128,3072]{1,0:T(8,128)(2,1)} %pad_maximum_fusion.10), channel_id=1, source_target_pairs={{0,64},{64,0},{1,65},{65,1},{2,66},{66,2},{3,67},{67,3},{4,68},{68... | collective-permute-start | bytes 2359304 | tf_op jit(solution)/shard_map/ppermute | solution.py:106
  358.8 37.7 %collective-permute-start.46 = (bf16[128,3584]{1,0:T(8,128)(2,1)S(1)}, bf16[128,3584]{1,0:T(8,128)(2,1)}, u32[]{:S(2)}, u32[]{:S(2)}) collective-permute-start(bf16[128,3584]{1,0:T(8,128)(2,1)S(1)} %constant_dynamic-update-slice_fusion.52), channel_id=1, source_target_pairs={{0,64},{64,0},{1,65},{65,1},{2,66},{66,2},{3,67},{67,3},{4,68},{68... | collective-permute-start | bytes 2752520 | tf_op jit(solution)/shard_map/ppermute | solution.py:106
  442.0 51.7 %collective-permute-start.59 = (bf16[256,2560]{1,0:T(8,128)(2,1)}, bf16[256,2560]{1,0:T(8,128)(2,1)}, u32[]{:S(2)}, u32[]{:S(2)}) collective-permute-start(bf16[256,2560]{1,0:T(8,128)(2,1)} %fusion.33), channel_id=1, source_target_pairs={{0,6},{1,7},{2,0},{3,1},{4,2},{5,3},{6,4},{7,5},{8,14},{9,15},{10,... | collective-permute-start | bytes 3932168 | tf_op jit(solution)/shard_map/ppermute | solution.py:94
  451.7 42.0 %collective-permute-start.57 = (bf16[256,2560]{1,0:T(8,128)(2,1)}, bf16[256,2560]{1,0:T(8,128)(2,1)}, u32[]{:S(2)}, u32[]{:S(2)}) collective-permute-start(bf16[256,2560]{1,0:T(8,128)(2,1)} %fusion.36), channel_id=1, source_target_pairs={{0,2},{1,3},{2,4},{3,5},{4,6},{5,7},{6,0},{7,1},{8,10},{9,11},{10,... | collective-permute-start | bytes 3932168 | tf_op jit(solution)/shard_map/ppermute | solution.py:94
  488.3 40.7 %collective-permute-start.21 = (bf16[128,3584]{1,0:T(8,128)(2,1)S(1)}, bf16[128,3584]{1,0:T(8,128)(2,1)S(1)}, u32[]{:S(2)}, u32[]{:S(2)}) collective-permute-start(bf16[128,3584]{1,0:T(8,128)(2,1)S(1)} %constant_dynamic-update-slice_fusion.24), channel_id=1, source_target_pairs={{0,64},{64,0},{1,65},{65,1},{2,66},{66,2},{3,67},{67,3},{4,68},{68... | collective-permute-start | bytes 2752520 | tf_op jit(solution)/shard_map/ppermute | solution.py:106
  517.8 60.7 %collective-permute-start.74 = (bf16[256,1280]{1,0:T(8,128)(2,1)S(1)}, bf16[256,1280]{1,0:T(8,128)(2,1)S(1)}, u32[]{:S(2)}, u32[]{:S(2)}) collective-permute-start(bf16[256,1280]{1,0:T(8,128)(2,1)S(1)} %convolution_convert_fusion.16), channel_id=1, source_target_pairs={{0,48},{8,56},{16,0},{24,8},{32,16},{40,24},{48,32},{56,40},{1,49}... | collective-permute-start | bytes 1966088 | tf_op jit(solution)/shard_map/ppermute | solution.py:90
  529.4 40.8 %collective-permute-start.68 = (bf16[128,2560]{1,0:T(8,128)(2,1)S(1)}, bf16[128,2560]{1,0:T(8,128)(2,1)S(1)}, u32[]{:S(2)}, u32[]{:S(2)}) collective-permute-start(bf16[128,2560]{1,0:T(8,128)(2,1)S(1)} %convolution_convert_fusion.7), channel_id=1, source_target_pairs={{0,2},{1,3},{2,4},{3,5},{4,6},{5,7},{6,0},{7,1},{8,10},{9,11},{10,... | collective-permute-start | bytes 1966088 | tf_op jit(solution)/shard_map/ppermute | solution.py:94
  529.8 42.3 %collective-permute-start.70 = (bf16[128,2560]{1,0:T(8,128)(2,1)S(1)}, bf16[128,2560]{1,0:T(8,128)(2,1)S(1)}, u32[]{:S(2)}, u32[]{:S(2)}) collective-permute-start(bf16[128,2560]{1,0:T(8,128)(2,1)S(1)} %convolution_convert_fusion.6), channel_id=1, source_target_pairs={{0,6},{1,7},{2,0},{3,1},{4,2},{5,3},{6,4},{7,5},{8,14},{9,15},{10,... | collective-permute-start | bytes 1966088 | tf_op jit(solution)/shard_map/ppermute | solution.py:94
  541.4 35.8 %collective-permute-start.66 = (bf16[640,512]{1,0:T(8,128)(2,1)S(1)}, bf16[640,512]{1,0:T(8,128)(2,1)S(1)}, u32[]{:S(2)}, u32[]{:S(2)}) collective-permute-start(bf16[640,512]{1,0:T(8,128)(2,1)S(1)} %convolution_convert_fusion.18), channel_id=1, source_target_pairs={{0,48},{8,56},{16,0},{24,8},{32,16},{40,24},{48,32},{56,40},{1,49}... | collective-permute-start | bytes 1966088 | tf_op jit(solution)/shard_map/ppermute | solution.py:90
  570.2 87.5 %collective-permute-start.102 = (bf16[128,2048]{1,0:T(8,128)(2,1)}, bf16[128,2048]{1,0:T(8,128)(2,1)}, u32[]{:S(2)}, u32[]{:S(2)}) collective-permute-start(bf16[128,2048]{1,0:T(8,128)(2,1)} %pad_maximum_fusion.21), channel_id=1, source_target_pairs={{0,64},{64,0},{1,65},{65,1},{2,66},{66,2},{3,67},{67,3},{4,68},{68... | collective-permute-start | bytes 1572872 | tf_op jit(solution)/shard_map/ppermute | solution.py:106
  572.1 89.0 %collective-permute-start.65 = (bf16[640,512]{1,0:T(8,128)(2,1)}, bf16[640,512]{1,0:T(8,128)(2,1)}, u32[]{:S(2)}, u32[]{:S(2)}) collective-permute-start(bf16[640,512]{1,0:T(8,128)(2,1)} %convolution_convert_fusion.20), channel_id=1, source_target_pairs={{0,16},{8,24},{16,32},{24,40},{32,48},{40,56},{48,0},{56,8},{1,17}... | collective-permute-start | bytes 1966088 | tf_op jit(solution)/shard_map/ppermute | solution.py:90
  617.4 44.8 %collective-permute-start.67 = (bf16[640,512]{1,0:T(8,128)(2,1)}, bf16[640,512]{1,0:T(8,128)(2,1)}, u32[]{:S(2)}, u32[]{:S(2)}) collective-permute-start(bf16[640,512]{1,0:T(8,128)(2,1)} %fusion.64), channel_id=1, source_target_pairs={{0,48},{8,56},{16,0},{24,8},{32,16},{40,24},{48,32},{56,40},{1,49}... | collective-permute-start | bytes 1966088 | tf_op jit(solution)/shard_map/ppermute | solution.py:90
  618.9 85.5 %collective-permute-start.71 = (bf16[256,2560]{1,0:T(8,128)(2,1)}, bf16[256,2560]{1,0:T(8,128)(2,1)}, u32[]{:S(2)}, u32[]{:S(2)}) collective-permute-start(bf16[256,2560]{1,0:T(8,128)(2,1)} %fusion.24), channel_id=1, source_target_pairs={{0,6},{1,7},{2,0},{3,1},{4,2},{5,3},{6,4},{7,5},{8,14},{9,15},{10,... | collective-permute-start | bytes 3932168 | tf_op jit(solution)/shard_map/ppermute | solution.py:94
  655.3 49.2 %collective-permute-start.69 = (bf16[256,2560]{1,0:T(8,128)(2,1)}, bf16[256,2560]{1,0:T(8,128)(2,1)}, u32[]{:S(2)}, u32[]{:S(2)}) collective-permute-start(bf16[256,2560]{1,0:T(8,128)(2,1)} %fusion.27), channel_id=1, source_target_pairs={{0,2},{1,3},{2,4},{3,5},{4,6},{5,7},{6,0},{7,1},{8,10},{9,11},{10,... | collective-permute-start | bytes 3932168 | tf_op jit(solution)/shard_map/ppermute | solution.py:94
  710.0 62.6 %collective-permute-start.89 = (bf16[128,960]{1,0:T(8,128)(2,1)S(1)}, bf16[128,960]{1,0:T(8,128)(2,1)S(1)}, u32[]{:S(2)}, u32[]{:S(2)}) collective-permute-start(bf16[128,960]{1,0:T(8,128)(2,1)S(1)} %get-tuple-element.60), channel_id=1, source_target_pairs={{0,64},{64,0},{1,65},{65,1},{2,66},{66,2},{3,67},{67,3},{4,68},{68... | collective-permute-start | bytes 737288 | tf_op jit(solution)/shard_map/ppermute | solution.py:106
  (289 other events, 3489.7 us)

commit v2 on v1

--- a/solution.py
+++ b/solution.py
@@ -118,13 +118,6 @@
     other = step(chunk(-way).astype(BF16), -way)
     nearer = (chunk(way).astype(F32) + relayed.astype(F32)).astype(BF16)
     return chunk(0).astype(F32) + other.astype(F32) + step(nearer, way).astype(F32)
-
-
-def direct_sum(step, chunk):
-    total = chunk(0).astype(F32)
-    for distance in (1, -1, 2):
-        total = total + step(chunk(distance).astype(BF16), distance).astype(F32)
-    return total
 
 
 class Place:
@@ -145,7 +138,7 @@
             (row // PART == self.z_shard[None]) & (row % PART == (column % PADDED)[None])
         ).astype(BF16)
         quarters = jnp.repeat(jnp.stack([(self.x + d) % 4 for d in DISTANCES]), SPREAD // 4)
-        shards = jnp.tile(jnp.repeat(self.near_shards, ROW_QUARTER), 4)
+        shards = jnp.tile(jnp.repeat(jnp.arange(8, dtype=jnp.int32), ROW_QUARTER), 4)
         inner = quarters * ROW_QUARTER + column % ROW_QUARTER
         self.by_x = ((row // PART == shards[None]) & (row % PART == inner[None])).astype(BF16)
 
@@ -185,19 +178,9 @@
     return (mine, sibling(mine), blocks[-1])
 
 
-def gather_down(place, own):
-    other = y_near(own)
-    low, high = (jnp.where(place.y == 0, own, other), jnp.where(place.y == 0, other, own))
-    pair = jnp.concatenate([low, high], axis=0)
-    blocks = ring_gather(z_step, -1, pair)
-    mine = jnp.concatenate(blocks, axis=0)
-    return (mine, sibling(mine), blocks[-1])
-
-
 def gather_column(place, own):
     quarter = lax.dynamic_slice_in_dim(own, place.x * ROW_QUARTER, ROW_QUARTER, 0)
-    pair = jnp.concatenate([quarter, y_near(quarter)], axis=0)
-    return ring_gather(z_step, -1, pair)
+    return lax.all_gather(quarter, "fsdp", axis=0, tiled=True)
 
 
 def gather_wide(column):
@@ -209,13 +192,12 @@
     return (mine, sibling(mine), far[0])
 
 
-def layer_weights(place, column, first, down):
+def layer_weights(place, first, column, low):
     one = gather_first(place, first)
     two = gather_wide(column)
-    low = gather_down(place, down)
     gains = one[0].reshape(8, PADDED, UNIT)[:, PART : PART + 2, :PADDED]
     gains = backward_product(gains.transpose(1, 0, 2).reshape(2, SPREAD), place.by_z)
-    return (one, two, low, gains[:1], gains[1:])
+    return (one, two, (low, sibling(low)), gains[:1], gains[1:])
 
 
 def gather_rows(own):
@@ -228,17 +210,6 @@
     pair = ring_sum(z_step, -1, lambda distance: parts[DISTANCES.index(distance)])
     rows = pair.shape[0] // 2
     return pair[:rows] + y_near(pair[rows:].astype(BF16)).astype(F32)
-
-
-def down_columns(place, hidden):
-    size = 2 * FF_PART
-    return jnp.concatenate(
-        [
-            lax.dynamic_slice_in_dim(hidden, (place.z + d) % 4 * size, size, 1)
-            for d in DISTANCES
-        ],
-        axis=1,
-    )
 
 
 def forward_layer(place, inputs, weights, cosine_table, sine_portion, allowed):
@@ -281,7 +252,7 @@
     inv_two = rms_scale(middle)
     normed_two = spread((middle * inv_two * gain_two).astype(BF16), place.by_x)
     gate_pre, up_pre = place.roles(product(normed_two, two[0]), product(normed_two, two[1]))
-    hidden = down_columns(place, (jax.nn.silu(gate_pre) * up_pre).astype(BF16))
+    hidden = (jax.nn.silu(gate_pre) * up_pre).astype(BF16)
     left, right = place.roles(product(hidden, low[0]), product(hidden, low[1]))
     result = middle + jnp.concatenate([left, right[:, DOWN_SKIP:]], axis=1)
     stored = (
@@ -322,32 +293,17 @@
     return chunk
 
 
-def by_quarter(place, block, rows):
-    quarters = block.reshape(4, rows, block.shape[-1])
-
-    def quarter(distance):
-        return lax.dynamic_index_in_dim(quarters, (place.x + distance) % 4, 0, keepdims=False)
-
-    return quarter
-
-
 def reduce_first(left, right):
     return ring_sum(z_step, 1, partial_chunks(left, right))
 
 
-def reduce_down(place, left, right):
-    pair = ring_sum(z_step, -1, partial_chunks(left, right)).astype(BF16)
-    pair = pair.reshape(2, PADDED, UNIT)
-    return jnp.concatenate(
-        [
-            lax.dynamic_index_in_dim(pair, place.y, 0, keepdims=False),
-            lax.dynamic_index_in_dim(pair, 1 - place.y, 0, keepdims=False),
-        ],
-        axis=0,
-    ).astype(F32)
-
-
-def reduce_wide(left, right):
+def reduce_down(left, right):
+    return lax.psum_scatter(
+        outer_sum(left, right).astype(BF16), "fsdp", scatter_dimension=0, tiled=True
+    )
+
+
+def reduce_wide(place, left, right):
     chunk = partial_chunks(left, right)
     half = SPREAD // 8
     from_before = x_step(outer_sum(left[:, -2 * half : -half], right).astype(BF16), 1)
@@ -359,31 +315,28 @@
         + x_step(after.astype(BF16), 1).astype(F32)
         + x_step(before.astype(BF16), -1).astype(F32)
     )
-    parts = column.reshape(4, 2 * ROW_QUARTER, 2 * UNIT)
-    pair = ring_sum(z_step, 1, lambda distance: parts[DISTANCES.index(distance)])
-    quarter = pair[:ROW_QUARTER] + y_near(pair[ROW_QUARTER:].astype(BF16)).astype(F32)
+    parts = column.reshape(4, 2, ROW_QUARTER, 2 * UNIT)
+
+    def part(distance):
+        return lax.dynamic_index_in_dim(parts, (place.z + distance) % 4, 0, keepdims=False)
+
+    pair = ring_sum(z_step, 1, part)
+    mine = lax.dynamic_index_in_dim(pair, place.y, 0, keepdims=False)
+    other = lax.dynamic_index_in_dim(pair, 1 - place.y, 0, keepdims=False)
+    quarter = mine + y_near(other.astype(BF16)).astype(F32)
     return ((from_before, from_after), column, quarter)
 
 
-def quarter_of(place, pair):
+def finish_wide(place, down, wide):
+    whole = jnp.zeros((4, ROW_QUARTER, 2 * UNIT), BF16)
+    whole = lax.dynamic_update_slice_in_dim(whole, wide.astype(BF16)[None], place.x, 0)
+    both = [down.reshape(PADDED, UNIT), whole.reshape(PADDED, 2 * UNIT)]
+    return lax.psum(jnp.concatenate(both, axis=1), "dp")
+
+
+def finish_first(pair, early):
     block = pair[:PADDED] + y_near(pair[PADDED:].astype(BF16)).astype(F32)
-    return direct_sum(x_step, by_quarter(place, block, ROW_QUARTER))
-
-
-def finish(place, quarter):
-    low = quarter.astype(BF16)
-    piece = (low.astype(F32) + y_far(low).astype(F32)).astype(BF16)
-    whole = jnp.zeros((4,) + piece.shape, BF16)
-    for distance in DISTANCES:
-        block = step_from(piece, distance)
-        whole = lax.dynamic_update_slice_in_dim(
-            whole, block[None], (place.x + distance) % 4, 0
-        )
-    return whole.reshape(-1, piece.shape[-1])
-
-
-def step_from(piece, distance):
-    return piece if distance == 0 else x_step(piece, -distance)
+    return lax.psum(gate(block, early).astype(BF16), "dp")
 
 
 def backward_layer(
@@ -412,16 +365,7 @@
     right_low = grad_low[:, WIDTH - DOWN_COLS :]
     right_once = jnp.where(jnp.arange(DOWN_COLS)[None] < DOWN_SKIP, 0, right_low)
     mine_low, other_low = place.roles(left_low, right_once)
-    hidden_grads = backward_product(mine_low, low[0]) + backward_product(other_low, low[1])
-    size = 2 * FF_PART
-    hidden_grad = jnp.zeros_like(hidden_grads)
-    for at, distance in enumerate(DISTANCES):
-        hidden_grad = lax.dynamic_update_slice_in_dim(
-            hidden_grad,
-            hidden_grads[:, at * size : (at + 1) * size],
-            (place.z + distance) % 4 * size,
-            1,
-        )
+    hidden_grad = backward_product(mine_low, low[0]) + backward_product(other_low, low[1])
     sigmoid_gate = jax.nn.sigmoid(gate_pre)
     grad_gate = (
         hidden_grad * up_pre * sigmoid_gate * (1.0 + gate_pre * (1.0 - sigmoid_gate))
@@ -434,8 +378,8 @@
         jnp.concatenate([place.role(left_low, right_low), mine], axis=1),
         jnp.concatenate([place.role(right_low, left_low), other], axis=1),
     )
-    down = reduce_down(place, left_rows[:, : 2 * UNIT], right_rows[:, :DOWN_COLS])
-    wide = reduce_wide(left_rows[:, 2 * UNIT :], right_rows[:, DOWN_COLS:])
+    down = reduce_down(left_rows[:, : 2 * UNIT], right_rows[:, :DOWN_COLS])
+    wide = reduce_wide(place, left_rows[:, 2 * UNIT :], right_rows[:, DOWN_COLS:])
     grad_normed_two = unspread(spread_two, place.by_x)
     unit_two = middle * inv_two
     grad_gain_two = jnp.sum(grad_normed_two * unit_two, axis=0)
@@ -520,7 +464,7 @@
     )
     right_rows = jnp.concatenate([right_rows[:, :UNIT], right_rows[:, UNIT:], gain_rows], axis=0)
     return (
-        gate(grad_in, down, column),
+        gate(grad_in, column),
         (reduce_first(left_rows, right_rows), down, wide),
     )
 
@@ -572,11 +516,11 @@
         layer_packs[0].append(jnp.where(first, kept, other))
         layer_packs[1].append(jnp.where(first, other, kept))
     first_pack, wide_pack, down_pack = layer_packs[0]
-    blocks = gather_column(place, wide_pack)
-    column = jnp.concatenate(blocks, axis=0)
-    weights_first = layer_weights(place, column, first_pack, gate(down_pack, blocks[3]))
+    column = gather_column(place, wide_pack)
+    low = lax.all_gather(gate(down_pack, column), "fsdp", axis=0, tiled=True)
+    weights_first = layer_weights(place, first_pack, column, low)
     first_pack, wide_pack, down_pack = layer_packs[1]
-    blocks = gather_column(place, gate(wide_pack, blocks[3]))
+    column = gather_column(place, gate(wide_pack, low))
 
     seq_lengths = jnp.where(first, lengths[0, 0], lengths[0, 1])
     inner = jnp.arange(rows_dev, dtype=jnp.int32)
@@ -592,21 +536,18 @@
 
     geometry = (cosine_table, sine_portion, allowed)
     middle, stored_first = forward_layer(place, inputs, weights_first, *geometry)
-    blocks[0], first_pack, down_pack = gate(
-        (blocks[0], first_pack, down_pack), stored_first[4]
-    )
-    column = jnp.concatenate(blocks, axis=0)
-    weights_second = layer_weights(place, column, first_pack, down_pack)
+    low = lax.all_gather(gate(down_pack, column), "fsdp", axis=0, tiled=True)
+    first_pack = gate(first_pack, stored_first[4])
+    weights_second = layer_weights(place, first_pack, column, low)
     middle = middle.astype(BF16).astype(F32)
     result, stored_second = forward_layer(place, middle, weights_second, *geometry)
     grad, pending = backward_layer(
         place, cotangent * live_rows[:, None], weights_second, stored_second, ((), (), ()), *geometry
     )
     pair, down, wide = pending
-    wide = jnp.concatenate([quarter_of(place, down), wide], axis=1)
-    low = quarter_of(place, pair)
-    early_second, late_second = (finish(place, wide), finish(place, low))
-    waits = ((pair,), (wide, low), (early_second, late_second))
+    early_second = finish_wide(place, down, wide)
+    late_second = finish_first(pair, early_second)
+    waits = ((pair, wide), (), (early_second, late_second))
     grad = grad.astype(BF16).astype(F32)
     grad, remaining = backward_layer(
         place, grad, weights_first, stored_first, waits, *geometry
@@ -619,8 +560,8 @@
     )[None, :, None]
 
     pair, down, wide = remaining
-    early_first = finish(place, jnp.concatenate([quarter_of(place, down), wide], axis=1))
-    late_first = finish(place, quarter_of(place, pair))
+    early_first = finish_wide(place, down, wide)
+    late_first = finish_first(pair, early_first)
     sums = []
     for for_first, for_second in ((early_first, early_second), (late_first, late_second)):
         own = jnp.where(first, for_first, for_second)

time: 814 us -> 994 us (1.22)
  waiting for transfers between devices: 292 us -> 500 us
  starting transfers between devices: 147 us -> 64.2 us
  matrix products: 141 us -> 177 us
  between operations: 24.3 us -> 37.3 us
    psum x0 -> x3, waiting for transfers between devices: none -> 189 us  [the longest x2 170 us: finish_first(): return lax.psum(gate(block, early).astype(BF16), 'dp')]
    reduce_scatter x0 -> x2, waiting for transfers between devices: none -> 60 us  [reduce_down(): lax.psum_scatter(outer_sum(left, right).astype(BF16), 'fsdp', scatter_dim...]
    ppermute x40 -> x16, waiting for transfers between devices: 103 us -> 65 us  [x_step(): lax.ppermute(value, 'dp', [(i, (i + 2 * step) % 8) for i in range(8)])]
    ppermute x40 -> x16, starting transfers between devices: 54.5 us -> 20.9 us  [x_step(): lax.ppermute(value, 'dp', [(i, (i + 2 * step) % 8) for i in range(8)])]
    ppermute x48 -> x30, starting transfers between devices: 58.2 us -> 33.7 us  [z_step(): lax.ppermute(value, 'fsdp', [(i, (i + 2 * step) % 8) for i in range(8)])]
    ppermute x16 -> x10, starting transfers between devices: 19.7 us -> 5.48 us  [y_near(): return lax.ppermute(value, 'fsdp', [(i, i ^ 1) for i in range(8)])]
    dot_general x16, matrix products: 24.1 us -> 37.8 us  [product(): return jnp.dot(left, right, preferred_element_type=F32)]
    ppermute x4 -> x0, waiting for transfers between devices: 11.3 us -> none  [y_far(): return lax.ppermute(value, 'dp', [(i, i ^ 1) for i in range(8)])]
  transfers between devices with their start and end apart: 129 -> 86, of which waited for: 58 -> 41; matrix products, arithmetic and copies ran while one was open for 37% -> 36% of each run, Pallas kernels for 0% -> 0%
where the time goes in v2:
time: 994 us; the launch traced here: 981 us
  waiting for transfers between devices  500 us (50%)
  matrix products  177 us (18%)
  local copies, waits for them, and re-layouts  101 us (10%)
  other arithmetic  101 us (10%)
  starting transfers between devices  64.2 us (6%)
  between operations  37.3 us (4%)
    psum x2, waiting for transfers between devices, finish_first(): return lax.psum(gate(block, early).astype(BF16), 'dp')  170 us
    ppermute x30, waiting for transfers between devices, z_step(): lax.ppermute(value, 'fsdp', [(i, (i + 2 * step) % 8) for i in range(8)])  149 us
    ppermute x16, waiting for transfers between devices, x_step(): lax.ppermute(value, 'dp', [(i, (i + 2 * step) % 8) for i in range(8)])  65 us
    reduce_scatter x2, waiting for transfers between devices, reduce_down(): lax.psum_scatter(outer_sum(left, right).astype(BF16), 'fsdp', scatter_dim...  60 us
    dot_general x24, matrix products, backward_product(): lax.dot_general(grad, weight, (((1,), (1,)), ((), ())), preferred_element...  49.1 us
    dot_general x20, matrix products, outer_sum(): lax.dot_general(left, right, (((0,), (0,)), ((), ())), preferred_element_...  39 us
    unnamed x431, local copies, waits for them, and re-layouts  38.6 us
    dot_general x16, matrix products, product(): return jnp.dot(left, right, preferred_element_type=F32)  37.8 us
  transfers between devices with their start and end apart: 86, of which 41 were waited for; matrix products, arithmetic and copies ran while one was open for 36% of the time, Pallas kernels for 0%

profile of v2, /device:TPU:0, one launch (start us, length us, event | category | flops | bytes accessed | tf_op | source)
XLA Modules:
  0.0 980.8 jit_solution(6238204273437032987)
XLA Ops:
  25.1 7.1 collective-permute-done.2
  41.7 10.8 %collective-permute-done.3 = bf16[256,1280]{1,0:T(8,128)(2,1)} collective-permute-done((bf16[256,1280]{1,0:T(8,128)(2,1)}, bf16[256,1280]{1,0:T(8,128)(2,1)}, u32[]{:S(2)}, u32[]{:S(2)}) %collective-permute-start.3) | collective-permute-done | bytes 655392 | tf_op jit(solution)/shard_map/ppermute | solution.py:90
  56.2 23.7 %collective-permute-done.5 = bf16[256,1280]{1,0:T(8,128)(2,1)S(1)} collective-permute-done((bf16[256,1280]{1,0:T(8,128)(2,1)}, bf16[256,1280]{1,0:T(8,128)(2,1)S(1)}, u32[]{:S(2)}, u32[]{:S(2)}) %collective-permute-start.5) | collective-permute-done | bytes 655392 | tf_op jit(solution)/shard_map/ppermute | solution.py:90
  96.8 19.3 %collective-permute-done.12 = bf16[256,2560]{1,0:T(8,128)(2,1)} collective-permute-done((bf16[256,2560]{1,0:T(8,128)(2,1)}, bf16[256,2560]{1,0:T(8,128)(2,1)}, u32[]{:S(2)}, u32[]{:S(2)}) %collective-permute-start.12) | collective-permute-done | bytes 1310752 | tf_op jit(solution)/shard_map/ppermute | solution.py:94
  150.6 9.3 collective-permute-done.8
  162.1 7.2 collective-permute-done.10
  210.8 10.7 %collective-permute-done.22 = bf16[256,1280]{1,0:T(8,128)(2,1)S(1)} collective-permute-done((bf16[256,1280]{1,0:T(8,128)(2,1)}, bf16[256,1280]{1,0:T(8,128)(2,1)S(1)}, u32[]{:S(2)}, u32[]{:S(2)}) %collective-permute-start.22) | collective-permute-done | bytes 655392 | tf_op jit(solution)/shard_map/ppermute | solution.py:90
  221.5 15.6 %collective-permute-done.23 = bf16[256,1280]{1,0:T(8,128)(2,1)S(1)} collective-permute-done((bf16[256,1280]{1,0:T(8,128)(2,1)}, bf16[256,1280]{1,0:T(8,128)(2,1)S(1)}, u32[]{:S(2)}, u32[]{:S(2)}) %collective-permute-start.23) | collective-permute-done | bytes 655392 | tf_op jit(solution)/shard_map/ppermute | solution.py:90
  282.6 10.6 %collective-permute-done.26 = bf16[256,640]{1,0:T(8,128)(2,1)S(1)} collective-permute-done((bf16[256,640]{1,0:T(8,128)(2,1)S(1)}, bf16[256,640]{1,0:T(8,128)(2,1)S(1)}, u32[]{:S(2)}, u32[]{:S(2)}) %collective-permute-start.26) | collective-permute-done | bytes 327712 | tf_op jit(solution)/shard_map/ppermute | solution.py:90
  293.5 13.8 %collective-permute-done.28 = bf16[256,640]{1,0:T(8,128)(2,1)S(1)} collective-permute-done((bf16[256,640]{1,0:T(8,128)(2,1)S(1)}, bf16[256,640]{1,0:T(8,128)(2,1)S(1)}, u32[]{:S(2)}, u32[]{:S(2)}) %collective-permute-start.28) | collective-permute-done | bytes 327712 | tf_op jit(solution)/shard_map/ppermute | solution.py:90
  383.3 8.6 fusion.3
  400.4 7.2 fusion.5
  464.2 9.2 collective-permute-done.40
  473.4 6.9 collective-permute-done.38
  509.2 9.1 collective-permute-done.57
  522.3 8.9 collective-permute-done.53
  538.5 8.2 collective-permute-done.48
  564.1 7.2 fusion.2
  619.0 8.9 collective-permute-done.49
  650.8 7.2 collective-permute-done.67
  658.1 18.7 %all-reduce.18.cloned.1.call-done = bf16[128,3840]{1,0:T(8,128)(2,1)} async-done(((bf16[128,3840]{1,0:T(8,128)(2,1)}), bf16[128,3840]{1,0:T(8,128)(2,1)}) %all-reduce.18.cloned.1.call-update) | async-done | bytes 983056 | tf_op jit(solution)/shard_map/psum | solution.py:334
  681.1 60.0 %reduce-scatter.3.cloned.1.call-done = bf16[320,512]{1,0:T(8,128)(2,1)} async-done(((bf16[2560,512]{1,0:T(8,128)(2,1)}), bf16[320,512]{1,0:T(8,128)(2,1)}) %reduce-scatter.3.cloned.1.call-update) | async-done | bytes 327696 | tf_op jit(solution)/shard_map/reduce_scatter | solution.py:301
  747.7 87.2 %all-reduce.22.cloned.1.call-done = (bf16[128,1280]{1,0:T(8,128)(2,1)}, bf16[128,3840]{1,0:T(8,128)(2,1)}) async-done(((bf16[128,1280]{1,0:T(8,128)(2,1)}, bf16[128,3840]{1,0:T(8,128)(2,1)}), (bf16[128,1280]{1,0:T(8,128)(2,1)}, bf16[128,3840]{1,0:T(8,128)(2,1)})) %all-reduce.22.cloned.1.call-update) | async-done | bytes 1310736 | tf_op jit(solution)/shard_map/psum | solution.py:339
  880.3 82.6 %all-reduce.20.cloned.1.call-done = bf16[128,1280]{1,0:T(8,128)(2,1)} async-done(((bf16[128,1280]{1,0:T(8,128)(2,1)}), bf16[128,1280]{1,0:T(8,128)(2,1)}) %all-reduce.20.cloned.1.call-update) | async-done | bytes 327696 | tf_op jit(solution)/shard_map/psum | solution.py:339
  (890 shorter events, 485.2 us)
Async XLA Ops:
  7.2 76.3 %all-gather.5.cloned.1.call-start = ((), (), s32[]{:S(2)}) async-start(), calls=%async_computation.2 | async-start | bytes 1474560 | tf_op jit(solution)/shard_map/all_gather | solution.py:183
  9.7 70.4 %collective-permute-start = (bf16[128,960]{1,0:T(8,128)(2,1)}, bf16[128,960]{1,0:T(8,128)(2,1)}, u32[]{:S(2)}, u32[]{:S(2)}) collective-permute-start(bf16[128,960]{1,0:T(8,128)(2,1)} %bitcast_select_fusion.5), channel_id=1, source_target_pairs={{0,64},{64,0},{1,65},{65,1},{2,66},{66,2},{3,67},{67,3},{4,68},{68... | collective-permute-start | bytes 737288 | tf_op jit(solution)/shard_map/ppermute | solution.py:106
  13.0 81.4 %collective-permute-start.18 = (bf16[320,512]{1,0:T(8,128)(2,1)}, bf16[320,512]{1,0:T(8,128)(2,1)}, u32[]{:S(2)}, u32[]{:S(2)}) collective-permute-start(bf16[320,512]{1,0:T(8,128)(2,1)} %select_bitcast_fusion), channel_id=1, source_target_pairs={{0,64},{64,0},{1,65},{65,1},{2,66},{66,2},{3,67},{67,3},{4,68},{68... | collective-permute-start | bytes 983048 | tf_op jit(solution)/shard_map/ppermute | solution.py:106
  37.5 155.9 %all-gather.7.cloned.1.call-start = ((), (), s32[]{:S(2)}) async-start(), calls=%async_computation.3 | async-start | bytes 2949120 | tf_op jit(solution)/shard_map/all_gather | solution.py:520
  79.9 44.8 %collective-permute-start.6 = (bf16[1024,1280]{1,0:T(8,128)(2,1)S(1)}, bf16[1024,1280]{1,0:T(8,128)(2,1)}, u32[]{:S(2)}, u32[]{:S(2)}) collective-permute-start(bf16[1024,1280]{1,0:T(8,128)(2,1)S(1)} %constant_dynamic-update-slice_fusion), channel_id=1, source_target_pairs={{0,64},{64,0},{1,65},{65,1},{2,66},{66,2},{3,67},{67,3},{4,68},{68... | collective-permute-start | bytes 7864328 | tf_op jit(solution)/shard_map/ppermute | solution.py:106
  85.1 33.3 %collective-permute-start.13 = (bf16[256,2560]{1,0:T(8,128)(2,1)}, bf16[256,2560]{1,0:T(8,128)(2,1)}, u32[]{:S(2)}, u32[]{:S(2)}) collective-permute-start(bf16[256,2560]{1,0:T(8,128)(2,1)} %all-gather.5.cloned.1.call-done), channel_id=1, source_target_pairs={{0,6},{1,7},{2,0},{3,1},{4,2},{5,3},{6,4},{7,5},{8,14},{9,15},{10,... | collective-permute-start | bytes 3932168 | tf_op jit(solution)/shard_map/ppermute | solution.py:94
  95.3 144.5 %all-gather.9.cloned.1.call-start = ((), (), s32[]{:S(2)}) async-start(), calls=%async_computation.4 | async-start | bytes 1474560 | tf_op jit(solution)/shard_map/all_gather | solution.py:183
  120.3 39.6 %collective-permute-start.15 = (bf16[128,2560]{1,0:T(8,128)(2,1)}, bf16[128,2560]{1,0:T(8,128)(2,1)}, u32[]{:S(2)}, u32[]{:S(2)}) collective-permute-start(bf16[128,2560]{1,0:T(8,128)(2,1)} %slice.537), channel_id=1, source_target_pairs={{0,6},{1,7},{2,0},{3,1},{4,2},{5,3},{6,4},{7,5},{8,14},{9,15},{10,... | collective-permute-start | bytes 1966088 | tf_op jit(solution)/shard_map/ppermute | solution.py:94
  162.0 82.3 %collective-permute-start.16 = (bf16[1024,2560]{1,0:T(8,128)(2,1)}, bf16[1024,2560]{1,0:T(8,128)(2,1)}, u32[]{:S(2)}, u32[]{:S(2)}) collective-permute-start(bf16[1024,2560]{1,0:T(8,128)(2,1)} %constant_dynamic-update-slice_fusion.10), channel_id=1, source_target_pairs={{0,64},{64,0},{1,65},{65,1},{2,66},{66,2},{3,67},{67,3},{4,68},{68... | collective-permute-start | bytes 15728648 | tf_op jit(solution)/shard_map/ppermute | solution.py:106
  197.7 145.5 %all-gather.11.cloned.1.call-start = ((), (), s32[]{:S(2)}) async-start(), calls=%async_computation.5 | async-start | bytes 2949120 | tf_op jit(solution)/shard_map/all_gather | solution.py:539
  202.3 47.5 %collective-permute-start.19 = (bf16[2560,512]{1,0:T(8,128)(2,1)}, bf16[2560,512]{1,0:T(8,128)(2,1)}, u32[]{:S(2)}, u32[]{:S(2)}) collective-permute-start(bf16[2560,512]{1,0:T(8,128)(2,1)} %all-gather.7.cloned.1.call-done), channel_id=1, source_target_pairs={{0,64},{64,0},{1,65},{65,1},{2,66},{66,2},{3,67},{67,3},{4,68},{68... | collective-permute-start | bytes 7864328 | tf_op jit(solution)/shard_map/ppermute | solution.py:106
  203.2 634.2 %collective-permute-start.69 = (bf16[128,2048]{1,0:T(8,128)(2,1)}, bf16[128,2048]{1,0:T(8,128)(2,1)}, u32[]{:S(2)}, u32[]{:S(2)}) collective-permute-start(bf16[128,2048]{1,0:T(8,128)(2,1)} %pad_maximum_fusion.26), channel_id=1, source_target_pairs={{0,64},{64,0},{1,65},{65,1},{2,66},{66,2},{3,67},{67,3},{4,68},{68... | collective-permute-start | bytes 1572872 | tf_op jit(solution)/shard_map/ppermute | solution.py:106
  244.2 339.2 %reduce-scatter.5.cloned.1.call-start = ((), (), s32[]{:S(2)}) async-start(), calls=%async_computation.7 | async-start | bytes 2949120 | tf_op jit(solution)/shard_map/reduce_scatter | solution.py:301
  271.1 39.2 %collective-permute-start.29 = (bf16[256,2560]{1,0:T(8,128)(2,1)}, bf16[256,2560]{1,0:T(8,128)(2,1)}, u32[]{:S(2)}, u32[]{:S(2)}) collective-permute-start(bf16[256,2560]{1,0:T(8,128)(2,1)} %all-gather.9.cloned.1.call-done), channel_id=1, source_target_pairs={{0,2},{1,3},{2,4},{3,5},{4,6},{5,7},{6,0},{7,1},{8,10},{9,11},{10,... | collective-permute-start | bytes 3932168 | tf_op jit(solution)/shard_map/ppermute | solution.py:94
  272.5 39.7 %collective-permute-start.30 = (bf16[256,2560]{1,0:T(8,128)(2,1)}, bf16[256,2560]{1,0:T(8,128)(2,1)}, u32[]{:S(2)}, u32[]{:S(2)}) collective-permute-start(bf16[256,2560]{1,0:T(8,128)(2,1)} %all-gather.9.cloned.1.call-done), channel_id=1, source_target_pairs={{0,6},{1,7},{2,0},{3,1},{4,2},{5,3},{6,4},{7,5},{8,14},{9,15},{10,... | collective-permute-start | bytes 3932168 | tf_op jit(solution)/shard_map/ppermute | solution.py:94
  293.3 225.4 %collective-permute-start.17 = (bf16[128,3584]{1,0:T(8,128)(2,1)}, bf16[128,3584]{1,0:T(8,128)(2,1)}, u32[]{:S(2)}, u32[]{:S(2)}) collective-permute-start(bf16[128,3584]{1,0:T(8,128)(2,1)} %pad_maximum_fusion.17), channel_id=1, source_target_pairs={{0,64},{64,0},{1,65},{65,1},{2,66},{66,2},{3,67},{67,3},{4,68},{68... | collective-permute-start | bytes 2752520 | tf_op jit(solution)/shard_map/ppermute | solution.py:106
  441.3 235.5 %all-reduce.18.cloned.1.call-start = ((), (), s32[]{:S(2)}) async-start(), calls=%async_computation.8 | async-start | bytes 1966080 | tf_op jit(solution)/shard_map/psum | solution.py:334
  464.1 34.9 %collective-permute-start.51 = (bf16[128,2560]{1,0:T(8,128)(2,1)S(1)}, bf16[128,2560]{1,0:T(8,128)(2,1)S(1)}, u32[]{:S(2)}, u32[]{:S(2)}) collective-permute-start(bf16[128,2560]{1,0:T(8,128)(2,1)S(1)} %pad_maximum_fusion.23), channel_id=1, source_target_pairs={{0,64},{64,0},{1,65},{65,1},{2,66},{66,2},{3,67},{67,3},{4,68},{68... | collective-permute-start | bytes 1966088 | tf_op jit(solution)/shard_map/ppermute | solution.py:106
  587.6 153.5 %reduce-scatter.3.cloned.1.call-start = ((), (), s32[]{:S(2)}) async-start(), calls=%async_computation.6 | async-start | bytes 2949120 | tf_op jit(solution)/shard_map/reduce_scatter | solution.py:301
  590.5 37.4 %collective-permute-start.49 = (bf16[256,2560]{1,0:T(8,128)(2,1)}, bf16[256,2560]{1,0:T(8,128)(2,1)}, u32[]{:S(2)}, u32[]{:S(2)}) collective-permute-start(bf16[256,2560]{1,0:T(8,128)(2,1)} %fusion.24), channel_id=1, source_target_pairs={{0,6},{1,7},{2,0},{3,1},{4,2},{5,3},{6,4},{7,5},{8,14},{9,15},{10,... | collective-permute-start | bytes 3932168 | tf_op jit(solution)/shard_map/ppermute | solution.py:94
  603.8 231.1 %all-reduce.22.cloned.1.call-start = ((), (), s32[]{:S(2)}) async-start(), calls=%async_computation.10 | async-start | bytes 2621440 | tf_op jit(solution)/shard_map/psum | solution.py:339
  610.9 68.4 %collective-permute-start.68 = (bf16[128,1280]{1,0:T(8,128)(2,1)}, bf16[128,1280]{1,0:T(8,128)(2,1)}, u32[]{:S(2)}, u32[]{:S(2)}) collective-permute-start(bf16[128,1280]{1,0:T(8,128)(2,1)} %slice.864), channel_id=1, source_target_pairs={{0,8},{8,0},{16,24},{24,16},{32,40},{40,32},{48,56},{56,48},{1,9},... | collective-permute-start | bytes 983048 | tf_op jit(solution)/shard_map/ppermute | solution.py:98
  642.1 104.2 %collective-permute-start.70 = (bf16[128,2560]{1,0:T(8,128)(2,1)}, bf16[128,2560]{1,0:T(8,128)(2,1)}, u32[]{:S(2)}, u32[]{:S(2)}) collective-permute-start(bf16[128,2560]{1,0:T(8,128)(2,1)} %pad_maximum_fusion.24), channel_id=1, source_target_pairs={{0,64},{64,0},{1,65},{65,1},{2,66},{66,2},{3,67},{67,3},{4,68},{68... | collective-permute-start | bytes 1966088 | tf_op jit(solution)/shard_map/ppermute | solution.py:106
  743.4 219.5 %all-reduce.20.cloned.1.call-start = ((), (), s32[]{:S(2)}) async-start(), calls=%async_computation.9 | async-start | bytes 655360 | tf_op jit(solution)/shard_map/psum | solution.py:339
  (262 other events, 3656.6 us)
Sparse Core Ops, SparseCore 0:
  37.6 43.7 all-gather.4
  95.4 63.5 all-gather.6
  197.8 42.0 all-gather.8
  244.3 64.4 all-gather.10
  441.4 61.0 reduce-scatter.4
  587.8 89.0 all-reduce.17
  679.4 61.7 reduce-scatter.2
  744.4 90.4 all-reduce.21
  879.2 83.5 all-reduce.19

commit v3 on v1

--- a/solution.py
+++ b/solution.py
@@ -178,41 +178,48 @@
     return jax.tree.map(lambda part: jnp.where(late, jnp.zeros_like(part), part), value)
 
 
+def ring_gather_both(step, block):
+    before = step(block, 1)
+    after = step(block, -1)
+    far = (step(before[0], 1), step(after[1], -1))
+    layers = [[block[n], before[n], after[n], far[n]] for n in range(2)]
+    return (layers, (before, after))
+
+
 def gather_first(place, own):
-    pair = jnp.concatenate([own, y_near(own)], axis=0)
-    blocks = ring_gather(z_step, 1, pair)
-    mine = jnp.concatenate(blocks, axis=0)
-    return (mine, sibling(mine), blocks[-1])
-
-
-def gather_down(place, own):
+    pair = jnp.stack([own, y_near(own)], axis=1).reshape(2, 2 * PADDED, UNIT)
+    layers, near = ring_gather_both(z_step, pair)
+    return ([jnp.concatenate(blocks, axis=0) for blocks in layers], near)
+
+
+def gather_down(place, own, waits):
     other = y_near(own)
     low, high = (jnp.where(place.y == 0, own, other), jnp.where(place.y == 0, other, own))
-    pair = jnp.concatenate([low, high], axis=0)
-    blocks = ring_gather(z_step, -1, pair)
-    mine = jnp.concatenate(blocks, axis=0)
-    return (mine, sibling(mine), blocks[-1])
-
-
-def gather_column(place, own):
-    quarter = lax.dynamic_slice_in_dim(own, place.x * ROW_QUARTER, ROW_QUARTER, 0)
-    pair = jnp.concatenate([quarter, y_near(quarter)], axis=0)
-    return ring_gather(z_step, -1, pair)
-
-
-def gather_wide(column):
-    before = x_step(column, 1)
-    after = x_step(column, -1)
-    half = column.shape[0] // 2
-    far = [x_step(before[:half], 1), x_step(after[half:], -1)]
-    mine = jnp.concatenate([column, before, after] + far, axis=0)
-    return (mine, sibling(mine), far[0])
-
-
-def layer_weights(place, column, first, down):
-    one = gather_first(place, first)
-    two = gather_wide(column)
-    low = gather_down(place, down)
+    pair = jnp.stack([low, high], axis=1).reshape(2, 2 * FF_PART, DOWN_COLS)
+    pair = gate(pair, *waits)
+    layers, near = ring_gather_both(z_step, pair)
+    wholes = []
+    for blocks in layers:
+        whole = jnp.zeros((4,) + pair.shape[1:], BF16)
+        for distance, block in zip(DISTANCES, blocks):
+            whole = lax.dynamic_update_slice_in_dim(
+                whole, block[None], (place.z + distance) % 4, 0
+            )
+        wholes.append(whole.reshape(-1, DOWN_COLS))
+    return (wholes, near)
+
+
+def gather_wide(place, own):
+    quarter = lax.dynamic_slice_in_dim(own, place.x * ROW_QUARTER, ROW_QUARTER, 1)
+    pair = jnp.stack([quarter, y_near(quarter)], axis=1)
+    column = jnp.stack(ring_gather(z_step, -1, pair), axis=1)
+    column = column.reshape(2, SPREAD // 4, 2 * UNIT)
+    layers, near = ring_gather_both(x_step, column)
+    return ([jnp.concatenate(blocks, axis=0) for blocks in layers], near)
+
+
+def layer_weights(place, mine):
+    one, two, low = [(value, sibling(value)) for value in mine]
     gains = one[0].reshape(8, PADDED, UNIT)[:, PART : PART + 2, :PADDED]
     gains = backward_product(gains.transpose(1, 0, 2).reshape(2, SPREAD), place.by_z)
     return (one, two, low, gains[:1], gains[1:])
@@ -230,18 +237,7 @@
     return pair[:rows] + y_near(pair[rows:].astype(BF16)).astype(F32)
 
 
-def down_columns(place, hidden):
-    size = 2 * FF_PART
-    return jnp.concatenate(
-        [
-            lax.dynamic_slice_in_dim(hidden, (place.z + d) % 4 * size, size, 1)
-            for d in DISTANCES
-        ],
-        axis=1,
-    )
-
-
-def forward_layer(place, inputs, weights, cosine_table, sine_portion, allowed):
+def forward_layer(place, inputs, weights, waits, cosine_table, sine_portion, allowed):
     one, two, low, gain_one, gain_two = weights
     count_of_rows = inputs.shape[0]
     inv_one = rms_scale(inputs)
@@ -258,6 +254,7 @@
     )
     key_portion = turned[:, QUERY_HEADS:].reshape(count_of_rows, KV_WIDTH)
     key_value = gather_rows(jnp.concatenate([key_portion, value_part], axis=1))
+    key_value = gate(key_value, *waits[0])
     key_row_block = key_value[:, :KV_WIDTH].reshape(-1, KEY_VALUE_HEADS, HEAD_SIZE)
     value_row_block = key_value[:, KV_WIDTH:].reshape(-1, KEY_VALUE_HEADS, HEAD_SIZE)
     scores = (
@@ -273,6 +270,7 @@
     mixture = jnp.einsum(
         "ghqk,kgd->qghd", attention, value_row_block, preferred_element_type=F32
     )
+    mixture = gate(mixture, *waits[1])
     mixture = spread(
         mixture.astype(BF16).reshape(count_of_rows, QUERY_HEADS * HEAD_SIZE), place.by_z
     )
@@ -281,7 +279,7 @@
     inv_two = rms_scale(middle)
     normed_two = spread((middle * inv_two * gain_two).astype(BF16), place.by_x)
     gate_pre, up_pre = place.roles(product(normed_two, two[0]), product(normed_two, two[1]))
-    hidden = down_columns(place, (jax.nn.silu(gate_pre) * up_pre).astype(BF16))
+    hidden = (jax.nn.silu(gate_pre) * up_pre).astype(BF16)
     left, right = place.roles(product(hidden, low[0]), product(hidden, low[1]))
     result = middle + jnp.concatenate([left, right[:, DOWN_SKIP:]], axis=1)
     stored = (
@@ -336,7 +334,13 @@
 
 
 def reduce_down(place, left, right):
-    pair = ring_sum(z_step, -1, partial_chunks(left, right)).astype(BF16)
+    size = 2 * FF_PART
+
+    def chunk(distance):
+        part = lax.dynamic_slice_in_dim(left, (place.z + distance) % 4 * size, size, 1)
+        return outer_sum(part, right).astype(BF16)
+
+    pair = ring_sum(z_step, -1, chunk).astype(BF16)
     pair = pair.reshape(2, PADDED, UNIT)
     return jnp.concatenate(
         [
@@ -365,8 +369,11 @@
     return ((from_before, from_after), column, quarter)
 
 
-def quarter_of(place, pair):
-    block = pair[:PADDED] + y_near(pair[PADDED:].astype(BF16)).astype(F32)
+def across_y(pair):
+    return pair[:PADDED] + y_near(pair[PADDED:].astype(BF16)).astype(F32)
+
+
+def across_x(place, block):
     return direct_sum(x_step, by_quarter(place, block, ROW_QUARTER))
 
 
@@ -412,16 +419,7 @@
     right_low = grad_low[:, WIDTH - DOWN_COLS :]
     right_once = jnp.where(jnp.arange(DOWN_COLS)[None] < DOWN_SKIP, 0, right_low)
     mine_low, other_low = place.roles(left_low, right_once)
-    hidden_grads = backward_product(mine_low, low[0]) + backward_product(other_low, low[1])
-    size = 2 * FF_PART
-    hidden_grad = jnp.zeros_like(hidden_grads)
-    for at, distance in enumerate(DISTANCES):
-        hidden_grad = lax.dynamic_update_slice_in_dim(
-            hidden_grad,
-            hidden_grads[:, at * size : (at + 1) * size],
-            (place.z + distance) % 4 * size,
-            1,
-        )
+    hidden_grad = backward_product(mine_low, low[0]) + backward_product(other_low, low[1])
     sigmoid_gate = jax.nn.sigmoid(gate_pre)
     grad_gate = (
         hidden_grad * up_pre * sigmoid_gate * (1.0 + gate_pre * (1.0 - sigmoid_gate))
@@ -514,7 +512,7 @@
         jnp.concatenate([place.role(grad_query_key, output_side), place.role(none, value_side)], 1),
         jnp.concatenate([place.role(output_side, grad_query_key), place.role(value_side, none)], 1),
     )
-    left_rows = gate(left_rows, *waits[2])
+    left_rows = gate(left_rows, column, down, *waits[2])
     left_rows = jnp.concatenate(
         [left_rows[:, :SPREAD], left_rows[:, SPREAD:], gain_place.astype(BF16)], axis=0
     )
@@ -571,12 +569,13 @@
         other = sibling(jnp.where(first, one, zero))
         layer_packs[0].append(jnp.where(first, kept, other))
         layer_packs[1].append(jnp.where(first, other, kept))
-    first_pack, wide_pack, down_pack = layer_packs[0]
-    blocks = gather_column(place, wide_pack)
-    column = jnp.concatenate(blocks, axis=0)
-    weights_first = layer_weights(place, column, first_pack, gate(down_pack, blocks[3]))
-    first_pack, wide_pack, down_pack = layer_packs[1]
-    blocks = gather_column(place, gate(wide_pack, blocks[3]))
+    first_pack, wide_pack, down_pack = [jnp.stack(both) for both in zip(*layer_packs)]
+    wide, near_wide = gather_wide(place, wide_pack)
+    one, near_one = gather_first(place, first_pack)
+    down, near_down = gather_down(place, down_pack, near_one)
+    weights_first, weights_second = [
+        layer_weights(place, mine) for mine in zip(one, wide, down)
+    ]
 
     seq_lengths = jnp.where(first, lengths[0, 0], lengths[0, 1])
     inner = jnp.arange(rows_dev, dtype=jnp.int32)
@@ -591,22 +590,17 @@
     live_rows = (segment_mine < seq_lengths.shape[0]).astype(F32)
 
     geometry = (cosine_table, sine_portion, allowed)
-    middle, stored_first = forward_layer(place, inputs, weights_first, *geometry)
-    blocks[0], first_pack, down_pack = gate(
-        (blocks[0], first_pack, down_pack), stored_first[4]
-    )
-    column = jnp.concatenate(blocks, axis=0)
-    weights_second = layer_weights(place, column, first_pack, down_pack)
+    middle, stored_first = forward_layer(
+        place, inputs, weights_first, (near_wide, near_down), *geometry
+    )
     middle = middle.astype(BF16).astype(F32)
-    result, stored_second = forward_layer(place, middle, weights_second, *geometry)
+    result, stored_second = forward_layer(place, middle, weights_second, ((), ()), *geometry)
     grad, pending = backward_layer(
         place, cotangent * live_rows[:, None], weights_second, stored_second, ((), (), ()), *geometry
     )
     pair, down, wide = pending
-    wide = jnp.concatenate([quarter_of(place, down), wide], axis=1)
-    low = quarter_of(place, pair)
-    early_second, late_second = (finish(place, wide), finish(place, low))
-    waits = ((pair,), (wide, low), (early_second, late_second))
+    before = jnp.concatenate([pair, down], axis=1)
+    waits = ((), (pair, wide), ())
     grad = grad.astype(BF16).astype(F32)
     grad, remaining = backward_layer(
         place, grad, weights_first, stored_first, waits, *geometry
@@ -618,9 +612,13 @@
         first, jnp.stack([ends[0], received]), jnp.stack([received, ends[1]])
     )[None, :, None]
 
-    pair, down, wide = remaining
-    early_first = finish(place, jnp.concatenate([quarter_of(place, down), wide], axis=1))
-    late_first = finish(place, quarter_of(place, pair))
+    pair, down, wide_first = remaining
+    early = across_x(place, across_y(jnp.concatenate([before, down], axis=1)))
+    early = finish(place, jnp.concatenate([early, wide, wide_first], axis=1))
+    late_first = finish(place, across_x(place, across_y(pair)))
+    late_second = early[:, :UNIT]
+    early_second = jnp.concatenate([early[:, UNIT : 2 * UNIT], early[:, 3 * UNIT : 5 * UNIT]], 1)
+    early_first = jnp.concatenate([early[:, 2 * UNIT : 3 * UNIT], early[:, 5 * UNIT :]], 1)
     sums = []
     for for_first, for_second in ((early_first, early_second), (late_first, late_second)):
         own = jnp.where(first, for_first, for_second)

time: 814 us -> 818 us (level)
  matrix products: 141 us -> 170 us
  starting transfers between devices: 147 us -> 118 us
  waiting for transfers between devices: 292 us -> 270 us
  other arithmetic: 95.2 us -> 110 us
  local copies, waits for them, and re-layouts: 102 us -> 111 us
    ppermute x40 -> x24, waiting for transfers between devices: 103 us -> 63.1 us  [x_step(): lax.ppermute(value, 'dp', [(i, (i + 2 * step) % 8) for i in range(8)])]
    ppermute x48 -> x41, waiting for transfers between devices: 145 us -> 175 us  [z_step(): lax.ppermute(value, 'fsdp', [(i, (i + 2 * step) % 8) for i in range(8)])]
    ppermute x40 -> x24, starting transfers between devices: 54.5 us -> 34.8 us  [x_step(): lax.ppermute(value, 'dp', [(i, (i + 2 * step) % 8) for i in range(8)])]
    dot_general x24, matrix products: 41.7 us -> 59.5 us  [backward_product(): lax.dot_general(grad, weight, (((1,), (1,)), ((), ())), preferred_element...]
    unnamed x416 -> x381, local copies, waits for them, and re-layouts: 39 us -> 23.6 us
    dot_general x16, matrix products: 24.1 us -> 39.3 us  [product(): return jnp.dot(left, right, preferred_element_type=F32)]
    concatenate x8, other arithmetic: 1.39 us -> 12.9 us  [the longest x2 8.46 us: gather_wide(): return ([jnp.concatenate(blocks, axis=0) for blocks in layers], near)]
    ppermute x4 -> x2, waiting for transfers between devices: 11.3 us -> 2.94 us  [y_far(): return lax.ppermute(value, 'dp', [(i, i ^ 1) for i in range(8)])]
  transfers between devices with their start and end apart: 129 -> 99, of which waited for: 58 -> 47; matrix products, arithmetic and copies ran while one was open for 37% -> 44% of each run, Pallas kernels for 0% -> 0%
where the time goes in v3:
time: 818 us; the launch traced here: 804 us
  waiting for transfers between devices  270 us (33%)
  matrix products  170 us (21%)
  starting transfers between devices  118 us (14%)
  local copies, waits for them, and re-layouts  111 us (14%)
  other arithmetic  110 us (13%)
  between operations  25.1 us (3%)
    ppermute x41, waiting for transfers between devices, z_step(): lax.ppermute(value, 'fsdp', [(i, (i + 2 * step) % 8) for i in range(8)])  175 us
    ppermute x24, waiting for transfers between devices, x_step(): lax.ppermute(value, 'dp', [(i, (i + 2 * step) % 8) for i in range(8)])  63.1 us
    dot_general x24, matrix products, backward_product(): lax.dot_general(grad, weight, (((1,), (1,)), ((), ())), preferred_element...  59.5 us
    ppermute x41, starting transfers between devices, z_step(): lax.ppermute(value, 'fsdp', [(i, (i + 2 * step) % 8) for i in range(8)])  59 us
    dot_general x16, matrix products, product(): return jnp.dot(left, right, preferred_element_type=F32)  39.3 us
    ppermute x24, starting transfers between devices, x_step(): lax.ppermute(value, 'dp', [(i, (i + 2 * step) % 8) for i in range(8)])  34.8 us
    dot_general x26, matrix products, outer_sum(): lax.dot_general(left, right, (((0,), (0,)), ((), ())), preferred_element_...  34.3 us
    ppermute x11, waiting for transfers between devices, y_near(): return lax.ppermute(value, 'fsdp', [(i, i ^ 1) for i in range(8)])  27.5 us
  transfers between devices with their start and end apart: 99, of which 47 were waited for; matrix products, arithmetic and copies ran while one was open for 44% of the time, Pallas kernels for 0%

profile of v3, /device:TPU:0, one launch (start us, length us, event | category | flops | bytes accessed | tf_op | source)
XLA Modules:
  0.0 804.4 jit_solution(14796627764016739644)
XLA Ops:
  23.5 20.2 %collective-permute-done.10 = bf16[2,32,2560]{2,1,0:T(8,128)(2,1)S(1)} collective-permute-done((bf16[2,32,2560]{2,1,0:T(8,128)(2,1)S(1)}, bf16[2,32,2560]{2,1,0:T(8,128)(2,1)S(1)}, u32[]{:S(2)}, u32[]{:S(2)}) %collective-permute-start.10) | collective-permute-done | bytes 327712 | tf_op jit(solution)/shard_map/ppermute | solution.py:98
  51.6 9.7 %collective-permute-done.12 = bf16[2,2,32,2560]{3,2,0,1:T(8,128)(2,1)S(1)} collective-permute-done((bf16[2,2,32,2560]{3,2,0,1:T(8,128)(2,1)S(1)}, bf16[2,2,32,2560]{3,2,0,1:T(8,128)(2,1)S(1)}, u32[]{:S(2)}, u32[]{:S(2)}) %collective-permute-start.12) | collective-permute-done | bytes 655392 | tf_op jit(solution)/shard_map/ppermute | solution.py:90
  69.1 11.1 %collective-permute-done.13 = bf16[2,2,32,2560]{3,2,0,1:T(8,128)(2,1)S(1)} collective-permute-done((bf16[2,2,32,2560]{3,2,0,1:T(8,128)(2,1)S(1)}, bf16[2,2,32,2560]{3,2,0,1:T(8,128)(2,1)S(1)}, u32[]{:S(2)}, u32[]{:S(2)}) %collective-permute-start.13) | collective-permute-done | bytes 655392 | tf_op jit(solution)/shard_map/ppermute | solution.py:90
  86.7 9.5 %collective-permute-done.3 = bf16[2,256,1280]{2,1,0:T(8,128)(2,1)S(1)} collective-permute-done((bf16[2,256,1280]{2,1,0:T(8,128)(2,1)S(1)}, bf16[2,256,1280]{2,1,0:T(8,128)(2,1)S(1)}, u32[]{:S(2)}, u32[]{:S(2)}) %collective-permute-start.3) | collective-permute-done | bytes 1310752 | tf_op jit(solution)/shard_map/ppermute | solution.py:90
  98.1 7.5 collective-permute-done.4
  117.1 9.9 %collective-permute-done.16 = bf16[256,1280]{1,0:T(8,128)(2,1)S(1)} collective-permute-done((bf16[256,1280]{1,0:T(8,128)(2,1)S(1)}, bf16[256,1280]{1,0:T(8,128)(2,1)S(1)}, u32[]{:S(2)}, u32[]{:S(2)}) %collective-permute-start.16) | collective-permute-done | bytes 655392 | tf_op jit(solution)/shard_map/ppermute | solution.py:90
  133.4 18.3 %collective-permute-done.7 = bf16[2,640,512]{2,1,0:T(8,128)(2,1)S(1)} collective-permute-done((bf16[2,640,512]{2,1,0:T(8,128)(2,1)S(1)}, bf16[2,640,512]{2,1,0:T(8,128)(2,1)S(1)}, u32[]{:S(2)}, u32[]{:S(2)}) %collective-permute-start.7) | collective-permute-done | bytes 1310752 | tf_op jit(solution)/shard_map/ppermute | solution.py:90
  161.7 9.8 %collective-permute-done.36 = bf16[640,512]{1,0:T(8,128)(2,1)S(1)} collective-permute-done((bf16[640,512]{1,0:T(8,128)(2,1)S(1)}, bf16[640,512]{1,0:T(8,128)(2,1)S(1)}, u32[]{:S(2)}, u32[]{:S(2)}) %collective-permute-start.36) | collective-permute-done | bytes 655392 | tf_op jit(solution)/shard_map/ppermute | solution.py:90
  203.6 6.2 collective-permute-done.20
  247.7 5.5 multiply_convert_fusion.5
  284.5 5.8 collective-permute-done.30
  293.7 5.8 collective-permute-done.32
  349.1 5.4 fusion.3
  368.4 7.3 fusion.5
  389.7 9.3 %collective-permute-done.44 = bf16[128,2560]{1,0:T(8,128)(2,1)S(1)} collective-permute-done((bf16[128,2560]{1,0:T(8,128)(2,1)S(1)}, bf16[128,2560]{1,0:T(8,128)(2,1)S(1)}, u32[]{:S(2)}, u32[]{:S(2)}) %collective-permute-start.44) | collective-permute-done | bytes 655392 | tf_op jit(solution)/shard_map/ppermute | solution.py:94
  436.8 5.8 collective-permute-done.48
  516.3 7.3 fusion.2
  580.1 6.1 collective-permute-done.53
  614.0 14.2 %collective-permute-done.61 = bf16[256,1280]{1,0:T(8,128)(2,1)S(1)} collective-permute-done((bf16[256,1280]{1,0:T(8,128)(2,1)S(1)}, bf16[256,1280]{1,0:T(8,128)(2,1)S(1)}, u32[]{:S(2)}, u32[]{:S(2)}) %collective-permute-start.61) | collective-permute-done | bytes 655392 | tf_op jit(solution)/shard_map/ppermute | solution.py:90
  629.0 6.3 collective-permute-done.90
  636.2 12.6 %collective-permute-done.62 = bf16[256,1280]{1,0:T(8,128)(2,1)S(1)} collective-permute-done((bf16[256,1280]{1,0:T(8,128)(2,1)S(1)}, bf16[256,1280]{1,0:T(8,128)(2,1)S(1)}, u32[]{:S(2)}, u32[]{:S(2)}) %collective-permute-start.62) | collective-permute-done | bytes 655392 | tf_op jit(solution)/shard_map/ppermute | solution.py:90
  728.6 9.0 %collective-permute-done.76 = bf16[256,1280]{1,0:T(8,128)(2,1)S(1)} collective-permute-done((bf16[256,1280]{1,0:T(8,128)(2,1)S(1)}, bf16[256,1280]{1,0:T(8,128)(2,1)S(1)}, u32[]{:S(2)}, u32[]{:S(2)}) %collective-permute-start.76) | collective-permute-done | bytes 655392 | tf_op jit(solution)/shard_map/ppermute | solution.py:90
  749.1 18.9 %collective-permute-done.94 = bf16[32,8960]{1,0:T(8,128)(2,1)S(1)} collective-permute-done((bf16[32,8960]{1,0:T(8,128)(2,1)S(1)}, bf16[32,8960]{1,0:T(8,128)(2,1)S(1)}, u32[]{:S(2)}, u32[]{:S(2)}) %collective-permute-start.94) | collective-permute-done | bytes 573472 | tf_op jit(solution)/shard_map/ppermute | solution.py:94
  769.0 5.1 collective-permute-done.80
  (898 shorter events, 552.7 us)
Async XLA Ops:
  7.4 41.3 %collective-permute-start.5 = (bf16[320,512]{1,0:T(8,128)(2,1)}, bf16[320,512]{1,0:T(8,128)(2,1)}, u32[]{:S(2)}, u32[]{:S(2)}) collective-permute-start(bf16[320,512]{1,0:T(8,128)(2,1)} %select_bitcast_fusion.4), channel_id=1, source_target_pairs={{0,64},{64,0},{1,65},{65,1},{2,66},{66,2},{3,67},{67,3},{4,68},{68... | collective-permute-start | bytes 983048 | tf_op jit(solution)/shard_map/ppermute | solution.py:106
  19.8 45.2 %collective-permute-start.2 = (bf16[2,128,1280]{2,1,0:T(8,128)(2,1)S(1)}, bf16[2,128,1280]{2,1,0:T(8,128)(2,1)S(1)}, u32[]{:S(2)}, u32[]{:S(2)}) collective-permute-start(bf16[2,128,1280]{2,1,0:T(8,128)(2,1)S(1)} %get-tuple-element.157), channel_id=1, source_target_pairs={{0,8},{8,0},{16,24},{24,16},{32,40},{40,32},{48,56},{56,48},{1,9},... | collective-permute-start | bytes 1966088 | tf_op jit(solution)/shard_map/ppermute | solution.py:98
  65.3 40.3 %collective-permute-start.4 = (bf16[2,256,1280]{2,1,0:T(8,128)(2,1)S(1)}, bf16[2,256,1280]{2,1,0:T(8,128)(2,1)S(1)}, u32[]{:S(2)}, u32[]{:S(2)}) collective-permute-start(bf16[2,256,1280]{2,1,0:T(8,128)(2,1)S(1)} %bitcast.460), channel_id=1, source_target_pairs={{0,48},{8,56},{16,0},{24,8},{32,16},{40,24},{48,32},{56,40},{1,49}... | collective-permute-start | bytes 3932168 | tf_op jit(solution)/shard_map/ppermute | solution.py:90
  82.3 106.0 %collective-permute-start.15 = (bf16[2,256,2560]{2,1,0:T(8,128)(2,1)}, bf16[2,256,2560]{2,1,0:T(8,128)(2,1)}, u32[]{:S(2)}, u32[]{:S(2)}) collective-permute-start(bf16[2,256,2560]{2,1,0:T(8,128)(2,1)} %bitcast.31), channel_id=1, source_target_pairs={{0,6},{1,7},{2,0},{3,1},{4,2},{5,3},{6,4},{7,5},{8,14},{9,15},{10,... | collective-permute-start | bytes 7864328 | tf_op jit(solution)/shard_map/ppermute | solution.py:94
  85.0 87.4 %collective-permute-start.14 = (bf16[2,256,2560]{2,1,0:T(8,128)(2,1)}, bf16[2,256,2560]{2,1,0:T(8,128)(2,1)S(1)}, u32[]{:S(2)}, u32[]{:S(2)}) collective-permute-start(bf16[2,256,2560]{2,1,0:T(8,128)(2,1)} %bitcast.31), channel_id=1, source_target_pairs={{0,2},{1,3},{2,4},{3,5},{4,6},{5,7},{6,0},{7,1},{8,10},{9,11},{10,... | collective-permute-start | bytes 7864328 | tf_op jit(solution)/shard_map/ppermute | solution.py:94
  111.7 40.0 %collective-permute-start.7 = (bf16[2,640,512]{2,1,0:T(8,128)(2,1)S(1)}, bf16[2,640,512]{2,1,0:T(8,128)(2,1)S(1)}, u32[]{:S(2)}, u32[]{:S(2)}) collective-permute-start(bf16[2,640,512]{2,1,0:T(8,128)(2,1)S(1)} %bitcast.427), channel_id=1, source_target_pairs={{0,16},{8,24},{16,32},{24,40},{32,48},{40,56},{48,0},{56,8},{1,17}... | collective-permute-start | bytes 3932168 | tf_op jit(solution)/shard_map/ppermute | solution.py:90
  129.5 46.8 %collective-permute-start.17 = (bf16[1024,1280]{1,0:T(8,128)(2,1)S(1)}, bf16[1024,1280]{1,0:T(8,128)(2,1)S(1)}, u32[]{:S(2)}, u32[]{:S(2)}) collective-permute-start(bf16[1024,1280]{1,0:T(8,128)(2,1)S(1)} %pad_maximum_fusion.4), channel_id=1, source_target_pairs={{0,64},{64,0},{1,65},{65,1},{2,66},{66,2},{3,67},{67,3},{4,68},{68... | collective-permute-start | bytes 7864328 | tf_op jit(solution)/shard_map/ppermute | solution.py:106
  151.7 107.6 %collective-permute-start.28 = (bf16[1024,1280]{1,0:T(8,128)(2,1)}, bf16[1024,1280]{1,0:T(8,128)(2,1)}, u32[]{:S(2)}, u32[]{:S(2)}) collective-permute-start(bf16[1024,1280]{1,0:T(8,128)(2,1)} %pad_maximum_fusion.5), channel_id=1, source_target_pairs={{0,64},{64,0},{1,65},{65,1},{2,66},{66,2},{3,67},{67,3},{4,68},{68... | collective-permute-start | bytes 7864328 | tf_op jit(solution)/shard_map/ppermute | solution.py:106
  174.8 35.0 %collective-permute-start.22 = (bf16[256,2560]{1,0:T(8,128)(2,1)}, bf16[256,2560]{1,0:T(8,128)(2,1)}, u32[]{:S(2)}, u32[]{:S(2)}) collective-permute-start(bf16[256,2560]{1,0:T(8,128)(2,1)} %get-tuple-element.87), channel_id=1, source_target_pairs={{0,2},{1,3},{2,4},{3,5},{4,6},{5,7},{6,0},{7,1},{8,10},{9,11},{10,... | collective-permute-start | bytes 3932168 | tf_op jit(solution)/shard_map/ppermute | solution.py:94
  203.4 70.8 %collective-permute-start.37 = (bf16[2560,512]{1,0:T(8,128)(2,1)}, bf16[2560,512]{1,0:T(8,128)(2,1)}, u32[]{:S(2)}, u32[]{:S(2)}) collective-permute-start(bf16[2560,512]{1,0:T(8,128)(2,1)} %bitcast.103), channel_id=1, source_target_pairs={{0,64},{64,0},{1,65},{65,1},{2,66},{66,2},{3,67},{67,3},{4,68},{68... | collective-permute-start | bytes 7864328 | tf_op jit(solution)/shard_map/ppermute | solution.py:106
  209.7 43.4 %collective-permute-start.26 = (bf16[2560,512]{1,0:T(8,128)(2,1)}, bf16[2560,512]{1,0:T(8,128)(2,1)}, u32[]{:S(2)}, u32[]{:S(2)}) collective-permute-start(bf16[2560,512]{1,0:T(8,128)(2,1)} %bitcast.76), channel_id=1, source_target_pairs={{0,64},{64,0},{1,65},{65,1},{2,66},{66,2},{3,67},{67,3},{4,68},{68... | collective-permute-start | bytes 7864328 | tf_op jit(solution)/shard_map/ppermute | solution.py:106
  223.7 97.8 %collective-permute-start.34 = (bf16[1024,2560]{1,0:T(8,128)(2,1)}, bf16[1024,2560]{1,0:T(8,128)(2,1)}, u32[]{:S(2)}, u32[]{:S(2)}) collective-permute-start(bf16[1024,2560]{1,0:T(8,128)(2,1)} %pad_maximum_fusion.1), channel_id=1, source_target_pairs={{0,64},{64,0},{1,65},{65,1},{2,66},{66,2},{3,67},{67,3},{4,68},{68... | collective-permute-start | bytes 15728648 | tf_op jit(solution)/shard_map/ppermute | solution.py:106
  247.6 354.9 %collective-permute-start.72 = (bf16[128,2048]{1,0:T(8,128)(2,1)}, bf16[128,2048]{1,0:T(8,128)(2,1)}, u32[]{:S(2)}, u32[]{:S(2)}) collective-permute-start(bf16[128,2048]{1,0:T(8,128)(2,1)} %pad_maximum_fusion.30), channel_id=1, source_target_pairs={{0,64},{64,0},{1,65},{65,1},{2,66},{66,2},{3,67},{67,3},{4,68},{68... | collective-permute-start | bytes 1572872 | tf_op jit(solution)/shard_map/ppermute | solution.py:106
  282.1 140.6 %collective-permute-start.24 = (bf16[128,3584]{1,0:T(8,128)(2,1)}, bf16[128,3584]{1,0:T(8,128)(2,1)}, u32[]{:S(2)}, u32[]{:S(2)}) collective-permute-start(bf16[128,3584]{1,0:T(8,128)(2,1)} %pad_maximum_fusion.19), channel_id=1, source_target_pairs={{0,64},{64,0},{1,65},{65,1},{2,66},{66,2},{3,67},{67,3},{4,68},{68... | collective-permute-start | bytes 2752520 | tf_op jit(solution)/shard_map/ppermute | solution.py:106
  412.8 31.5 %collective-permute-start.39 = (bf16[640,512]{1,0:T(8,128)(2,1)S(1)}, bf16[640,512]{1,0:T(8,128)(2,1)S(1)}, u32[]{:S(2)}, u32[]{:S(2)}) collective-permute-start(bf16[640,512]{1,0:T(8,128)(2,1)S(1)} %convolution_convert_fusion.24), channel_id=1, source_target_pairs={{0,16},{8,24},{16,32},{24,40},{32,48},{40,56},{48,0},{56,8},{1,17}... | collective-permute-start | bytes 1966088 | tf_op jit(solution)/shard_map/ppermute | solution.py:90
  436.8 89.2 %collective-permute-start.58 = (bf16[128,2048]{1,0:T(8,128)(2,1)}, bf16[128,2048]{1,0:T(8,128)(2,1)}, u32[]{:S(2)}, u32[]{:S(2)}) collective-permute-start(bf16[128,2048]{1,0:T(8,128)(2,1)} %pad_maximum_fusion.29), channel_id=1, source_target_pairs={{0,64},{64,0},{1,65},{65,1},{2,66},{66,2},{3,67},{67,3},{4,68},{68... | collective-permute-start | bytes 1572872 | tf_op jit(solution)/shard_map/ppermute | solution.py:106
  442.6 37.9 %collective-permute-start.43 = (bf16[256,2560]{1,0:T(8,128)(2,1)}, bf16[256,2560]{1,0:T(8,128)(2,1)}, u32[]{:S(2)}, u32[]{:S(2)}) collective-permute-start(bf16[256,2560]{1,0:T(8,128)(2,1)} %fusion.36), channel_id=1, source_target_pairs={{0,2},{1,3},{2,4},{3,5},{4,6},{5,7},{6,0},{7,1},{8,10},{9,11},{10,... | collective-permute-start | bytes 3932168 | tf_op jit(solution)/shard_map/ppermute | solution.py:94
  444.3 36.2 %collective-permute-start.45 = (bf16[256,2560]{1,0:T(8,128)(2,1)}, bf16[256,2560]{1,0:T(8,128)(2,1)}, u32[]{:S(2)}, u32[]{:S(2)}) collective-permute-start(bf16[256,2560]{1,0:T(8,128)(2,1)} %fusion.33), channel_id=1, source_target_pairs={{0,6},{1,7},{2,0},{3,1},{4,2},{5,3},{6,4},{7,5},{8,14},{9,15},{10,... | collective-permute-start | bytes 3932168 | tf_op jit(solution)/shard_map/ppermute | solution.py:94
  468.6 69.7 %collective-permute-start.59 = (bf16[128,2560]{1,0:T(8,128)(2,1)}, bf16[128,2560]{1,0:T(8,128)(2,1)}, u32[]{:S(2)}, u32[]{:S(2)}) collective-permute-start(bf16[128,2560]{1,0:T(8,128)(2,1)} %pad_maximum_fusion.26), channel_id=1, source_target_pairs={{0,64},{64,0},{1,65},{65,1},{2,66},{66,2},{3,67},{67,3},{4,68},{68... | collective-permute-start | bytes 1966088 | tf_op jit(solution)/shard_map/ppermute | solution.py:106
  493.9 48.5 %collective-permute-start.50 = (bf16[128,3072]{1,0:T(8,128)(2,1)}, bf16[128,3072]{1,0:T(8,128)(2,1)}, u32[]{:S(2)}, u32[]{:S(2)}) collective-permute-start(bf16[128,3072]{1,0:T(8,128)(2,1)} %pad_maximum_fusion.22), channel_id=1, source_target_pairs={{0,64},{64,0},{1,65},{65,1},{2,66},{66,2},{3,67},{67,3},{4,68},{68... | collective-permute-start | bytes 2359304 | tf_op jit(solution)/shard_map/ppermute | solution.py:106
  495.3 45.5 %collective-permute-start.64 = (bf16[64,2560]{1,0:T(8,128)(2,1)}, bf16[64,2560]{1,0:T(8,128)(2,1)}, u32[]{:S(2)}, u32[]{:S(2)}) collective-permute-start(bf16[64,2560]{1,0:T(8,128)(2,1)} %get-tuple-element.108), channel_id=1, source_target_pairs={{0,16},{8,24},{16,32},{24,40},{32,48},{40,56},{48,0},{56,8},{1,17}... | collective-permute-start | bytes 983048 | tf_op jit(solution)/shard_map/ppermute | solution.py:90
  611.2 43.8 %collective-permute-start.89 = (bf16[64,2560]{1,0:T(8,128)(2,1)}, bf16[64,2560]{1,0:T(8,128)(2,1)}, u32[]{:S(2)}, u32[]{:S(2)}) collective-permute-start(bf16[64,2560]{1,0:T(8,128)(2,1)} %get-tuple-element.103), channel_id=1, source_target_pairs={{0,48},{8,56},{16,0},{24,8},{32,16},{40,24},{48,32},{56,40},{1,49}... | collective-permute-start | bytes 983048 | tf_op jit(solution)/shard_map/ppermute | solution.py:90
  741.4 35.7 %collective-permute-start.95 = (bf16[32,8960]{1,0:T(8,128)(2,1)S(1)}, bf16[32,8960]{1,0:T(8,128)(2,1)S(1)}, u32[]{:S(2)}, u32[]{:S(2)}) collective-permute-start(bf16[32,8960]{1,0:T(8,128)(2,1)S(1)} %get-tuple-element.49), channel_id=1, source_target_pairs={{0,6},{1,7},{2,0},{3,1},{4,2},{5,3},{6,4},{7,5},{8,14},{9,15},{10,... | collective-permute-start | bytes 1720328 | tf_op jit(solution)/shard_map/ppermute | solution.py:94
  743.8 36.4 %collective-permute-start.96 = (bf16[32,8960]{1,0:T(8,128)(2,1)S(1)}, bf16[32,8960]{1,0:T(8,128)(2,1)S(1)}, u32[]{:S(2)}, u32[]{:S(2)}) collective-permute-start(bf16[32,8960]{1,0:T(8,128)(2,1)S(1)} %get-tuple-element.49), channel_id=1, source_target_pairs={{0,4},{1,5},{2,6},{3,7},{4,0},{5,1},{6,2},{7,3},{8,12},{9,13},{10,... | collective-permute-start | bytes 1720328 | tf_op jit(solution)/shard_map/ppermute | solution.py:94
  (257 other events, 3089.1 us)

commit v4 on v3

--- a/solution.py
+++ b/solution.py
@@ -173,7 +173,7 @@
 def gate(value, *others):
     late = False
     for other in others:
-        corner = other[(0,) * other.ndim]
+        corner = other[(-1,) * other.ndim]
         late = late | (corner != corner)
     return jax.tree.map(lambda part: jnp.where(late, jnp.zeros_like(part), part), value)
 
@@ -186,7 +186,8 @@
     return (layers, (before, after))
 
 
-def gather_first(place, own):
+def gather_first(place, own, waits):
+    own = gate(own, *waits)
     pair = jnp.stack([own, y_near(own)], axis=1).reshape(2, 2 * PADDED, UNIT)
     layers, near = ring_gather_both(z_step, pair)
     return ([jnp.concatenate(blocks, axis=0) for blocks in layers], near)
@@ -211,18 +212,19 @@
 
 def gather_wide(place, own):
     quarter = lax.dynamic_slice_in_dim(own, place.x * ROW_QUARTER, ROW_QUARTER, 1)
-    pair = jnp.stack([quarter, y_near(quarter)], axis=1)
+    other = y_near(quarter)
+    pair = jnp.stack([quarter, other], axis=1)
     column = jnp.stack(ring_gather(z_step, -1, pair), axis=1)
     column = column.reshape(2, SPREAD // 4, 2 * UNIT)
     layers, near = ring_gather_both(x_step, column)
-    return ([jnp.concatenate(blocks, axis=0) for blocks in layers], near)
+    return ([jnp.concatenate(blocks, axis=0) for blocks in layers], near, (other,))
 
 
 def layer_weights(place, mine):
-    one, two, low = [(value, sibling(value)) for value in mine]
+    one, two = [(value, sibling(value)) for value in mine]
     gains = one[0].reshape(8, PADDED, UNIT)[:, PART : PART + 2, :PADDED]
     gains = backward_product(gains.transpose(1, 0, 2).reshape(2, SPREAD), place.by_z)
-    return (one, two, low, gains[:1], gains[1:])
+    return (one, two, gains[:1], gains[1:])
 
 
 def gather_rows(own):
@@ -237,8 +239,8 @@
     return pair[:rows] + y_near(pair[rows:].astype(BF16)).astype(F32)
 
 
-def forward_layer(place, inputs, weights, waits, cosine_table, sine_portion, allowed):
-    one, two, low, gain_one, gain_two = weights
+def forward_layer(place, inputs, weights, fetch, waits, cosine_table, sine_portion, allowed):
+    one, two, gain_one, gain_two = weights
     count_of_rows = inputs.shape[0]
     inv_one = rms_scale(inputs)
     normed_one = spread((inputs * inv_one * gain_one).astype(BF16), place.by_z)
@@ -254,7 +256,9 @@
     )
     key_portion = turned[:, QUERY_HEADS:].reshape(count_of_rows, KV_WIDTH)
     key_value = gather_rows(jnp.concatenate([key_portion, value_part], axis=1))
-    key_value = gate(key_value, *waits[0])
+    downs, near = fetch(key_value)
+    low = downs[0]
+    key_value = gate(key_value, *waits)
     key_row_block = key_value[:, :KV_WIDTH].reshape(-1, KEY_VALUE_HEADS, HEAD_SIZE)
     value_row_block = key_value[:, KV_WIDTH:].reshape(-1, KEY_VALUE_HEADS, HEAD_SIZE)
     scores = (
@@ -270,7 +274,7 @@
     mixture = jnp.einsum(
         "ghqk,kgd->qghd", attention, value_row_block, preferred_element_type=F32
     )
-    mixture = gate(mixture, *waits[1])
+    mixture = gate(mixture, *near)
     mixture = spread(
         mixture.astype(BF16).reshape(count_of_rows, QUERY_HEADS * HEAD_SIZE), place.by_z
     )
@@ -298,7 +302,7 @@
         up_pre,
         hidden,
     )
-    return (result, stored)
+    return (result, stored, downs)
 
 
 def with_sibling(own, sent):
@@ -394,9 +398,9 @@
 
 
 def backward_layer(
-    place, grad_out, weights, stored, waits, cosine_table, sine_portion, allowed
+    place, grad_out, weights, low, stored, waits, before, cosine_table, sine_portion, allowed
 ):
-    one, two, low, gain_one, gain_two = weights
+    one, two, gain_one, gain_two = weights
     (
         inputs,
         inv_one,
@@ -437,7 +441,7 @@
     grad_normed_two = unspread(spread_two, place.by_x)
     unit_two = middle * inv_two
     grad_gain_two = jnp.sum(grad_normed_two * unit_two, axis=0)
-    grad_normed_two = gate(grad_normed_two, *waits[0])
+    grad_normed_two = gate(grad_normed_two, *waits)
     grad_mid = grad_out + norm_backward(grad_normed_two, unit_two, inv_two, gain_two)
     none_narrow = jnp.zeros((count_of_rows, KV_WIDTH), BF16)
     output_side = jnp.concatenate([grad_mid.astype(BF16), none_narrow], axis=1)
@@ -462,13 +466,13 @@
         "qghd,kgd->ghqk", grad_mixture, value_row_block, preferred_element_type=F32
     )
     row_dots = jnp.sum(attention_full * grad_attention, axis=-1, keepdims=True)
+    far, column, wide = wide
+    row_dots = gate(row_dots, *far)
     grad_scores = (attention_full * (grad_attention - row_dots)).astype(BF16)
     key_gradient = (
         jnp.einsum("ghqk,qghd->kgd", grad_scores, query_rows, preferred_element_type=F32)
         * SCALE
     )
-    far, column, wide = wide
-    key_gradient = gate(key_gradient, *waits[1], *far)
     key_value = scatter_rows(
         jnp.concatenate(
             [key_gradient.reshape(-1, KV_WIDTH), value_gradient.reshape(-1, KV_WIDTH)], axis=1
@@ -478,6 +482,9 @@
         jnp.einsum("ghqk,kgd->qghd", grad_scores, key_row_block, preferred_element_type=F32)
         * SCALE
     )
+    key_value = gate(key_value, column, down)
+    before = before + [down]
+    early = across_y(jnp.concatenate(before, axis=1)) if len(before) > 1 else None
     key_gradient, value_low = (key_value[:, :KV_WIDTH], key_value[:, KV_WIDTH:].astype(BF16))
     grad_query_key = rotary_embedding_backward(
         jnp.concatenate(
@@ -512,14 +519,17 @@
         jnp.concatenate([place.role(grad_query_key, output_side), place.role(none, value_side)], 1),
         jnp.concatenate([place.role(output_side, grad_query_key), place.role(value_side, none)], 1),
     )
-    left_rows = gate(left_rows, column, down, *waits[2])
+    if len(before) > 1:
+        early = across_x(place, early)
+        left_rows = gate(left_rows, early)
     left_rows = jnp.concatenate(
         [left_rows[:, :SPREAD], left_rows[:, SPREAD:], gain_place.astype(BF16)], axis=0
     )
     right_rows = jnp.concatenate([right_rows[:, :UNIT], right_rows[:, UNIT:], gain_rows], axis=0)
     return (
-        gate(grad_in, down, column),
+        grad_in,
         (reduce_first(left_rows, right_rows), down, wide),
+        early,
     )
 
 
@@ -570,12 +580,9 @@
         layer_packs[0].append(jnp.where(first, kept, other))
         layer_packs[1].append(jnp.where(first, other, kept))
     first_pack, wide_pack, down_pack = [jnp.stack(both) for both in zip(*layer_packs)]
-    wide, near_wide = gather_wide(place, wide_pack)
-    one, near_one = gather_first(place, first_pack)
-    down, near_down = gather_down(place, down_pack, near_one)
-    weights_first, weights_second = [
-        layer_weights(place, mine) for mine in zip(one, wide, down)
-    ]
+    wide, near_wide, started = gather_wide(place, wide_pack)
+    one, unused = gather_first(place, first_pack, started)
+    weights_first, weights_second = [layer_weights(place, mine) for mine in zip(one, wide)]
 
     seq_lengths = jnp.where(first, lengths[0, 0], lengths[0, 1])
     inner = jnp.arange(rows_dev, dtype=jnp.int32)
@@ -590,20 +597,37 @@
     live_rows = (segment_mine < seq_lengths.shape[0]).astype(F32)
 
     geometry = (cosine_table, sine_portion, allowed)
-    middle, stored_first = forward_layer(
-        place, inputs, weights_first, (near_wide, near_down), *geometry
+    def fetch(key_value):
+        wholes, near = gather_down(place, down_pack, (key_value,))
+        return ([(value, sibling(value)) for value in wholes], near)
+
+    middle, stored_first, downs = forward_layer(
+        place, inputs, weights_first, fetch, near_wide, *geometry
     )
     middle = middle.astype(BF16).astype(F32)
-    result, stored_second = forward_layer(place, middle, weights_second, ((), ()), *geometry)
-    grad, pending = backward_layer(
-        place, cotangent * live_rows[:, None], weights_second, stored_second, ((), (), ()), *geometry
-    )
-    pair, down, wide = pending
-    before = jnp.concatenate([pair, down], axis=1)
-    waits = ((), (pair, wide), ())
+    result, stored_second, unused = forward_layer(
+        place, middle, weights_second, lambda key_value: (downs[1:], ()), (), *geometry
+    )
+    grad, (pair, down, wide), unused = backward_layer(
+        place,
+        cotangent * live_rows[:, None],
+        weights_second,
+        downs[1],
+        stored_second,
+        (),
+        [],
+        *geometry,
+    )
     grad = grad.astype(BF16).astype(F32)
-    grad, remaining = backward_layer(
-        place, grad, weights_first, stored_first, waits, *geometry
+    grad, (last, unused, wide_first), early = backward_layer(
+        place,
+        grad,
+        weights_first,
+        downs[0],
+        stored_first,
+        (pair, wide),
+        [pair, down],
+        *geometry,
     )
 
     ends = (grad.astype(BF16), result.astype(BF16))
@@ -612,10 +636,8 @@
         first, jnp.stack([ends[0], received]), jnp.stack([received, ends[1]])
     )[None, :, None]
 
-    pair, down, wide_first = remaining
-    early = across_x(place, across_y(jnp.concatenate([before, down], axis=1)))
     early = finish(place, jnp.concatenate([early, wide, wide_first], axis=1))
-    late_first = finish(place, across_x(place, across_y(pair)))
+    late_first = finish(place, across_x(place, across_y(last)))
     late_second = early[:, :UNIT]
     early_second = jnp.concatenate([early[:, UNIT : 2 * UNIT], early[:, 3 * UNIT : 5 * UNIT]], 1)
     early_first = jnp.concatenate([early[:, 2 * UNIT : 3 * UNIT], early[:, 5 * UNIT :]], 1)

time: 818 us -> 818 us (level)
  waiting for transfers between devices: 270 us -> 304 us
  local copies, waits for them, and re-layouts: 111 us -> 97 us
  starting transfers between devices: 118 us -> 107 us
    ppermute x24, waiting for transfers between devices: 63.1 us -> 101 us  [x_step(): lax.ppermute(value, 'dp', [(i, (i + 2 * step) % 8) for i in range(8)])]
    ppermute x41, waiting for transfers between devices: 175 us -> 151 us  [z_step(): lax.ppermute(value, 'fsdp', [(i, (i + 2 * step) % 8) for i in range(8)])]
    ppermute x11, waiting for transfers between devices: 27.5 us -> 46.6 us  [y_near(): return lax.ppermute(value, 'fsdp', [(i, i ^ 1) for i in range(8)])]
    unnamed x381 -> x391, local copies, waits for them, and re-layouts: 23.6 us -> 23.4 us
  transfers between devices with their start and end apart: 99 -> 99, of which waited for: 47 -> 44; matrix products, arithmetic and copies ran while one was open for 44% -> 38% of each run, Pallas kernels for 0% -> 0%
where the time goes in v4:
time: 818 us; the launch traced here: 805 us
  waiting for transfers between devices  304 us (37%)
  matrix products  163 us (20%)
  other arithmetic  108 us (13%)
  starting transfers between devices  107 us (13%)
  local copies, waits for them, and re-layouts  97 us (12%)
  between operations  27.3 us (3%)
    ppermute x41, waiting for transfers between devices, z_step(): lax.ppermute(value, 'fsdp', [(i, (i + 2 * step) % 8) for i in range(8)])  151 us
    ppermute x24, waiting for transfers between devices, x_step(): lax.ppermute(value, 'dp', [(i, (i + 2 * step) % 8) for i in range(8)])  101 us
    dot_general x24, matrix products, backward_product(): lax.dot_general(grad, weight, (((1,), (1,)), ((), ())), preferred_element...  53.4 us
    ppermute x41, starting transfers between devices, z_step(): lax.ppermute(value, 'fsdp', [(i, (i + 2 * step) % 8) for i in range(8)])  52.8 us
    ppermute x11, waiting for transfers between devices, y_near(): return lax.ppermute(value, 'fsdp', [(i, i ^ 1) for i in range(8)])  46.6 us
    dot_general x16, matrix products, product(): return jnp.dot(left, right, preferred_element_type=F32)  35 us
    dot_general x26, matrix products, outer_sum(): lax.dot_general(left, right, (((0,), (0,)), ((), ())), preferred_element_...  31.4 us
    ppermute x24, starting transfers between devices, x_step(): lax.ppermute(value, 'dp', [(i, (i + 2 * step) % 8) for i in range(8)])  29 us
  transfers between devices with their start and end apart: 99, of which 44 were waited for; matrix products, arithmetic and copies ran while one was open for 38% of the time, Pallas kernels for 0%

profile of v4, /device:TPU:0, one launch (start us, length us, event | category | flops | bytes accessed | tf_op | source)
XLA Modules:
  0.0 805.2 jit_solution(11447248226291847508)
XLA Ops:
  22.7 18.9 %collective-permute-done.2 = bf16[2,32,2560]{2,1,0:T(8,128)(2,1)S(1)} collective-permute-done((bf16[2,32,2560]{2,1,0:T(8,128)(2,1)S(1)}, bf16[2,32,2560]{2,1,0:T(8,128)(2,1)S(1)}, u32[]{:S(2)}, u32[]{:S(2)}) %collective-permute-start.2) | collective-permute-done | bytes 327712 | tf_op jit(solution)/shard_map/ppermute | solution.py:98
  49.6 9.9 %collective-permute-done.4 = bf16[2,128,1280]{2,1,0:T(8,128)(2,1)S(1)} collective-permute-done((bf16[2,128,1280]{2,1,0:T(8,128)(2,1)S(1)}, bf16[2,128,1280]{2,1,0:T(8,128)(2,1)S(1)}, u32[]{:S(2)}, u32[]{:S(2)}) %collective-permute-start.4) | collective-permute-done | bytes 655392 | tf_op jit(solution)/shard_map/ppermute | solution.py:98
  68.1 37.1 %collective-permute-done.16 = bf16[2,2,32,2560]{3,2,0,1:T(8,128)(2,1)S(1)} collective-permute-done((bf16[2,2,32,2560]{3,2,0,1:T(8,128)(2,1)S(1)}, bf16[2,2,32,2560]{3,2,0,1:T(8,128)(2,1)S(1)}, u32[]{:S(2)}, u32[]{:S(2)}) %collective-permute-start.16) | collective-permute-done | bytes 655392 | tf_op jit(solution)/shard_map/ppermute | solution.py:90
  113.8 10.1 %collective-permute-done.7 = bf16[256,1280]{1,0:T(8,128)(2,1)S(1)} collective-permute-done((bf16[256,1280]{1,0:T(8,128)(2,1)S(1)}, bf16[256,1280]{1,0:T(8,128)(2,1)S(1)}, u32[]{:S(2)}, u32[]{:S(2)}) %collective-permute-start.7) | collective-permute-done | bytes 655392 | tf_op jit(solution)/shard_map/ppermute | solution.py:90
  130.6 31.8 %collective-permute-done.20 = bf16[2,256,2560]{2,1,0:T(8,128)(2,1)S(1)} collective-permute-done((bf16[2,256,2560]{2,1,0:T(8,128)(2,1)S(1)}, bf16[2,256,2560]{2,1,0:T(8,128)(2,1)S(1)}, u32[]{:S(2)}, u32[]{:S(2)}) %collective-permute-start.20) | collective-permute-done | bytes 2621472 | tf_op jit(solution)/shard_map/ppermute | solution.py:94
  186.7 11.4 %collective-permute-done.22 = bf16[256,2560]{1,0:T(8,128)(2,1)} collective-permute-done((bf16[256,2560]{1,0:T(8,128)(2,1)}, bf16[256,2560]{1,0:T(8,128)(2,1)}, u32[]{:S(2)}, u32[]{:S(2)}) %collective-permute-start.22) | collective-permute-done | bytes 1310752 | tf_op jit(solution)/shard_map/ppermute | solution.py:94
  198.1 6.2 pad_maximum_fusion
  220.1 6.2 collective-permute-done.11
  236.2 6.3 fusion.394
  255.2 5.3 collective-permute-done.14
  275.2 6.1 collective-permute-done.24
  333.8 7.2 collective-permute-done.31
  412.9 9.0 %collective-permute-done.39 = bf16[128,2560]{1,0:T(8,128)(2,1)S(1)} collective-permute-done((bf16[128,2560]{1,0:T(8,128)(2,1)S(1)}, bf16[128,2560]{1,0:T(8,128)(2,1)S(1)}, u32[]{:S(2)}, u32[]{:S(2)}) %collective-permute-start.39) | collective-permute-done | bytes 655392 | tf_op jit(solution)/shard_map/ppermute | solution.py:94
  427.4 7.2 fusion.5
  459.3 6.0 collective-permute-done.47
  526.4 5.5 collective-permute-done.56
  568.1 7.6 collective-permute-done.51
  601.7 7.2 fusion.2
  648.4 9.9 %collective-permute-done.70 = bf16[128,640]{1,0:T(8,128)(2,1)S(1)} collective-permute-done((bf16[128,640]{1,0:T(8,128)(2,1)S(1)}, bf16[128,640]{1,0:T(8,128)(2,1)S(1)}, u32[]{:S(2)}, u32[]{:S(2)}) %collective-permute-start.70) | collective-permute-done | bytes 163872 | tf_op jit(solution)/shard_map/ppermute | solution.py:98
  680.5 10.2 %collective-permute-done.73 = bf16[32,3840]{1,0:T(8,128)(2,1)S(1)} collective-permute-done((bf16[32,3840]{1,0:T(8,128)(2,1)S(1)}, bf16[32,3840]{1,0:T(8,128)(2,1)S(1)}, u32[]{:S(2)}, u32[]{:S(2)}) %collective-permute-start.73) | collective-permute-done | bytes 245792 | tf_op jit(solution)/shard_map/ppermute | solution.py:94
  694.6 7.4 collective-permute-done.91
  709.3 13.5 %collective-permute-done.79 = bf16[256,1280]{1,0:T(8,128)(2,1)S(1)} collective-permute-done((bf16[256,1280]{1,0:T(8,128)(2,1)S(1)}, bf16[256,1280]{1,0:T(8,128)(2,1)S(1)}, u32[]{:S(2)}, u32[]{:S(2)}) %collective-permute-start.79) | collective-permute-done | bytes 655392 | tf_op jit(solution)/shard_map/ppermute | solution.py:90
  727.3 12.6 %collective-permute-done.80 = bf16[256,1280]{1,0:T(8,128)(2,1)S(1)} collective-permute-done((bf16[256,1280]{1,0:T(8,128)(2,1)S(1)}, bf16[256,1280]{1,0:T(8,128)(2,1)S(1)}, u32[]{:S(2)}, u32[]{:S(2)}) %collective-permute-start.80) | collective-permute-done | bytes 655392 | tf_op jit(solution)/shard_map/ppermute | solution.py:90
  750.8 17.9 %collective-permute-done.94 = bf16[32,8960]{1,0:T(8,128)(2,1)S(1)} collective-permute-done((bf16[32,8960]{1,0:T(8,128)(2,1)S(1)}, bf16[32,8960]{1,0:T(8,128)(2,1)S(1)}, u32[]{:S(2)}, u32[]{:S(2)}) %collective-permute-start.94) | collective-permute-done | bytes 573472 | tf_op jit(solution)/shard_map/ppermute | solution.py:94
  (915 shorter events, 507.6 us)
Async XLA Ops:
  17.9 48.9 %collective-permute-start.13 = (bf16[2,320,512]{2,1,0:T(8,128)(2,1)S(1)}, bf16[2,320,512]{2,1,0:T(8,128)(2,1)S(1)}, u32[]{:S(2)}, u32[]{:S(2)}) collective-permute-start(bf16[2,320,512]{2,1,0:T(8,128)(2,1)S(1)} %pad_maximum_fusion.24), channel_id=1, source_target_pairs={{0,8},{8,0},{16,24},{24,16},{32,40},{40,32},{48,56},{56,48},{1,9},... | collective-permute-start | bytes 1966088 | tf_op jit(solution)/shard_map/ppermute | solution.py:98
  59.7 48.8 %collective-permute-start.5 = (bf16[2,256,1280]{2,1,0:T(8,128)(2,1)S(1)}, bf16[2,256,1280]{2,1,0:T(8,128)(2,1)S(1)}, u32[]{:S(2)}, u32[]{:S(2)}) collective-permute-start(bf16[2,256,1280]{2,1,0:T(8,128)(2,1)S(1)} %bitcast.470), channel_id=1, source_target_pairs={{0,16},{8,24},{16,32},{24,40},{32,48},{40,56},{48,0},{56,8},{1,17}... | collective-permute-start | bytes 3932168 | tf_op jit(solution)/shard_map/ppermute | solution.py:90
  62.6 42.5 %collective-permute-start.16 = (bf16[2,2,32,2560]{3,2,0,1:T(8,128)(2,1)S(1)}, bf16[2,2,32,2560]{3,2,0,1:T(8,128)(2,1)S(1)}, u32[]{:S(2)}, u32[]{:S(2)}) collective-permute-start(bf16[2,2,32,2560]{3,2,0,1:T(8,128)(2,1)S(1)} %get-tuple-element.157), channel_id=1, source_target_pairs={{0,16},{8,24},{16,32},{24,40},{32,48},{40,56},{48,0},{56,8},{1,17}... | collective-permute-start | bytes 1966088 | tf_op jit(solution)/shard_map/ppermute | solution.py:90
  64.5 40.6 %collective-permute-start.18 = (bf16[2,2,32,2560]{3,2,0,1:T(8,128)(2,1)S(1)}, bf16[2,2,32,2560]{3,2,0,1:T(8,128)(2,1)S(1)}, u32[]{:S(2)}, u32[]{:S(2)}) collective-permute-start(bf16[2,2,32,2560]{3,2,0,1:T(8,128)(2,1)S(1)} %collective-permute-done.17), channel_id=1, source_target_pairs={{0,48},{8,56},{16,0},{24,8},{32,16},{40,24},{48,32},{56,40},{1,49}... | collective-permute-start | bytes 1966088 | tf_op jit(solution)/shard_map/ppermute | solution.py:90
  66.3 42.4 %collective-permute-start.6 = (bf16[2,256,1280]{2,1,0:T(8,128)(2,1)S(1)}, bf16[2,256,1280]{2,1,0:T(8,128)(2,1)S(1)}, u32[]{:S(2)}, u32[]{:S(2)}) collective-permute-start(bf16[2,256,1280]{2,1,0:T(8,128)(2,1)S(1)} %bitcast.471), channel_id=1, source_target_pairs={{0,48},{8,56},{16,0},{24,8},{32,16},{40,24},{48,32},{56,40},{1,49}... | collective-permute-start | bytes 3932168 | tf_op jit(solution)/shard_map/ppermute | solution.py:90
  105.7 56.7 %collective-permute-start.20 = (bf16[2,256,2560]{2,1,0:T(8,128)(2,1)S(1)}, bf16[2,256,2560]{2,1,0:T(8,128)(2,1)S(1)}, u32[]{:S(2)}, u32[]{:S(2)}) collective-permute-start(bf16[2,256,2560]{2,1,0:T(8,128)(2,1)S(1)} %bitcast.454), channel_id=1, source_target_pairs={{0,6},{1,7},{2,0},{3,1},{4,2},{5,3},{6,4},{7,5},{8,14},{9,15},{10,... | collective-permute-start | bytes 7864328 | tf_op jit(solution)/shard_map/ppermute | solution.py:94
  108.5 59.3 %collective-permute-start.19 = (bf16[2,256,2560]{2,1,0:T(8,128)(2,1)S(1)}, bf16[2,256,2560]{2,1,0:T(8,128)(2,1)S(1)}, u32[]{:S(2)}, u32[]{:S(2)}) collective-permute-start(bf16[2,256,2560]{2,1,0:T(8,128)(2,1)S(1)} %bitcast.455), channel_id=1, source_target_pairs={{0,2},{1,3},{2,4},{3,5},{4,6},{5,7},{6,0},{7,1},{8,10},{9,11},{10,... | collective-permute-start | bytes 7864328 | tf_op jit(solution)/shard_map/ppermute | solution.py:94
  124.2 49.1 %collective-permute-start.8 = (bf16[1024,1280]{1,0:T(8,128)(2,1)S(1)}, bf16[1024,1280]{1,0:T(8,128)(2,1)S(1)}, u32[]{:S(2)}, u32[]{:S(2)}) collective-permute-start(bf16[1024,1280]{1,0:T(8,128)(2,1)S(1)} %pad_maximum_fusion.3), channel_id=1, source_target_pairs={{0,64},{64,0},{1,65},{65,1},{2,66},{66,2},{3,67},{67,3},{4,68},{68... | collective-permute-start | bytes 7864328 | tf_op jit(solution)/shard_map/ppermute | solution.py:106
  126.0 173.5 %collective-permute-start.27 = (bf16[1024,1280]{1,0:T(8,128)(2,1)}, bf16[1024,1280]{1,0:T(8,128)(2,1)}, u32[]{:S(2)}, u32[]{:S(2)}) collective-permute-start(bf16[1024,1280]{1,0:T(8,128)(2,1)} %pad_maximum_fusion.5), channel_id=1, source_target_pairs={{0,64},{64,0},{1,65},{65,1},{2,66},{66,2},{3,67},{67,3},{4,68},{68... | collective-permute-start | bytes 7864328 | tf_op jit(solution)/shard_map/ppermute | solution.py:106
  164.2 40.3 %collective-permute-start.34 = (bf16[256,2560]{1,0:T(8,128)(2,1)}, bf16[256,2560]{1,0:T(8,128)(2,1)}, u32[]{:S(2)}, u32[]{:S(2)}) collective-permute-start(bf16[256,2560]{1,0:T(8,128)(2,1)} %get-tuple-element.90), channel_id=1, source_target_pairs={{0,6},{1,7},{2,0},{3,1},{4,2},{5,3},{6,4},{7,5},{8,14},{9,15},{10,... | collective-permute-start | bytes 3932168 | tf_op jit(solution)/shard_map/ppermute | solution.py:94
  204.3 87.2 %collective-permute-start.23 = (bf16[1024,2560]{1,0:T(8,128)(2,1)}, bf16[1024,2560]{1,0:T(8,128)(2,1)}, u32[]{:S(2)}, u32[]{:S(2)}) collective-permute-start(bf16[1024,2560]{1,0:T(8,128)(2,1)} %pad_maximum_fusion), channel_id=1, source_target_pairs={{0,64},{64,0},{1,65},{65,1},{2,66},{66,2},{3,67},{67,3},{4,68},{68... | collective-permute-start | bytes 15728648 | tf_op jit(solution)/shard_map/ppermute | solution.py:106
  209.2 148.3 %collective-permute-start.35 = (bf16[1024,2560]{1,0:T(8,128)(2,1)}, bf16[1024,2560]{1,0:T(8,128)(2,1)}, u32[]{:S(2)}, u32[]{:S(2)}) collective-permute-start(bf16[1024,2560]{1,0:T(8,128)(2,1)} %pad_maximum_fusion.1), channel_id=1, source_target_pairs={{0,64},{64,0},{1,65},{65,1},{2,66},{66,2},{3,67},{67,3},{4,68},{68... | collective-permute-start | bytes 15728648 | tf_op jit(solution)/shard_map/ppermute | solution.py:106
  410.9 55.4 %collective-permute-start.42 = (bf16[640,512]{1,0:T(8,128)(2,1)}, bf16[640,512]{1,0:T(8,128)(2,1)}, u32[]{:S(2)}, u32[]{:S(2)}) collective-permute-start(bf16[640,512]{1,0:T(8,128)(2,1)} %convolution_convert_fusion.24), channel_id=1, source_target_pairs={{0,16},{8,24},{16,32},{24,40},{32,48},{40,56},{48,0},{56,8},{1,17}... | collective-permute-start | bytes 1966088 | tf_op jit(solution)/shard_map/ppermute | solution.py:90
  427.2 41.1 %collective-permute-start.44 = (bf16[640,512]{1,0:T(8,128)(2,1)}, bf16[640,512]{1,0:T(8,128)(2,1)}, u32[]{:S(2)}, u32[]{:S(2)}) collective-permute-start(bf16[640,512]{1,0:T(8,128)(2,1)} %fusion.72), channel_id=1, source_target_pairs={{0,48},{8,56},{16,0},{24,8},{32,16},{40,24},{48,32},{56,40},{1,49}... | collective-permute-start | bytes 1966088 | tf_op jit(solution)/shard_map/ppermute | solution.py:90
  465.3 227.8 %collective-permute-start.76 = (bf16[128,2048]{1,0:T(8,128)(2,1)}, bf16[128,2048]{1,0:T(8,128)(2,1)}, u32[]{:S(2)}, u32[]{:S(2)}) collective-permute-start(bf16[128,2048]{1,0:T(8,128)(2,1)} %pad_maximum_fusion.30), channel_id=1, source_target_pairs={{0,64},{64,0},{1,65},{65,1},{2,66},{66,2},{3,67},{67,3},{4,68},{68... | collective-permute-start | bytes 1572872 | tf_op jit(solution)/shard_map/ppermute | solution.py:106
  558.2 62.5 %collective-permute-start.64 = (bf16[640,512]{1,0:T(8,128)(2,1)}, bf16[640,512]{1,0:T(8,128)(2,1)}, u32[]{:S(2)}, u32[]{:S(2)}) collective-permute-start(bf16[640,512]{1,0:T(8,128)(2,1)} %convolution_convert_fusion.20), channel_id=1, source_target_pairs={{0,16},{8,24},{16,32},{24,40},{32,48},{40,56},{48,0},{56,8},{1,17}... | collective-permute-start | bytes 1966088 | tf_op jit(solution)/shard_map/ppermute | solution.py:90
  565.2 74.7 %collective-permute-start.62 = (bf16[256,2560]{1,0:T(8,128)(2,1)}, bf16[256,2560]{1,0:T(8,128)(2,1)}, u32[]{:S(2)}, u32[]{:S(2)}) collective-permute-start(bf16[256,2560]{1,0:T(8,128)(2,1)} %fusion.27), channel_id=1, source_target_pairs={{0,2},{1,3},{2,4},{3,5},{4,6},{5,7},{6,0},{7,1},{8,10},{9,11},{10,... | collective-permute-start | bytes 3932168 | tf_op jit(solution)/shard_map/ppermute | solution.py:94
  575.6 64.3 %collective-permute-start.63 = (bf16[256,2560]{1,0:T(8,128)(2,1)}, bf16[256,2560]{1,0:T(8,128)(2,1)}, u32[]{:S(2)}, u32[]{:S(2)}) collective-permute-start(bf16[256,2560]{1,0:T(8,128)(2,1)} %fusion.24), channel_id=1, source_target_pairs={{0,6},{1,7},{2,0},{3,1},{4,2},{5,3},{6,4},{7,5},{8,14},{9,15},{10,... | collective-permute-start | bytes 3932168 | tf_op jit(solution)/shard_map/ppermute | solution.py:94
  577.4 43.3 %collective-permute-start.66 = (bf16[640,512]{1,0:T(8,128)(2,1)}, bf16[640,512]{1,0:T(8,128)(2,1)}, u32[]{:S(2)}, u32[]{:S(2)}) collective-permute-start(bf16[640,512]{1,0:T(8,128)(2,1)} %fusion.66), channel_id=1, source_target_pairs={{0,48},{8,56},{16,0},{24,8},{32,16},{40,24},{48,32},{56,40},{1,49}... | collective-permute-start | bytes 1966088 | tf_op jit(solution)/shard_map/ppermute | solution.py:90
  635.8 38.1 %collective-permute-start.72 = (bf16[128,3840]{1,0:T(8,128)(2,1)}, bf16[128,3840]{1,0:T(8,128)(2,1)}, u32[]{:S(2)}, u32[]{:S(2)}) collective-permute-start(bf16[128,3840]{1,0:T(8,128)(2,1)} %slice.1107), channel_id=1, source_target_pairs={{0,8},{8,0},{16,24},{24,16},{32,40},{40,32},{48,56},{56,48},{1,9},... | collective-permute-start | bytes 2949128 | tf_op jit(solution)/shard_map/ppermute | solution.py:98
  643.3 36.1 %collective-permute-start.90 = (bf16[64,2560]{1,0:T(8,128)(2,1)}, bf16[64,2560]{1,0:T(8,128)(2,1)}, u32[]{:S(2)}, u32[]{:S(2)}) collective-permute-start(bf16[64,2560]{1,0:T(8,128)(2,1)} %get-tuple-element.106), channel_id=1, source_target_pairs={{0,16},{8,24},{16,32},{24,40},{32,48},{40,56},{48,0},{56,8},{1,17}... | collective-permute-start | bytes 983048 | tf_op jit(solution)/shard_map/ppermute | solution.py:90
  643.3 51.3 %collective-permute-start.89 = (bf16[64,2560]{1,0:T(8,128)(2,1)}, bf16[64,2560]{1,0:T(8,128)(2,1)}, u32[]{:S(2)}, u32[]{:S(2)}) collective-permute-start(bf16[64,2560]{1,0:T(8,128)(2,1)} %get-tuple-element.105), channel_id=1, source_target_pairs={{0,48},{8,56},{16,0},{24,8},{32,16},{40,24},{48,32},{56,40},{1,49}... | collective-permute-start | bytes 983048 | tf_op jit(solution)/shard_map/ppermute | solution.py:90
  742.2 35.6 %collective-permute-start.95 = (bf16[32,8960]{1,0:T(8,128)(2,1)S(1)}, bf16[32,8960]{1,0:T(8,128)(2,1)S(1)}, u32[]{:S(2)}, u32[]{:S(2)}) collective-permute-start(bf16[32,8960]{1,0:T(8,128)(2,1)S(1)} %get-tuple-element.49), channel_id=1, source_target_pairs={{0,6},{1,7},{2,0},{3,1},{4,2},{5,3},{6,4},{7,5},{8,14},{9,15},{10,... | collective-permute-start | bytes 1720328 | tf_op jit(solution)/shard_map/ppermute | solution.py:94
  745.4 35.5 %collective-permute-start.96 = (bf16[32,8960]{1,0:T(8,128)(2,1)S(1)}, bf16[32,8960]{1,0:T(8,128)(2,1)S(1)}, u32[]{:S(2)}, u32[]{:S(2)}) collective-permute-start(bf16[32,8960]{1,0:T(8,128)(2,1)S(1)} %get-tuple-element.49), channel_id=1, source_target_pairs={{0,4},{1,5},{2,6},{3,7},{4,0},{5,1},{6,2},{7,3},{8,12},{9,13},{10,... | collective-permute-start | bytes 1720328 | tf_op jit(solution)/shard_map/ppermute | solution.py:94
  (262 other events, 2771.2 us)

commit v5 on v4

--- a/solution.py
+++ b/solution.py
@@ -113,11 +113,12 @@
     return [block, before, after, far]
 
 
-def ring_sum(step, way, chunk):
-    relayed = step(chunk(2).astype(BF16), way)
+def ring_sum(step, way, chunk, waits=((), ())):
+    relayed = gate(step(chunk(2).astype(BF16), way), *waits[0])
     other = step(chunk(-way).astype(BF16), -way)
     nearer = (chunk(way).astype(F32) + relayed.astype(F32)).astype(BF16)
-    return chunk(0).astype(F32) + other.astype(F32) + step(nearer, way).astype(F32)
+    total = chunk(0).astype(F32) + other.astype(F32) + step(nearer, way).astype(F32)
+    return gate(total, *waits[1])
 
 
 def direct_sum(step, chunk):
@@ -187,13 +188,16 @@
 
 
 def gather_first(place, own, waits):
-    own = gate(own, *waits)
-    pair = jnp.stack([own, y_near(own)], axis=1).reshape(2, 2 * PADDED, UNIT)
-    layers, near = ring_gather_both(z_step, pair)
-    return ([jnp.concatenate(blocks, axis=0) for blocks in layers], near)
-
-
-def gather_down(place, own, waits):
+    own = gate(own, waits[0])
+    other = y_near(own)
+    pair = jnp.stack([own, other], axis=1).reshape(2, 2 * PADDED, UNIT)
+    pair = gate(pair, waits[1])
+    layers, unused = ring_gather_both(z_step, pair)
+    return ([jnp.concatenate(blocks, axis=0) for blocks in layers], other)
+
+
+def gather_down(place, own, start, waits):
+    own = gate(own, start)
     other = y_near(own)
     low, high = (jnp.where(place.y == 0, own, other), jnp.where(place.y == 0, other, own))
     pair = jnp.stack([low, high], axis=1).reshape(2, 2 * FF_PART, DOWN_COLS)
@@ -214,10 +218,12 @@
     quarter = lax.dynamic_slice_in_dim(own, place.x * ROW_QUARTER, ROW_QUARTER, 1)
     other = y_near(quarter)
     pair = jnp.stack([quarter, other], axis=1)
-    column = jnp.stack(ring_gather(z_step, -1, pair), axis=1)
+    blocks = ring_gather(z_step, -1, pair)
+    column = jnp.stack(blocks, axis=1)
     column = column.reshape(2, SPREAD // 4, 2 * UNIT)
     layers, near = ring_gather_both(x_step, column)
-    return ([jnp.concatenate(blocks, axis=0) for blocks in layers], near, (other,))
+    started = (other, blocks[-1])
+    return ([jnp.concatenate(blocks, axis=0) for blocks in layers], near, started)
 
 
 def layer_weights(place, mine):
@@ -333,8 +339,8 @@
     return quarter
 
 
-def reduce_first(left, right):
-    return ring_sum(z_step, 1, partial_chunks(left, right))
+def reduce_first(left, right, waits):
+    return ring_sum(z_step, 1, partial_chunks(left, right), waits)
 
 
 def reduce_down(place, left, right):
@@ -381,9 +387,12 @@
     return direct_sum(x_step, by_quarter(place, block, ROW_QUARTER))
 
 
-def finish(place, quarter):
+def across_far(quarter):
     low = quarter.astype(BF16)
-    piece = (low.astype(F32) + y_far(low).astype(F32)).astype(BF16)
+    return (low.astype(F32) + y_far(low).astype(F32)).astype(BF16)
+
+
+def all_quarters(place, piece):
     whole = jnp.zeros((4,) + piece.shape, BF16)
     for distance in DISTANCES:
         block = step_from(piece, distance)
@@ -483,8 +492,9 @@
         * SCALE
     )
     key_value = gate(key_value, column, down)
-    before = before + [down]
-    early = across_y(jnp.concatenate(before, axis=1)) if len(before) > 1 else None
+    early = None
+    if before:
+        early = across_y(jnp.concatenate(before[:2] + [down], axis=1))
     key_gradient, value_low = (key_value[:, :KV_WIDTH], key_value[:, KV_WIDTH:].astype(BF16))
     grad_query_key = rotary_embedding_backward(
         jnp.concatenate(
@@ -519,16 +529,20 @@
         jnp.concatenate([place.role(grad_query_key, output_side), place.role(none, value_side)], 1),
         jnp.concatenate([place.role(output_side, grad_query_key), place.role(value_side, none)], 1),
     )
-    if len(before) > 1:
+    waits = ((), ())
+    if before:
+        left_rows = gate(left_rows, early)
         early = across_x(place, early)
-        left_rows = gate(left_rows, early)
+        piece = across_far(jnp.concatenate([early, before[2]], axis=1))
+        waits = ((early,), (piece,))
+        early = all_quarters(place, piece)
     left_rows = jnp.concatenate(
         [left_rows[:, :SPREAD], left_rows[:, SPREAD:], gain_place.astype(BF16)], axis=0
     )
     right_rows = jnp.concatenate([right_rows[:, :UNIT], right_rows[:, UNIT:], gain_rows], axis=0)
     return (
         grad_in,
-        (reduce_first(left_rows, right_rows), down, wide),
+        (reduce_first(left_rows, right_rows, waits), down, wide),
         early,
     )
 
@@ -581,7 +595,7 @@
         layer_packs[1].append(jnp.where(first, other, kept))
     first_pack, wide_pack, down_pack = [jnp.stack(both) for both in zip(*layer_packs)]
     wide, near_wide, started = gather_wide(place, wide_pack)
-    one, unused = gather_first(place, first_pack, started)
+    one, other = gather_first(place, first_pack, started)
     weights_first, weights_second = [layer_weights(place, mine) for mine in zip(one, wide)]
 
     seq_lengths = jnp.where(first, lengths[0, 0], lengths[0, 1])
@@ -598,7 +612,7 @@
 
     geometry = (cosine_table, sine_portion, allowed)
     def fetch(key_value):
-        wholes, near = gather_down(place, down_pack, (key_value,))
+        wholes, near = gather_down(place, down_pack, other, (key_value,))
         return ([(value, sibling(value)) for value in wholes], near)
 
     middle, stored_first, downs = forward_layer(
@@ -626,7 +640,7 @@
         downs[0],
         stored_first,
         (pair, wide),
-        [pair, down],
+        [pair, down, wide],
         *geometry,
     )
 
@@ -636,11 +650,13 @@
         first, jnp.stack([ends[0], received]), jnp.stack([received, ends[1]])
     )[None, :, None]
 
-    early = finish(place, jnp.concatenate([early, wide, wide_first], axis=1))
-    late_first = finish(place, across_x(place, across_y(last)))
+    late = across_x(place, across_y(gate(last, early)))
+    late = all_quarters(place, across_far(jnp.concatenate([late, wide_first], axis=1)))
+    late_first = late[:, :UNIT]
+    early_first = jnp.concatenate([early[:, 2 * UNIT : 3 * UNIT], late[:, UNIT:]], axis=1)
     late_second = early[:, :UNIT]
-    early_second = jnp.concatenate([early[:, UNIT : 2 * UNIT], early[:, 3 * UNIT : 5 * UNIT]], 1)
-    early_first = jnp.concatenate([early[:, 2 * UNIT : 3 * UNIT], early[:, 5 * UNIT :]], 1)
+    early_second = jnp.concatenate([early[:, UNIT : 2 * UNIT], early[:, 3 * UNIT :]], axis=1)
+
     sums = []
     for for_first, for_second in ((early_first, early_second), (late_first, late_second)):
         own = jnp.where(first, for_first, for_second)

time: 818 us -> 779 us (0.952)
  waiting for transfers between devices: 304 us -> 247 us
    ppermute x11, waiting for transfers between devices: 46.6 us -> 17 us  [y_near(): return lax.ppermute(value, 'fsdp', [(i, i ^ 1) for i in range(8)])]
    ppermute x24, waiting for transfers between devices: 101 us -> 77.3 us  [x_step(): lax.ppermute(value, 'dp', [(i, (i + 2 * step) % 8) for i in range(8)])]
    ppermute x41, waiting for transfers between devices: 151 us -> 139 us  [z_step(): lax.ppermute(value, 'fsdp', [(i, (i + 2 * step) % 8) for i in range(8)])]
    ppermute x2, waiting for transfers between devices: 2.98 us -> 14.2 us  [y_far(): return lax.ppermute(value, 'dp', [(i, i ^ 1) for i in range(8)])]
    unnamed x391 -> x399, local copies, waits for them, and re-layouts: 23.4 us -> 24.7 us
  transfers between devices with their start and end apart: 99 -> 99, of which waited for: 44 -> 41; matrix products, arithmetic and copies ran while one was open for 38% -> 41% of each run, Pallas kernels for 0% -> 0%
where the time goes in v5:
time: 779 us; the launch traced here: 766 us
  waiting for transfers between devices  247 us (32%)
  matrix products  164 us (21%)
  other arithmetic  111 us (14%)
  starting transfers between devices  108 us (14%)
  local copies, waits for them, and re-layouts  103 us (13%)
  between operations  33.3 us (4%)
    ppermute x41, waiting for transfers between devices, z_step(): lax.ppermute(value, 'fsdp', [(i, (i + 2 * step) % 8) for i in range(8)])  139 us
    ppermute x24, waiting for transfers between devices, x_step(): lax.ppermute(value, 'dp', [(i, (i + 2 * step) % 8) for i in range(8)])  77.3 us
    ppermute x41, starting transfers between devices, z_step(): lax.ppermute(value, 'fsdp', [(i, (i + 2 * step) % 8) for i in range(8)])  53.5 us
    dot_general x24, matrix products, backward_product(): lax.dot_general(grad, weight, (((1,), (1,)), ((), ())), preferred_element...  53.4 us
    dot_general x16, matrix products, product(): return jnp.dot(left, right, preferred_element_type=F32)  35 us
    ppermute x24, starting transfers between devices, x_step(): lax.ppermute(value, 'dp', [(i, (i + 2 * step) % 8) for i in range(8)])  33.4 us
    dot_general x26, matrix products, outer_sum(): lax.dot_general(left, right, (((0,), (0,)), ((), ())), preferred_element_...  31.4 us
    unnamed x399, local copies, waits for them, and re-layouts  24.7 us
  transfers between devices with their start and end apart: 99, of which 41 were waited for; matrix products, arithmetic and copies ran while one was open for 41% of the time, Pallas kernels for 0%

profile of v5, /device:TPU:0, one launch (start us, length us, event | category | flops | bytes accessed | tf_op | source)
XLA Modules:
  0.0 766.3 jit_solution(3816836459878591550)
XLA Ops:
  21.2 8.0 %collective-permute-done.2 = bf16[2,32,2560]{2,1,0:T(8,128)(2,1)S(1)} collective-permute-done((bf16[2,32,2560]{2,1,0:T(8,128)(2,1)S(1)}, bf16[2,32,2560]{2,1,0:T(8,128)(2,1)S(1)}, u32[]{:S(2)}, u32[]{:S(2)}) %collective-permute-start.2) | collective-permute-done | bytes 327712 | tf_op jit(solution)/shard_map/ppermute | solution.py:98
  38.3 8.5 %collective-permute-done.3 = bf16[2,2,32,2560]{3,2,0,1:T(8,128)(2,1)S(1)} collective-permute-done((bf16[2,2,32,2560]{3,2,0,1:T(8,128)(2,1)S(1)}, bf16[2,2,32,2560]{3,2,0,1:T(8,128)(2,1)S(1)}, u32[]{:S(2)}, u32[]{:S(2)}) %collective-permute-start.3) | collective-permute-done | bytes 655392 | tf_op jit(solution)/shard_map/ppermute | solution.py:90
  54.1 8.8 %collective-permute-done.4 = bf16[2,2,32,2560]{3,2,0,1:T(8,128)(2,1)S(1)} collective-permute-done((bf16[2,2,32,2560]{3,2,0,1:T(8,128)(2,1)S(1)}, bf16[2,2,32,2560]{3,2,0,1:T(8,128)(2,1)S(1)}, u32[]{:S(2)}, u32[]{:S(2)}) %collective-permute-start.4) | collective-permute-done | bytes 655392 | tf_op jit(solution)/shard_map/ppermute | solution.py:90
  75.6 20.0 %collective-permute-done.7 = bf16[2,256,1280]{2,1,0:T(8,128)(2,1)S(1)} collective-permute-done((bf16[2,256,1280]{2,1,0:T(8,128)(2,1)S(1)}, bf16[2,256,1280]{2,1,0:T(8,128)(2,1)S(1)}, u32[]{:S(2)}, u32[]{:S(2)}) %collective-permute-start.7) | collective-permute-done | bytes 1310752 | tf_op jit(solution)/shard_map/ppermute | solution.py:90
  100.9 9.9 %collective-permute-done.9 = bf16[256,1280]{1,0:T(8,128)(2,1)S(1)} collective-permute-done((bf16[256,1280]{1,0:T(8,128)(2,1)S(1)}, bf16[256,1280]{1,0:T(8,128)(2,1)S(1)}, u32[]{:S(2)}, u32[]{:S(2)}) %collective-permute-start.9) | collective-permute-done | bytes 655392 | tf_op jit(solution)/shard_map/ppermute | solution.py:90
  117.8 9.2 %collective-permute-done.20 = bf16[2,256,2560]{2,1,0:T(8,128)(2,1)S(1)} collective-permute-done((bf16[2,256,2560]{2,1,0:T(8,128)(2,1)S(1)}, bf16[2,256,2560]{2,1,0:T(8,128)(2,1)S(1)}, u32[]{:S(2)}, u32[]{:S(2)}) %collective-permute-start.20) | collective-permute-done | bytes 2621472 | tf_op jit(solution)/shard_map/ppermute | solution.py:94
  148.6 13.2 %collective-permute-done.22 = bf16[256,2560]{1,0:T(8,128)(2,1)} collective-permute-done((bf16[256,2560]{1,0:T(8,128)(2,1)}, bf16[256,2560]{1,0:T(8,128)(2,1)}, u32[]{:S(2)}, u32[]{:S(2)}) %collective-permute-start.22) | collective-permute-done | bytes 1310752 | tf_op jit(solution)/shard_map/ppermute | solution.py:94
  161.8 6.1 pad_maximum_fusion
  183.8 6.2 collective-permute-done.13
  199.6 6.3 fusion.392
  287.3 8.9 %collective-permute-done.31 = bf16[256,640]{1,0:T(8,128)(2,1)S(1)} collective-permute-done((bf16[256,640]{1,0:T(8,128)(2,1)S(1)}, bf16[256,640]{1,0:T(8,128)(2,1)S(1)}, u32[]{:S(2)}, u32[]{:S(2)}) %collective-permute-start.31) | collective-permute-done | bytes 327712 | tf_op jit(solution)/shard_map/ppermute | solution.py:90
  370.9 9.0 %collective-permute-done.39 = bf16[128,2560]{1,0:T(8,128)(2,1)S(1)} collective-permute-done((bf16[128,2560]{1,0:T(8,128)(2,1)S(1)}, bf16[128,2560]{1,0:T(8,128)(2,1)S(1)}, u32[]{:S(2)}, u32[]{:S(2)}) %collective-permute-start.39) | collective-permute-done | bytes 655392 | tf_op jit(solution)/shard_map/ppermute | solution.py:94
  385.4 7.1 fusion.5
  417.3 6.0 collective-permute-done.47
  481.8 5.9 collective-permute-done.56
  510.8 11.1 %collective-permute-done.65 = bf16[640,512]{1,0:T(8,128)(2,1)S(1)} collective-permute-done((bf16[640,512]{1,0:T(8,128)(2,1)S(1)}, bf16[640,512]{1,0:T(8,128)(2,1)S(1)}, u32[]{:S(2)}, u32[]{:S(2)}) %collective-permute-start.65) | collective-permute-done | bytes 655392 | tf_op jit(solution)/shard_map/ppermute | solution.py:90
  564.4 7.2 fusion.2
  640.1 9.0 %collective-permute-done.73 = bf16[32,3840]{1,0:T(8,128)(2,1)S(1)} collective-permute-done((bf16[32,3840]{1,0:T(8,128)(2,1)S(1)}, bf16[32,3840]{1,0:T(8,128)(2,1)S(1)}, u32[]{:S(2)}, u32[]{:S(2)}) %collective-permute-start.73) | collective-permute-done | bytes 245792 | tf_op jit(solution)/shard_map/ppermute | solution.py:94
  656.8 6.7 collective-permute-done.76
  667.5 5.6 collective-permute-done.83
  676.9 15.1 %collective-permute-done.78 = bf16[32,6400]{1,0:T(8,128)(2,1)S(1)} collective-permute-done((bf16[32,6400]{1,0:T(8,128)(2,1)S(1)}, bf16[32,6400]{1,0:T(8,128)(2,1)S(1)}, u32[]{:S(2)}, u32[]{:S(2)}) %collective-permute-start.78) | collective-permute-done | bytes 409632 | tf_op jit(solution)/shard_map/ppermute | solution.py:94
  694.0 9.8 %collective-permute-done.84 = bf16[256,1280]{1,0:T(8,128)(2,1)S(1)} collective-permute-done((bf16[256,1280]{1,0:T(8,128)(2,1)S(1)}, bf16[256,1280]{1,0:T(8,128)(2,1)S(1)}, u32[]{:S(2)}, u32[]{:S(2)}) %collective-permute-start.84) | collective-permute-done | bytes 655392 | tf_op jit(solution)/shard_map/ppermute | solution.py:90
  725.0 7.4 collective-permute-done.93
  740.0 7.5 collective-permute-done.95
  (930 shorter events, 520.4 us)
Async XLA Ops:
  7.0 43.4 %collective-permute-start.14 = (bf16[320,512]{1,0:T(8,128)(2,1)}, bf16[320,512]{1,0:T(8,128)(2,1)}, u32[]{:S(2)}, u32[]{:S(2)}) collective-permute-start(bf16[320,512]{1,0:T(8,128)(2,1)} %select_bitcast_fusion.4), channel_id=1, source_target_pairs={{0,64},{64,0},{1,65},{65,1},{2,66},{66,2},{3,67},{67,3},{4,68},{68... | collective-permute-start | bytes 983048 | tf_op jit(solution)/shard_map/ppermute | solution.py:106
  65.0 30.6 %collective-permute-start.7 = (bf16[2,256,1280]{2,1,0:T(8,128)(2,1)S(1)}, bf16[2,256,1280]{2,1,0:T(8,128)(2,1)S(1)}, u32[]{:S(2)}, u32[]{:S(2)}) collective-permute-start(bf16[2,256,1280]{2,1,0:T(8,128)(2,1)S(1)} %bitcast.471), channel_id=1, source_target_pairs={{0,16},{8,24},{16,32},{24,40},{32,48},{40,56},{48,0},{56,8},{1,17}... | collective-permute-start | bytes 3932168 | tf_op jit(solution)/shard_map/ppermute | solution.py:90
  65.2 34.5 %collective-permute-start.15 = (bf16[2,320,512]{2,1,0:T(8,128)(2,1)S(1)}, bf16[2,320,512]{2,1,0:T(8,128)(2,1)S(1)}, u32[]{:S(2)}, u32[]{:S(2)}) collective-permute-start(bf16[2,320,512]{2,1,0:T(8,128)(2,1)S(1)} %maximum_select_fusion.5), channel_id=1, source_target_pairs={{0,8},{8,0},{16,24},{24,16},{32,40},{40,32},{48,56},{56,48},{1,9},... | collective-permute-start | bytes 1966088 | tf_op jit(solution)/shard_map/ppermute | solution.py:98
  66.8 28.9 %collective-permute-start.8 = (bf16[2,256,1280]{2,1,0:T(8,128)(2,1)S(1)}, bf16[2,256,1280]{2,1,0:T(8,128)(2,1)S(1)}, u32[]{:S(2)}, u32[]{:S(2)}) collective-permute-start(bf16[2,256,1280]{2,1,0:T(8,128)(2,1)S(1)} %bitcast.472), channel_id=1, source_target_pairs={{0,48},{8,56},{16,0},{24,8},{32,16},{40,24},{48,32},{56,40},{1,49}... | collective-permute-start | bytes 3932168 | tf_op jit(solution)/shard_map/ppermute | solution.py:90
  71.1 55.9 %collective-permute-start.20 = (bf16[2,256,2560]{2,1,0:T(8,128)(2,1)S(1)}, bf16[2,256,2560]{2,1,0:T(8,128)(2,1)S(1)}, u32[]{:S(2)}, u32[]{:S(2)}) collective-permute-start(bf16[2,256,2560]{2,1,0:T(8,128)(2,1)S(1)} %bitcast.455), channel_id=1, source_target_pairs={{0,6},{1,7},{2,0},{3,1},{4,2},{5,3},{6,4},{7,5},{8,14},{9,15},{10,... | collective-permute-start | bytes 7864328 | tf_op jit(solution)/shard_map/ppermute | solution.py:94
  73.9 58.4 %collective-permute-start.19 = (bf16[2,256,2560]{2,1,0:T(8,128)(2,1)S(1)}, bf16[2,256,2560]{2,1,0:T(8,128)(2,1)S(1)}, u32[]{:S(2)}, u32[]{:S(2)}) collective-permute-start(bf16[2,256,2560]{2,1,0:T(8,128)(2,1)S(1)} %bitcast.456), channel_id=1, source_target_pairs={{0,2},{1,3},{2,4},{3,5},{4,6},{5,7},{6,0},{7,1},{8,10},{9,11},{10,... | collective-permute-start | bytes 7864328 | tf_op jit(solution)/shard_map/ppermute | solution.py:94
  112.9 148.1 %collective-permute-start.27 = (bf16[1024,1280]{1,0:T(8,128)(2,1)}, bf16[1024,1280]{1,0:T(8,128)(2,1)}, u32[]{:S(2)}, u32[]{:S(2)}) collective-permute-start(bf16[1024,1280]{1,0:T(8,128)(2,1)} %pad_maximum_fusion.5), channel_id=1, source_target_pairs={{0,64},{64,0},{1,65},{65,1},{2,66},{66,2},{3,67},{67,3},{4,68},{68... | collective-permute-start | bytes 7864328 | tf_op jit(solution)/shard_map/ppermute | solution.py:106
  128.6 39.5 %collective-permute-start.34 = (bf16[256,2560]{1,0:T(8,128)(2,1)}, bf16[256,2560]{1,0:T(8,128)(2,1)}, u32[]{:S(2)}, u32[]{:S(2)}) collective-permute-start(bf16[256,2560]{1,0:T(8,128)(2,1)} %get-tuple-element.90), channel_id=1, source_target_pairs={{0,6},{1,7},{2,0},{3,1},{4,2},{5,3},{6,4},{7,5},{8,14},{9,15},{10,... | collective-permute-start | bytes 3932168 | tf_op jit(solution)/shard_map/ppermute | solution.py:94
  167.9 83.6 %collective-permute-start.23 = (bf16[1024,2560]{1,0:T(8,128)(2,1)}, bf16[1024,2560]{1,0:T(8,128)(2,1)}, u32[]{:S(2)}, u32[]{:S(2)}) collective-permute-start(bf16[1024,2560]{1,0:T(8,128)(2,1)} %pad_maximum_fusion), channel_id=1, source_target_pairs={{0,64},{64,0},{1,65},{65,1},{2,66},{66,2},{3,67},{67,3},{4,68},{68... | collective-permute-start | bytes 15728648 | tf_op jit(solution)/shard_map/ppermute | solution.py:106
  172.9 143.6 %collective-permute-start.35 = (bf16[1024,2560]{1,0:T(8,128)(2,1)}, bf16[1024,2560]{1,0:T(8,128)(2,1)}, u32[]{:S(2)}, u32[]{:S(2)}) collective-permute-start(bf16[1024,2560]{1,0:T(8,128)(2,1)} %pad_maximum_fusion.1), channel_id=1, source_target_pairs={{0,64},{64,0},{1,65},{65,1},{2,66},{66,2},{3,67},{67,3},{4,68},{68... | collective-permute-start | bytes 15728648 | tf_op jit(solution)/shard_map/ppermute | solution.py:106
  193.1 31.0 %collective-permute-start.16 = (bf16[2,640,512]{2,1,0:T(8,128)(2,1)}, bf16[2,640,512]{2,1,0:T(8,128)(2,1)}, u32[]{:S(2)}, u32[]{:S(2)}) collective-permute-start(bf16[2,640,512]{2,1,0:T(8,128)(2,1)} %bitcast.50), channel_id=1, source_target_pairs={{0,16},{8,24},{16,32},{24,40},{32,48},{40,56},{48,0},{56,8},{1,17}... | collective-permute-start | bytes 3932168 | tf_op jit(solution)/shard_map/ppermute | solution.py:90
  193.1 33.3 %collective-permute-start.17 = (bf16[2,640,512]{2,1,0:T(8,128)(2,1)}, bf16[2,640,512]{2,1,0:T(8,128)(2,1)}, u32[]{:S(2)}, u32[]{:S(2)}) collective-permute-start(bf16[2,640,512]{2,1,0:T(8,128)(2,1)} %bitcast.50), channel_id=1, source_target_pairs={{0,48},{8,56},{16,0},{24,8},{32,16},{40,24},{48,32},{56,40},{1,49}... | collective-permute-start | bytes 3932168 | tf_op jit(solution)/shard_map/ppermute | solution.py:90
  368.8 55.5 %collective-permute-start.42 = (bf16[640,512]{1,0:T(8,128)(2,1)}, bf16[640,512]{1,0:T(8,128)(2,1)}, u32[]{:S(2)}, u32[]{:S(2)}) collective-permute-start(bf16[640,512]{1,0:T(8,128)(2,1)} %convolution_convert_fusion.24), channel_id=1, source_target_pairs={{0,16},{8,24},{16,32},{24,40},{32,48},{40,56},{48,0},{56,8},{1,17}... | collective-permute-start | bytes 1966088 | tf_op jit(solution)/shard_map/ppermute | solution.py:90
  385.2 41.5 %collective-permute-start.44 = (bf16[640,512]{1,0:T(8,128)(2,1)}, bf16[640,512]{1,0:T(8,128)(2,1)}, u32[]{:S(2)}, u32[]{:S(2)}) collective-permute-start(bf16[640,512]{1,0:T(8,128)(2,1)} %fusion.72), channel_id=1, source_target_pairs={{0,48},{8,56},{16,0},{24,8},{32,16},{40,24},{48,32},{56,40},{1,49}... | collective-permute-start | bytes 1966088 | tf_op jit(solution)/shard_map/ppermute | solution.py:90
  404.1 32.0 %collective-permute-start.40 = (bf16[256,2560]{1,0:T(8,128)(2,1)}, bf16[256,2560]{1,0:T(8,128)(2,1)}, u32[]{:S(2)}, u32[]{:S(2)}) collective-permute-start(bf16[256,2560]{1,0:T(8,128)(2,1)} %fusion.36), channel_id=1, source_target_pairs={{0,2},{1,3},{2,4},{3,5},{4,6},{5,7},{6,0},{7,1},{8,10},{9,11},{10,... | collective-permute-start | bytes 3932168 | tf_op jit(solution)/shard_map/ppermute | solution.py:94
  410.3 30.0 %collective-permute-start.41 = (bf16[256,2560]{1,0:T(8,128)(2,1)}, bf16[256,2560]{1,0:T(8,128)(2,1)}, u32[]{:S(2)}, u32[]{:S(2)}) collective-permute-start(bf16[256,2560]{1,0:T(8,128)(2,1)} %fusion.33), channel_id=1, source_target_pairs={{0,6},{1,7},{2,0},{3,1},{4,2},{5,3},{6,4},{7,5},{8,14},{9,15},{10,... | collective-permute-start | bytes 3932168 | tf_op jit(solution)/shard_map/ppermute | solution.py:94
  423.3 215.2 %collective-permute-start.80 = (bf16[128,2048]{1,0:T(8,128)(2,1)}, bf16[128,2048]{1,0:T(8,128)(2,1)}, u32[]{:S(2)}, u32[]{:S(2)}) collective-permute-start(bf16[128,2048]{1,0:T(8,128)(2,1)} %pad_maximum_fusion.27), channel_id=1, source_target_pairs={{0,64},{64,0},{1,65},{65,1},{2,66},{66,2},{3,67},{67,3},{4,68},{68... | collective-permute-start | bytes 1572872 | tf_op jit(solution)/shard_map/ppermute | solution.py:106
  464.9 30.4 %collective-permute-start.59 = (bf16[128,3072]{1,0:T(8,128)(2,1)}, bf16[128,3072]{1,0:T(8,128)(2,1)}, u32[]{:S(2)}, u32[]{:S(2)}) collective-permute-start(bf16[128,3072]{1,0:T(8,128)(2,1)} %pad_maximum_fusion.22), channel_id=1, source_target_pairs={{0,64},{64,0},{1,65},{65,1},{2,66},{66,2},{3,67},{67,3},{4,68},{68... | collective-permute-start | bytes 2359304 | tf_op jit(solution)/shard_map/ppermute | solution.py:106
  523.2 62.2 %collective-permute-start.64 = (bf16[640,512]{1,0:T(8,128)(2,1)}, bf16[640,512]{1,0:T(8,128)(2,1)}, u32[]{:S(2)}, u32[]{:S(2)}) collective-permute-start(bf16[640,512]{1,0:T(8,128)(2,1)} %convolution_convert_fusion.20), channel_id=1, source_target_pairs={{0,16},{8,24},{16,32},{24,40},{32,48},{40,56},{48,0},{56,8},{1,17}... | collective-permute-start | bytes 1966088 | tf_op jit(solution)/shard_map/ppermute | solution.py:90
  528.8 58.4 %collective-permute-start.66 = (bf16[640,512]{1,0:T(8,128)(2,1)}, bf16[640,512]{1,0:T(8,128)(2,1)}, u32[]{:S(2)}, u32[]{:S(2)}) collective-permute-start(bf16[640,512]{1,0:T(8,128)(2,1)} %fusion.66), channel_id=1, source_target_pairs={{0,48},{8,56},{16,0},{24,8},{32,16},{40,24},{48,32},{56,40},{1,49}... | collective-permute-start | bytes 1966088 | tf_op jit(solution)/shard_map/ppermute | solution.py:90
  536.0 70.6 %collective-permute-start.62 = (bf16[256,2560]{1,0:T(8,128)(2,1)}, bf16[256,2560]{1,0:T(8,128)(2,1)}, u32[]{:S(2)}, u32[]{:S(2)}) collective-permute-start(bf16[256,2560]{1,0:T(8,128)(2,1)} %fusion.27), channel_id=1, source_target_pairs={{0,2},{1,3},{2,4},{3,5},{4,6},{5,7},{6,0},{7,1},{8,10},{9,11},{10,... | collective-permute-start | bytes 3932168 | tf_op jit(solution)/shard_map/ppermute | solution.py:94
  540.9 65.6 %collective-permute-start.63 = (bf16[256,2560]{1,0:T(8,128)(2,1)}, bf16[256,2560]{1,0:T(8,128)(2,1)}, u32[]{:S(2)}, u32[]{:S(2)}) collective-permute-start(bf16[256,2560]{1,0:T(8,128)(2,1)} %fusion.24), channel_id=1, source_target_pairs={{0,6},{1,7},{2,0},{3,1},{4,2},{5,3},{6,4},{7,5},{8,14},{9,15},{10,... | collective-permute-start | bytes 3932168 | tf_op jit(solution)/shard_map/ppermute | solution.py:94
  612.8 91.5 %collective-permute-start.89 = (bf16[64,2560]{1,0:T(8,128)(2,1)}, bf16[64,2560]{1,0:T(8,128)(2,1)}, u32[]{:S(2)}, u32[]{:S(2)}) collective-permute-start(bf16[64,2560]{1,0:T(8,128)(2,1)} %get-tuple-element.105), channel_id=1, source_target_pairs={{0,48},{8,56},{16,0},{24,8},{32,16},{40,24},{48,32},{56,40},{1,49}... | collective-permute-start | bytes 983048 | tf_op jit(solution)/shard_map/ppermute | solution.py:90
  649.1 55.2 %collective-permute-start.91 = (bf16[64,2560]{1,0:T(8,128)(2,1)S(1)}, bf16[64,2560]{1,0:T(8,128)(2,1)S(1)}, u32[]{:S(2)}, u32[]{:S(2)}) collective-permute-start(bf16[64,2560]{1,0:T(8,128)(2,1)S(1)} %fusion.97), channel_id=1, source_target_pairs={{0,16},{8,24},{16,32},{24,40},{32,48},{40,56},{48,0},{56,8},{1,17}... | collective-permute-start | bytes 983048 | tf_op jit(solution)/shard_map/ppermute | solution.py:90
  (266 other events, 2734.6 us)

commit v6 on v5

--- a/solution.py
+++ b/solution.py
@@ -179,10 +179,9 @@
     return jax.tree.map(lambda part: jnp.where(late, jnp.zeros_like(part), part), value)
 
 
-def ring_gather_both(step, block):
-    before = step(block, 1)
-    after = step(block, -1)
-    far = (step(before[0], 1), step(after[1], -1))
+def ring_gather_both(step, block, near=None, waits=()):
+    before, after = (step(block, 1), step(block, -1)) if near is None else near
+    far = (step(gate(before[0], *waits), 1), step(gate(after[1], *waits), -1))
     layers = [[block[n], before[n], after[n], far[n]] for n in range(2)]
     return (layers, (before, after))
 
@@ -221,16 +220,15 @@
     blocks = ring_gather(z_step, -1, pair)
     column = jnp.stack(blocks, axis=1)
     column = column.reshape(2, SPREAD // 4, 2 * UNIT)
-    layers, near = ring_gather_both(x_step, column)
-    started = (other, blocks[-1])
-    return ([jnp.concatenate(blocks, axis=0) for blocks in layers], near, started)
+    near = (x_step(column, 1), x_step(column, -1))
+    return (column, near, (other, blocks[-1]))
 
 
 def layer_weights(place, mine):
-    one, two = [(value, sibling(value)) for value in mine]
+    one = (mine, sibling(mine))
     gains = one[0].reshape(8, PADDED, UNIT)[:, PART : PART + 2, :PADDED]
     gains = backward_product(gains.transpose(1, 0, 2).reshape(2, SPREAD), place.by_z)
-    return (one, two, gains[:1], gains[1:])
+    return (one, gains[:1], gains[1:])
 
 
 def gather_rows(own):
@@ -246,7 +244,7 @@
 
 
 def forward_layer(place, inputs, weights, fetch, waits, cosine_table, sine_portion, allowed):
-    one, two, gain_one, gain_two = weights
+    one, gain_one, gain_two = weights
     count_of_rows = inputs.shape[0]
     inv_one = rms_scale(inputs)
     normed_one = spread((inputs * inv_one * gain_one).astype(BF16), place.by_z)
@@ -262,8 +260,8 @@
     )
     key_portion = turned[:, QUERY_HEADS:].reshape(count_of_rows, KV_WIDTH)
     key_value = gather_rows(jnp.concatenate([key_portion, value_part], axis=1))
-    downs, near = fetch(key_value)
-    low = downs[0]
+    others, near = fetch(key_value)
+    two, low = others[0]
     key_value = gate(key_value, *waits)
     key_row_block = key_value[:, :KV_WIDTH].reshape(-1, KEY_VALUE_HEADS, HEAD_SIZE)
     value_row_block = key_value[:, KV_WIDTH:].reshape(-1, KEY_VALUE_HEADS, HEAD_SIZE)
@@ -308,7 +306,7 @@
         up_pre,
         hidden,
     )
-    return (result, stored, downs)
+    return (result, stored, others)
 
 
 def with_sibling(own, sent):
@@ -407,9 +405,10 @@
 
 
 def backward_layer(
-    place, grad_out, weights, low, stored, waits, before, cosine_table, sine_portion, allowed
+    place, grad_out, weights, others, stored, waits, before, cosine_table, sine_portion, allowed
 ):
-    one, two, gain_one, gain_two = weights
+    one, gain_one, gain_two = weights
+    two, low = others
     (
         inputs,
         inv_one,
@@ -476,6 +475,10 @@
     )
     row_dots = jnp.sum(attention_full * grad_attention, axis=-1, keepdims=True)
     far, column, wide = wide
+    early = None
+    if before:
+        early = across_y(jnp.concatenate(before[:2], axis=1))
+        far = far + (early,)
     row_dots = gate(row_dots, *far)
     grad_scores = (attention_full * (grad_attention - row_dots)).astype(BF16)
     key_gradient = (
@@ -492,9 +495,12 @@
         * SCALE
     )
     key_value = gate(key_value, column, down)
-    early = None
     if before:
-        early = across_y(jnp.concatenate(before[:2] + [down], axis=1))
+        early = across_x(place, early)
+        key_value = gate(key_value, early)
+        piece = jnp.concatenate([early, before[2]], axis=1).astype(BF16)
+        pieces = lax.all_gather(piece, "dp").astype(F32)
+        early = (pieces[0::2] + pieces[1::2]).astype(BF16).reshape(-1, piece.shape[-1])
     key_gradient, value_low = (key_value[:, :KV_WIDTH], key_value[:, KV_WIDTH:].astype(BF16))
     grad_query_key = rotary_embedding_backward(
         jnp.concatenate(
@@ -531,11 +537,8 @@
     )
     waits = ((), ())
     if before:
-        left_rows = gate(left_rows, early)
-        early = across_x(place, early)
-        piece = across_far(jnp.concatenate([early, before[2]], axis=1))
-        waits = ((early,), (piece,))
-        early = all_quarters(place, piece)
+        down = across_x(place, across_y(down))
+        waits = ((down,), ())
     left_rows = jnp.concatenate(
         [left_rows[:, :SPREAD], left_rows[:, SPREAD:], gain_place.astype(BF16)], axis=0
     )
@@ -594,9 +597,9 @@
         layer_packs[0].append(jnp.where(first, kept, other))
         layer_packs[1].append(jnp.where(first, other, kept))
     first_pack, wide_pack, down_pack = [jnp.stack(both) for both in zip(*layer_packs)]
-    wide, near_wide, started = gather_wide(place, wide_pack)
+    column, near_wide, started = gather_wide(place, wide_pack)
     one, other = gather_first(place, first_pack, started)
-    weights_first, weights_second = [layer_weights(place, mine) for mine in zip(one, wide)]
+    weights_first, weights_second = [layer_weights(place, mine) for mine in one]
 
     seq_lengths = jnp.where(first, lengths[0, 0], lengths[0, 1])
     inner = jnp.arange(rows_dev, dtype=jnp.int32)
@@ -612,32 +615,34 @@
 
     geometry = (cosine_table, sine_portion, allowed)
     def fetch(key_value):
+        layers, unused = ring_gather_both(x_step, column, near_wide, (key_value,))
+        wide = [jnp.concatenate(blocks, axis=0) for blocks in layers]
         wholes, near = gather_down(place, down_pack, other, (key_value,))
-        return ([(value, sibling(value)) for value in wholes], near)
-
-    middle, stored_first, downs = forward_layer(
+        return ([[(value, sibling(value)) for value in pair] for pair in zip(wide, wholes)], near)
+
+    middle, stored_first, others = forward_layer(
         place, inputs, weights_first, fetch, near_wide, *geometry
     )
     middle = middle.astype(BF16).astype(F32)
     result, stored_second, unused = forward_layer(
-        place, middle, weights_second, lambda key_value: (downs[1:], ()), (), *geometry
+        place, middle, weights_second, lambda key_value: (others[1:], ()), (), *geometry
     )
     grad, (pair, down, wide), unused = backward_layer(
         place,
         cotangent * live_rows[:, None],
         weights_second,
-        downs[1],
+        others[1],
         stored_second,
         (),
         [],
         *geometry,
     )
     grad = grad.astype(BF16).astype(F32)
-    grad, (last, unused, wide_first), early = backward_layer(
+    grad, (last, down_first, wide_first), early = backward_layer(
         place,
         grad,
         weights_first,
-        downs[0],
+        others[0],
         stored_first,
         (pair, wide),
         [pair, down, wide],
@@ -650,13 +655,11 @@
         first, jnp.stack([ends[0], received]), jnp.stack([received, ends[1]])
     )[None, :, None]
 
-    late = across_x(place, across_y(gate(last, early)))
-    late = all_quarters(place, across_far(jnp.concatenate([late, wide_first], axis=1)))
-    late_first = late[:, :UNIT]
-    early_first = jnp.concatenate([early[:, 2 * UNIT : 3 * UNIT], late[:, UNIT:]], axis=1)
-    late_second = early[:, :UNIT]
-    early_second = jnp.concatenate([early[:, UNIT : 2 * UNIT], early[:, 3 * UNIT :]], axis=1)
-
+    late = across_x(place, across_y(last))
+    late = jnp.concatenate([late, down_first, wide_first], axis=1)
+    late = all_quarters(place, across_far(late))
+    late_first, early_first = (late[:, :UNIT], late[:, UNIT:])
+    late_second, early_second = (early[:, :UNIT], early[:, UNIT:])
     sums = []
     for for_first, for_second in ((early_first, early_second), (late_first, late_second)):
         own = jnp.where(first, for_first, for_second)

time: 779 us -> 840 us (1.078)
  waiting for transfers between devices: 247 us -> 287 us
  between operations: 33.3 us -> 45.5 us
  other arithmetic: 111 us -> 120 us
    ppermute x41, waiting for transfers between devices: 139 us -> 200 us  [z_step(): lax.ppermute(value, 'fsdp', [(i, (i + 2 * step) % 8) for i in range(8)])]
    ppermute x24, waiting for transfers between devices: 77.3 us -> 62.3 us  [x_step(): lax.ppermute(value, 'dp', [(i, (i + 2 * step) % 8) for i in range(8)])]
    ppermute x2 -> x1, waiting for transfers between devices: 14.2 us -> 5.29 us  [y_far(): return lax.ppermute(value, 'dp', [(i, i ^ 1) for i in range(8)])]
    ppermute x11 -> x12, waiting for transfers between devices: 17 us -> 19.7 us  [y_near(): return lax.ppermute(value, 'fsdp', [(i, i ^ 1) for i in range(8)])]
    unnamed x399 -> x403, local copies, waits for them, and re-layouts: 24.7 us -> 25.5 us
  transfers between devices with their start and end apart: 99 -> 100, of which waited for: 41 -> 41; matrix products, arithmetic and copies ran while one was open for 41% -> 42% of each run, Pallas kernels for 0% -> 0%
where the time goes in v6:
time: 840 us; the launch traced here: 827 us
  waiting for transfers between devices  287 us (34%)
  matrix products  162 us (19%)
  other arithmetic  120 us (14%)
  local copies, waits for them, and re-layouts  107 us (13%)
  starting transfers between devices  106 us (13%)
  between operations  45.5 us (5%)
    ppermute x41, waiting for transfers between devices, z_step(): lax.ppermute(value, 'fsdp', [(i, (i + 2 * step) % 8) for i in range(8)])  200 us
    ppermute x24, waiting for transfers between devices, x_step(): lax.ppermute(value, 'dp', [(i, (i + 2 * step) % 8) for i in range(8)])  62.3 us
    dot_general x24, matrix products, backward_product(): lax.dot_general(grad, weight, (((1,), (1,)), ((), ())), preferred_element...  51.1 us
    ppermute x41, starting transfers between devices, z_step(): lax.ppermute(value, 'fsdp', [(i, (i + 2 * step) % 8) for i in range(8)])  51.1 us
    dot_general x26, matrix products, outer_sum(): lax.dot_general(left, right, (((0,), (0,)), ((), ())), preferred_element_...  35.3 us
    ppermute x24, starting transfers between devices, x_step(): lax.ppermute(value, 'dp', [(i, (i + 2 * step) % 8) for i in range(8)])  30.8 us
    dot_general x16, matrix products, product(): return jnp.dot(left, right, preferred_element_type=F32)  30.7 us
    unnamed x403, local copies, waits for them, and re-layouts  25.5 us
  transfers between devices with their start and end apart: 100, of which 41 were waited for; matrix products, arithmetic and copies ran while one was open for 42% of the time, Pallas kernels for 0%

profile of v6, /device:TPU:0, one launch (start us, length us, event | category | flops | bytes accessed | tf_op | source)
XLA Modules:
  0.0 826.9 jit_solution(9434640195185884375)
XLA Ops:
  23.6 7.9 collective-permute-done.2
  40.6 8.5 %collective-permute-done.3 = bf16[2,2,32,2560]{3,2,0,1:T(8,128)(2,1)S(1)} collective-permute-done((bf16[2,2,32,2560]{3,2,0,1:T(8,128)(2,1)S(1)}, bf16[2,2,32,2560]{3,2,0,1:T(8,128)(2,1)S(1)}, u32[]{:S(2)}, u32[]{:S(2)}) %collective-permute-start.3) | collective-permute-done | bytes 655392 | tf_op jit(solution)/shard_map/ppermute | solution.py:90
  54.6 10.6 %collective-permute-done.4 = bf16[2,2,32,2560]{3,2,0,1:T(8,128)(2,1)S(1)} collective-permute-done((bf16[2,2,32,2560]{3,2,0,1:T(8,128)(2,1)S(1)}, bf16[2,2,32,2560]{3,2,0,1:T(8,128)(2,1)S(1)}, u32[]{:S(2)}, u32[]{:S(2)}) %collective-permute-start.4) | collective-permute-done | bytes 655392 | tf_op jit(solution)/shard_map/ppermute | solution.py:90
  77.4 23.4 %collective-permute-done.7 = bf16[2,256,1280]{2,1,0:T(8,128)(2,1)S(1)} collective-permute-done((bf16[2,256,1280]{2,1,0:T(8,128)(2,1)S(1)}, bf16[2,256,1280]{2,1,0:T(8,128)(2,1)S(1)}, u32[]{:S(2)}, u32[]{:S(2)}) %collective-permute-start.7) | collective-permute-done | bytes 1310752 | tf_op jit(solution)/shard_map/ppermute | solution.py:90
  101.2 24.3 %collective-permute-done.9 = bf16[256,1280]{1,0:T(8,128)(2,1)S(1)} collective-permute-done((bf16[256,1280]{1,0:T(8,128)(2,1)S(1)}, bf16[256,1280]{1,0:T(8,128)(2,1)S(1)}, u32[]{:S(2)}, u32[]{:S(2)}) %collective-permute-start.9) | collective-permute-done | bytes 655392 | tf_op jit(solution)/shard_map/ppermute | solution.py:90
  135.5 13.2 %collective-permute-done.26 = bf16[256,1280]{1,0:T(8,128)(2,1)S(1)} collective-permute-done((bf16[256,1280]{1,0:T(8,128)(2,1)S(1)}, bf16[256,1280]{1,0:T(8,128)(2,1)S(1)}, u32[]{:S(2)}, u32[]{:S(2)}) %collective-permute-start.26) | collective-permute-done | bytes 655392 | tf_op jit(solution)/shard_map/ppermute | solution.py:90
  167.5 20.3 %collective-permute-done.20 = bf16[2,256,2560]{2,1,0:T(8,128)(2,1)} collective-permute-done((bf16[2,256,2560]{2,1,0:T(8,128)(2,1)}, bf16[2,256,2560]{2,1,0:T(8,128)(2,1)}, u32[]{:S(2)}, u32[]{:S(2)}) %collective-permute-start.20) | collective-permute-done | bytes 2621472 | tf_op jit(solution)/shard_map/ppermute | solution.py:94
  231.8 6.3 fusion.401
  248.9 9.3 %collective-permute-done.22 = bf16[256,2560]{1,0:T(8,128)(2,1)} collective-permute-done((bf16[256,2560]{1,0:T(8,128)(2,1)}, bf16[256,2560]{1,0:T(8,128)(2,1)}, u32[]{:S(2)}, u32[]{:S(2)}) %collective-permute-start.22) | collective-permute-done | bytes 1310752 | tf_op jit(solution)/shard_map/ppermute | solution.py:94
  285.1 9.5 %pad_maximum_fusion.1 = bf16[1024,2560]{1,0:T(8,128)(2,1)} fusion(bf16[256,2560]{1,0:T(8,128)(2,1)} %collective-permute-done.34, bf16[256,2560]{1,0:T(8,128)(2,1)S(1)} %copy-done.60, bf16[256,2560]{1,0:T(8,128)(2,1)S(1)} %copy-done.61, bf16[256,2560]{1,0:T(8,128)(2,1)S(1)} %bitcast.448), kind=kLoop, calls=%fused_computation.29 | loop fusion | flops 20971520 | bytes 10485760 | tf_op jit(solution)/shard_map/concatenate | solution.py:619
  330.5 5.9 collective-permute-done.29
  338.2 7.7 collective-permute-done.31
  424.4 7.1 collective-permute-done.39
  439.0 7.2 fusion.5
  467.2 6.4 collective-permute-done.47
  527.5 6.5 collective-permute-done.55
  536.0 8.9 %collective-permute-done.56 = bf16[64,2560]{1,0:T(8,128)(2,1)S(1)} collective-permute-done((bf16[64,2560]{1,0:T(8,128)(2,1)S(1)}, bf16[64,2560]{1,0:T(8,128)(2,1)S(1)}, u32[]{:S(2)}, u32[]{:S(2)}) %collective-permute-start.56) | collective-permute-done | bytes 327712 | tf_op jit(solution)/shard_map/ppermute | solution.py:90
  568.3 11.0 %collective-permute-done.69 = bf16[640,512]{1,0:T(8,128)(2,1)S(1)} collective-permute-done((bf16[640,512]{1,0:T(8,128)(2,1)S(1)}, bf16[640,512]{1,0:T(8,128)(2,1)S(1)}, u32[]{:S(2)}, u32[]{:S(2)}) %collective-permute-start.69) | collective-permute-done | bytes 655392 | tf_op jit(solution)/shard_map/ppermute | solution.py:90
  614.1 8.5 %fusion = (f32[5,3,128]{2,1,0:T(4,128)}, f32[5,1024,128,3]{2,1,3,0:T(8,128)}) fusion(f32[5,3,128,1024]{2,3,1,0:T(8,128)} %get-tuple-element.213, f32[5,3,128]{2,1,0:T(4,128)} %log_add_fusion, bf16[1024,5,64,1]{0,2,3,1:T(8,128)(2,1)S(1)} %bitcast.459, bf16[128,5,3,64]{0,3,2,1:T(8,128)(2,1)} %bitcast.492), kind=kOutput, calls=%fused_computation.2 | convolution fusion | flops 257554560 | bytes 16645120 | tf_op jit(solution)/shard_map/qghd,kgd->ghqk/dot_general | solution.py:473
  650.7 7.2 fusion.2
  716.0 13.9 %collective-permute-done.83 = bf16[256,1280]{1,0:T(8,128)(2,1)} collective-permute-done((bf16[256,1280]{1,0:T(8,128)(2,1)}, bf16[256,1280]{1,0:T(8,128)(2,1)}, u32[]{:S(2)}, u32[]{:S(2)}) %collective-permute-start.83) | collective-permute-done | bytes 655392 | tf_op jit(solution)/shard_map/ppermute | solution.py:90
  734.3 16.4 %collective-permute-done.84 = bf16[256,1280]{1,0:T(8,128)(2,1)S(1)} collective-permute-done((bf16[256,1280]{1,0:T(8,128)(2,1)S(1)}, bf16[256,1280]{1,0:T(8,128)(2,1)S(1)}, u32[]{:S(2)}, u32[]{:S(2)}) %collective-permute-start.84) | collective-permute-done | bytes 655392 | tf_op jit(solution)/shard_map/ppermute | solution.py:90
  758.3 9.4 %collective-permute-done.85 = bf16[128,1280]{1,0:T(8,128)(2,1)S(1)} collective-permute-done((bf16[128,1280]{1,0:T(8,128)(2,1)S(1)}, bf16[128,1280]{1,0:T(8,128)(2,1)S(1)}, u32[]{:S(2)}, u32[]{:S(2)}) %collective-permute-start.85) | collective-permute-done | bytes 327712 | tf_op jit(solution)/shard_map/ppermute | solution.py:98
  791.9 9.7 %collective-permute-done.94 = bf16[32,5120]{1,0:T(8,128)(2,1)S(1)} collective-permute-done((bf16[32,5120]{1,0:T(8,128)(2,1)S(1)}, bf16[32,5120]{1,0:T(8,128)(2,1)S(1)}, u32[]{:S(2)}, u32[]{:S(2)}) %collective-permute-start.94) | collective-permute-done | bytes 327712 | tf_op jit(solution)/shard_map/ppermute | solution.py:94
  (934 shorter events, 522.5 us)
Async XLA Ops:
  7.2 794.5 %all-gather.2.cloned.1.call-start = ((), (), s32[]{:S(2)}) async-start(), calls=%async_computation | async-start | bytes 2949120 | tf_op jit(solution)/shard_map/all_gather | solution.py:502
  12.5 54.9 %collective-permute-start = (bf16[128,960]{1,0:T(8,128)(2,1)}, bf16[128,960]{1,0:T(8,128)(2,1)S(1)}, u32[]{:S(2)}, u32[]{:S(2)}) collective-permute-start(bf16[128,960]{1,0:T(8,128)(2,1)} %bitcast_select_fusion.5), channel_id=1, source_target_pairs={{0,64},{64,0},{1,65},{65,1},{2,66},{66,2},{3,67},{67,3},{4,68},{68... | collective-permute-start | bytes 737288 | tf_op jit(solution)/shard_map/ppermute | solution.py:106
  13.4 59.1 %collective-permute-start.14 = (bf16[320,512]{1,0:T(8,128)(2,1)}, bf16[320,512]{1,0:T(8,128)(2,1)}, u32[]{:S(2)}, u32[]{:S(2)}) collective-permute-start(bf16[320,512]{1,0:T(8,128)(2,1)} %select_bitcast_fusion.4), channel_id=1, source_target_pairs={{0,64},{64,0},{1,65},{65,1},{2,66},{66,2},{3,67},{67,3},{4,68},{68... | collective-permute-start | bytes 983048 | tf_op jit(solution)/shard_map/ppermute | solution.py:106
  73.7 52.1 %collective-permute-start.18 = (bf16[2,2,32,2560]{3,2,0,1:T(8,128)(2,1)S(1)}, bf16[2,2,32,2560]{3,2,0,1:T(8,128)(2,1)S(1)}, u32[]{:S(2)}, u32[]{:S(2)}) collective-permute-start(bf16[2,2,32,2560]{3,2,0,1:T(8,128)(2,1)S(1)} %get-tuple-element.166), channel_id=1, source_target_pairs={{0,16},{8,24},{16,32},{24,40},{32,48},{40,56},{48,0},{56,8},{1,17}... | collective-permute-start | bytes 1966088 | tf_op jit(solution)/shard_map/ppermute | solution.py:90
  75.8 55.0 %collective-permute-start.15 = (bf16[2,320,512]{2,1,0:T(8,128)(2,1)S(1)}, bf16[2,320,512]{2,1,0:T(8,128)(2,1)S(1)}, u32[]{:S(2)}, u32[]{:S(2)}) collective-permute-start(bf16[2,320,512]{2,1,0:T(8,128)(2,1)S(1)} %maximum_select_fusion.4), channel_id=1, source_target_pairs={{0,8},{8,0},{16,24},{24,16},{32,40},{40,32},{48,56},{56,48},{1,9},... | collective-permute-start | bytes 1966088 | tf_op jit(solution)/shard_map/ppermute | solution.py:98
  128.0 59.7 %collective-permute-start.20 = (bf16[2,256,2560]{2,1,0:T(8,128)(2,1)}, bf16[2,256,2560]{2,1,0:T(8,128)(2,1)}, u32[]{:S(2)}, u32[]{:S(2)}) collective-permute-start(bf16[2,256,2560]{2,1,0:T(8,128)(2,1)} %bitcast.56), channel_id=1, source_target_pairs={{0,6},{1,7},{2,0},{3,1},{4,2},{5,3},{6,4},{7,5},{8,14},{9,15},{10,... | collective-permute-start | bytes 7864328 | tf_op jit(solution)/shard_map/ppermute | solution.py:94
  130.8 60.5 %collective-permute-start.19 = (bf16[2,256,2560]{2,1,0:T(8,128)(2,1)}, bf16[2,256,2560]{2,1,0:T(8,128)(2,1)}, u32[]{:S(2)}, u32[]{:S(2)}) collective-permute-start(bf16[2,256,2560]{2,1,0:T(8,128)(2,1)} %bitcast.56), channel_id=1, source_target_pairs={{0,2},{1,3},{2,4},{3,5},{4,6},{5,7},{6,0},{7,1},{8,10},{9,11},{10,... | collective-permute-start | bytes 7864328 | tf_op jit(solution)/shard_map/ppermute | solution.py:94
  150.3 155.2 %collective-permute-start.27 = (bf16[1024,1280]{1,0:T(8,128)(2,1)}, bf16[1024,1280]{1,0:T(8,128)(2,1)}, u32[]{:S(2)}, u32[]{:S(2)}) collective-permute-start(bf16[1024,1280]{1,0:T(8,128)(2,1)} %pad_maximum_fusion.4), channel_id=1, source_target_pairs={{0,64},{64,0},{1,65},{65,1},{2,66},{66,2},{3,67},{67,3},{4,68},{68... | collective-permute-start | bytes 7864328 | tf_op jit(solution)/shard_map/ppermute | solution.py:106
  216.9 44.5 %collective-permute-start.16 = (bf16[2,640,512]{2,1,0:T(8,128)(2,1)}, bf16[2,640,512]{2,1,0:T(8,128)(2,1)}, u32[]{:S(2)}, u32[]{:S(2)}) collective-permute-start(bf16[2,640,512]{2,1,0:T(8,128)(2,1)} %bitcast.50), channel_id=1, source_target_pairs={{0,16},{8,24},{16,32},{24,40},{32,48},{40,56},{48,0},{56,8},{1,17}... | collective-permute-start | bytes 3932168 | tf_op jit(solution)/shard_map/ppermute | solution.py:90
  216.9 47.7 %collective-permute-start.17 = (bf16[2,640,512]{2,1,0:T(8,128)(2,1)}, bf16[2,640,512]{2,1,0:T(8,128)(2,1)}, u32[]{:S(2)}, u32[]{:S(2)}) collective-permute-start(bf16[2,640,512]{2,1,0:T(8,128)(2,1)} %bitcast.50), channel_id=1, source_target_pairs={{0,48},{8,56},{16,0},{24,8},{32,16},{40,24},{48,32},{56,40},{1,49}... | collective-permute-start | bytes 3932168 | tf_op jit(solution)/shard_map/ppermute | solution.py:90
  222.6 61.9 %collective-permute-start.34 = (bf16[256,2560]{1,0:T(8,128)(2,1)}, bf16[256,2560]{1,0:T(8,128)(2,1)}, u32[]{:S(2)}, u32[]{:S(2)}) collective-permute-start(bf16[256,2560]{1,0:T(8,128)(2,1)} %broadcast_select_fusion), channel_id=1, source_target_pairs={{0,6},{1,7},{2,0},{3,1},{4,2},{5,3},{6,4},{7,5},{8,14},{9,15},{10,... | collective-permute-start | bytes 3932168 | tf_op jit(solution)/shard_map/ppermute | solution.py:94
  296.3 67.2 %collective-permute-start.35 = (bf16[1024,2560]{1,0:T(8,128)(2,1)}, bf16[1024,2560]{1,0:T(8,128)(2,1)}, u32[]{:S(2)}, u32[]{:S(2)}) collective-permute-start(bf16[1024,2560]{1,0:T(8,128)(2,1)} %pad_maximum_fusion.1), channel_id=1, source_target_pairs={{0,64},{64,0},{1,65},{65,1},{2,66},{66,2},{3,67},{67,3},{4,68},{68... | collective-permute-start | bytes 15728648 | tf_op jit(solution)/shard_map/ppermute | solution.py:106
  327.7 79.6 %collective-permute-start.58 = (bf16[128,3584]{1,0:T(8,128)(2,1)}, bf16[128,3584]{1,0:T(8,128)(2,1)}, u32[]{:S(2)}, u32[]{:S(2)}) collective-permute-start(bf16[128,3584]{1,0:T(8,128)(2,1)} %pad_maximum_fusion.19), channel_id=1, source_target_pairs={{0,64},{64,0},{1,65},{65,1},{2,66},{66,2},{3,67},{67,3},{4,68},{68... | collective-permute-start | bytes 2752520 | tf_op jit(solution)/shard_map/ppermute | solution.py:106
  371.5 41.5 %collective-permute-start.36 = (bf16[128,3584]{1,0:T(8,128)(2,1)}, bf16[128,3584]{1,0:T(8,128)(2,1)}, u32[]{:S(2)}, u32[]{:S(2)}) collective-permute-start(bf16[128,3584]{1,0:T(8,128)(2,1)} %pad_maximum_fusion.18), channel_id=1, source_target_pairs={{0,64},{64,0},{1,65},{65,1},{2,66},{66,2},{3,67},{67,3},{4,68},{68... | collective-permute-start | bytes 2752520 | tf_op jit(solution)/shard_map/ppermute | solution.py:106
  423.1 52.4 %collective-permute-start.42 = (bf16[640,512]{1,0:T(8,128)(2,1)}, bf16[640,512]{1,0:T(8,128)(2,1)}, u32[]{:S(2)}, u32[]{:S(2)}) collective-permute-start(bf16[640,512]{1,0:T(8,128)(2,1)} %convolution_convert_fusion.24), channel_id=1, source_target_pairs={{0,16},{8,24},{16,32},{24,40},{32,48},{40,56},{48,0},{56,8},{1,17}... | collective-permute-start | bytes 1966088 | tf_op jit(solution)/shard_map/ppermute | solution.py:90
  505.5 41.1 %collective-permute-start.50 = (bf16[128,2560]{1,0:T(8,128)(2,1)}, bf16[128,2560]{1,0:T(8,128)(2,1)}, u32[]{:S(2)}, u32[]{:S(2)}) collective-permute-start(bf16[128,2560]{1,0:T(8,128)(2,1)} %pad_maximum_fusion.23), channel_id=1, source_target_pairs={{0,64},{64,0},{1,65},{65,1},{2,66},{66,2},{3,67},{67,3},{4,68},{68... | collective-permute-start | bytes 1966088 | tf_op jit(solution)/shard_map/ppermute | solution.py:106
  549.7 42.0 %collective-permute-start.51 = (bf16[256,1280]{1,0:T(8,128)(2,1)S(1)}, bf16[256,1280]{1,0:T(8,128)(2,1)S(1)}, u32[]{:S(2)}, u32[]{:S(2)}) collective-permute-start(bf16[256,1280]{1,0:T(8,128)(2,1)S(1)} %convolution_convert_fusion.16), channel_id=1, source_target_pairs={{0,48},{8,56},{16,0},{24,8},{32,16},{40,24},{48,32},{56,40},{1,49}... | collective-permute-start | bytes 1966088 | tf_op jit(solution)/shard_map/ppermute | solution.py:90
  589.1 80.4 %collective-permute-start.66 = (bf16[256,2560]{1,0:T(8,128)(2,1)}, bf16[256,2560]{1,0:T(8,128)(2,1)}, u32[]{:S(2)}, u32[]{:S(2)}) collective-permute-start(bf16[256,2560]{1,0:T(8,128)(2,1)} %fusion.27), channel_id=1, source_target_pairs={{0,2},{1,3},{2,4},{3,5},{4,6},{5,7},{6,0},{7,1},{8,10},{9,11},{10,... | collective-permute-start | bytes 3932168 | tf_op jit(solution)/shard_map/ppermute | solution.py:94
  598.6 42.9 %collective-permute-start.62 = (bf16[128,2560]{1,0:T(8,128)(2,1)}, bf16[128,2560]{1,0:T(8,128)(2,1)}, u32[]{:S(2)}, u32[]{:S(2)}) collective-permute-start(bf16[128,2560]{1,0:T(8,128)(2,1)} %fusion.80), channel_id=1, source_target_pairs={{0,8},{8,0},{16,24},{24,16},{32,40},{40,32},{48,56},{56,48},{1,9},... | collective-permute-start | bytes 1966088 | tf_op jit(solution)/shard_map/ppermute | solution.py:98
  645.9 44.4 %collective-permute-start.63 = (bf16[32,2560]{1,0:T(8,128)(2,1)}, bf16[32,2560]{1,0:T(8,128)(2,1)}, u32[]{:S(2)}, u32[]{:S(2)}) collective-permute-start(bf16[32,2560]{1,0:T(8,128)(2,1)} %get-tuple-element.112), channel_id=1, source_target_pairs={{0,2},{1,3},{2,4},{3,5},{4,6},{5,7},{6,0},{7,1},{8,10},{9,11},{10,... | collective-permute-start | bytes 491528 | tf_op jit(solution)/shard_map/ppermute | solution.py:94
  647.1 43.8 %collective-permute-start.64 = (bf16[32,2560]{1,0:T(8,128)(2,1)}, bf16[32,2560]{1,0:T(8,128)(2,1)}, u32[]{:S(2)}, u32[]{:S(2)}) collective-permute-start(bf16[32,2560]{1,0:T(8,128)(2,1)} %get-tuple-element.114), channel_id=1, source_target_pairs={{0,6},{1,7},{2,0},{3,1},{4,2},{5,3},{6,4},{7,5},{8,14},{9,15},{10,... | collective-permute-start | bytes 491528 | tf_op jit(solution)/shard_map/ppermute | solution.py:94
  649.2 41.7 %collective-permute-start.65 = (bf16[32,2560]{1,0:T(8,128)(2,1)}, bf16[32,2560]{1,0:T(8,128)(2,1)}, u32[]{:S(2)}, u32[]{:S(2)}) collective-permute-start(bf16[32,2560]{1,0:T(8,128)(2,1)} %get-tuple-element.113), channel_id=1, source_target_pairs={{0,4},{1,5},{2,6},{3,7},{4,0},{5,1},{6,2},{7,3},{8,12},{9,13},{10,... | collective-permute-start | bytes 491528 | tf_op jit(solution)/shard_map/ppermute | solution.py:94
  682.1 50.2 %collective-permute-start.90 = (bf16[64,2560]{1,0:T(8,128)(2,1)}, bf16[64,2560]{1,0:T(8,128)(2,1)}, u32[]{:S(2)}, u32[]{:S(2)}) collective-permute-start(bf16[64,2560]{1,0:T(8,128)(2,1)} %get-tuple-element.111), channel_id=1, source_target_pairs={{0,16},{8,24},{16,32},{24,40},{32,48},{40,56},{48,0},{56,8},{1,17}... | collective-permute-start | bytes 983048 | tf_op jit(solution)/shard_map/ppermute | solution.py:90
  689.8 61.8 %collective-permute-start.89 = (bf16[64,2560]{1,0:T(8,128)(2,1)}, bf16[64,2560]{1,0:T(8,128)(2,1)}, u32[]{:S(2)}, u32[]{:S(2)}) collective-permute-start(bf16[64,2560]{1,0:T(8,128)(2,1)} %get-tuple-element.110), channel_id=1, source_target_pairs={{0,48},{8,56},{16,0},{24,8},{32,16},{40,24},{48,32},{56,40},{1,49}... | collective-permute-start | bytes 983048 | tf_op jit(solution)/shard_map/ppermute | solution.py:90
  (269 other events, 3494.5 us)
Sparse Core Ops, SparseCore 0:
  713.8 66.3 all-gather.1

commit v7 on v6

--- a/solution.py
+++ b/solution.py
@@ -190,7 +190,7 @@
     own = gate(own, waits[0])
     other = y_near(own)
     pair = jnp.stack([own, other], axis=1).reshape(2, 2 * PADDED, UNIT)
-    pair = gate(pair, waits[1])
+    pair = gate(pair, *waits[1:])
     layers, unused = ring_gather_both(z_step, pair)
     return ([jnp.concatenate(blocks, axis=0) for blocks in layers], other)
 
@@ -221,7 +221,7 @@
     column = jnp.stack(blocks, axis=1)
     column = column.reshape(2, SPREAD // 4, 2 * UNIT)
     near = (x_step(column, 1), x_step(column, -1))
-    return (column, near, (other, blocks[-1]))
+    return (column, near, (other, blocks[1], blocks[-1]))
 
 
 def layer_weights(place, mine):
@@ -232,8 +232,9 @@
 
 
 def gather_rows(own):
-    pair = jnp.concatenate([own, y_near(own)], axis=0)
-    return jnp.concatenate(ring_gather(z_step, 1, pair), axis=0)
+    other = y_near(own)
+    pair = jnp.concatenate([own, other], axis=0)
+    return (jnp.concatenate(ring_gather(z_step, 1, pair), axis=0), other)
 
 
 def scatter_rows(partial):
@@ -259,8 +260,8 @@
         count_of_rows, KEY_VALUE_HEADS, QUERY_HEADS // KEY_VALUE_HEADS, HEAD_SIZE
     )
     key_portion = turned[:, QUERY_HEADS:].reshape(count_of_rows, KV_WIDTH)
-    key_value = gather_rows(jnp.concatenate([key_portion, value_part], axis=1))
-    others, near = fetch(key_value)
+    key_value, near_rows = gather_rows(jnp.concatenate([key_portion, value_part], axis=1))
+    others, near = fetch(key_value, near_rows)
     two, low = others[0]
     key_value = gate(key_value, *waits)
     key_row_block = key_value[:, :KV_WIDTH].reshape(-1, KEY_VALUE_HEADS, HEAD_SIZE)
@@ -475,10 +476,6 @@
     )
     row_dots = jnp.sum(attention_full * grad_attention, axis=-1, keepdims=True)
     far, column, wide = wide
-    early = None
-    if before:
-        early = across_y(jnp.concatenate(before[:2], axis=1))
-        far = far + (early,)
     row_dots = gate(row_dots, *far)
     grad_scores = (attention_full * (grad_attention - row_dots)).astype(BF16)
     key_gradient = (
@@ -495,12 +492,9 @@
         * SCALE
     )
     key_value = gate(key_value, column, down)
+    early = None
     if before:
-        early = across_x(place, early)
-        key_value = gate(key_value, early)
-        piece = jnp.concatenate([early, before[2]], axis=1).astype(BF16)
-        pieces = lax.all_gather(piece, "dp").astype(F32)
-        early = (pieces[0::2] + pieces[1::2]).astype(BF16).reshape(-1, piece.shape[-1])
+        early = across_y(jnp.concatenate(before[:2] + [down], axis=1))
     key_gradient, value_low = (key_value[:, :KV_WIDTH], key_value[:, KV_WIDTH:].astype(BF16))
     grad_query_key = rotary_embedding_backward(
         jnp.concatenate(
@@ -537,8 +531,10 @@
     )
     waits = ((), ())
     if before:
-        down = across_x(place, across_y(down))
-        waits = ((down,), ())
+        left_rows = gate(left_rows, early, wide)
+        early = across_x(place, early)
+        piece = across_far(jnp.concatenate([early, before[2]], axis=1))
+        early = all_quarters(place, piece)
     left_rows = jnp.concatenate(
         [left_rows[:, :SPREAD], left_rows[:, SPREAD:], gain_place.astype(BF16)], axis=0
     )
@@ -614,8 +610,8 @@
     live_rows = (segment_mine < seq_lengths.shape[0]).astype(F32)
 
     geometry = (cosine_table, sine_portion, allowed)
-    def fetch(key_value):
-        layers, unused = ring_gather_both(x_step, column, near_wide, (key_value,))
+    def fetch(key_value, near_rows):
+        layers, unused = ring_gather_both(x_step, column, near_wide, (near_rows,))
         wide = [jnp.concatenate(blocks, axis=0) for blocks in layers]
         wholes, near = gather_down(place, down_pack, other, (key_value,))
         return ([[(value, sibling(value)) for value in pair] for pair in zip(wide, wholes)], near)
@@ -625,7 +621,7 @@
     )
     middle = middle.astype(BF16).astype(F32)
     result, stored_second, unused = forward_layer(
-        place, middle, weights_second, lambda key_value: (others[1:], ()), (), *geometry
+        place, middle, weights_second, lambda *unused: (others[1:], ()), (), *geometry
     )
     grad, (pair, down, wide), unused = backward_layer(
         place,
@@ -638,7 +634,7 @@
         *geometry,
     )
     grad = grad.astype(BF16).astype(F32)
-    grad, (last, down_first, wide_first), early = backward_layer(
+    grad, (last, unused, wide_first), early = backward_layer(
         place,
         grad,
         weights_first,
@@ -656,10 +652,12 @@
     )[None, :, None]
 
     late = across_x(place, across_y(last))
-    late = jnp.concatenate([late, down_first, wide_first], axis=1)
-    late = all_quarters(place, across_far(late))
-    late_first, early_first = (late[:, :UNIT], late[:, UNIT:])
-    late_second, early_second = (early[:, :UNIT], early[:, UNIT:])
+    late = all_quarters(place, across_far(jnp.concatenate([late, wide_first], axis=1)))
+    late_first = late[:, :UNIT]
+    early_first = jnp.concatenate([early[:, 2 * UNIT : 3 * UNIT], late[:, UNIT:]], axis=1)
+    late_second = early[:, :UNIT]
+    early_second = jnp.concatenate([early[:, UNIT : 2 * UNIT], early[:, 3 * UNIT :]], axis=1)
+
     sums = []
     for for_first, for_second in ((early_first, early_second), (late_first, late_second)):
         own = jnp.where(first, for_first, for_second)

time: 840 us -> 795 us (0.946)
  waiting for transfers between devices: 287 us -> 233 us
  between operations: 45.5 us -> 33.6 us
    ppermute x41, waiting for transfers between devices: 200 us -> 140 us  [z_step(): lax.ppermute(value, 'fsdp', [(i, (i + 2 * step) % 8) for i in range(8)])]
    ppermute x24, waiting for transfers between devices: 62.3 us -> 70.7 us  [x_step(): lax.ppermute(value, 'dp', [(i, (i + 2 * step) % 8) for i in range(8)])]
    ppermute x12 -> x11, waiting for transfers between devices: 19.7 us -> 17.2 us  [y_near(): return lax.ppermute(value, 'fsdp', [(i, i ^ 1) for i in range(8)])]
    slice x21 -> x22, local copies, waits for them, and re-layouts: 15.9 us -> 17.1 us  [gate(): corner = other[(-1,) * other.ndim]]
    unnamed x403 -> x401, local copies, waits for them, and re-layouts: 25.5 us -> 24.5 us
  transfers between devices with their start and end apart: 100 -> 99, of which waited for: 41 -> 42; matrix products, arithmetic and copies ran while one was open for 42% -> 48% of each run, Pallas kernels for 0% -> 0%
where the time goes in v7:
time: 795 us; the launch traced here: 781 us
  waiting for transfers between devices  233 us (29%)
  matrix products  165 us (21%)
  other arithmetic  126 us (16%)
  local copies, waits for them, and re-layouts  112 us (14%)
  starting transfers between devices  112 us (14%)
  between operations  33.6 us (4%)
    ppermute x41, waiting for transfers between devices, z_step(): lax.ppermute(value, 'fsdp', [(i, (i + 2 * step) % 8) for i in range(8)])  140 us
    ppermute x24, waiting for transfers between devices, x_step(): lax.ppermute(value, 'dp', [(i, (i + 2 * step) % 8) for i in range(8)])  70.7 us
    dot_general x24, matrix products, backward_product(): lax.dot_general(grad, weight, (((1,), (1,)), ((), ())), preferred_element...  54.6 us
    ppermute x41, starting transfers between devices, z_step(): lax.ppermute(value, 'fsdp', [(i, (i + 2 * step) % 8) for i in range(8)])  53.2 us
    dot_general x16, matrix products, product(): return jnp.dot(left, right, preferred_element_type=F32)  35.3 us
    ppermute x24, starting transfers between devices, x_step(): lax.ppermute(value, 'dp', [(i, (i + 2 * step) % 8) for i in range(8)])  34.1 us
    dot_general x26, matrix products, outer_sum(): lax.dot_general(left, right, (((0,), (0,)), ((), ())), preferred_element_...  34.1 us
    unnamed x401, local copies, waits for them, and re-layouts  24.5 us
  transfers between devices with their start and end apart: 99, of which 42 were waited for; matrix products, arithmetic and copies ran while one was open for 48% of the time, Pallas kernels for 0%

profile of v7, /device:TPU:0, one launch (start us, length us, event | category | flops | bytes accessed | tf_op | source)
XLA Modules:
  0.0 781.4 jit_solution(12061124420219611432)
XLA Ops:
  11.6 5.1 fusion.18
  20.0 7.9 %collective-permute-done.2 = bf16[2,32,2560]{2,1,0:T(8,128)(2,1)S(1)} collective-permute-done((bf16[2,32,2560]{2,1,0:T(8,128)(2,1)S(1)}, bf16[2,32,2560]{2,1,0:T(8,128)(2,1)S(1)}, u32[]{:S(2)}, u32[]{:S(2)}) %collective-permute-start.2) | collective-permute-done | bytes 327712 | tf_op jit(solution)/shard_map/ppermute | solution.py:98
  38.6 8.0 %collective-permute-done.4 = bf16[2,2,32,2560]{3,2,0,1:T(8,128)(2,1)} collective-permute-done((bf16[2,2,32,2560]{3,2,0,1:T(8,128)(2,1)}, bf16[2,2,32,2560]{3,2,0,1:T(8,128)(2,1)}, u32[]{:S(2)}, u32[]{:S(2)}) %collective-permute-start.4) | collective-permute-done | bytes 655392 | tf_op jit(solution)/shard_map/ppermute | solution.py:90
  53.8 9.2 %collective-permute-done.5 = bf16[2,2,32,2560]{3,2,0,1:T(8,128)(2,1)} collective-permute-done((bf16[2,2,32,2560]{3,2,0,1:T(8,128)(2,1)}, bf16[2,2,32,2560]{3,2,0,1:T(8,128)(2,1)}, u32[]{:S(2)}, u32[]{:S(2)}) %collective-permute-start.5) | collective-permute-done | bytes 655392 | tf_op jit(solution)/shard_map/ppermute | solution.py:90
  77.1 19.9 %collective-permute-done.8 = bf16[2,256,1280]{2,1,0:T(8,128)(2,1)S(1)} collective-permute-done((bf16[2,256,1280]{2,1,0:T(8,128)(2,1)S(1)}, bf16[2,256,1280]{2,1,0:T(8,128)(2,1)S(1)}, u32[]{:S(2)}, u32[]{:S(2)}) %collective-permute-start.8) | collective-permute-done | bytes 1310752 | tf_op jit(solution)/shard_map/ppermute | solution.py:90
  122.9 37.1 %collective-permute-done.19 = bf16[2,256,2560]{2,1,0:T(8,128)(2,1)S(1)} collective-permute-done((bf16[2,256,2560]{2,1,0:T(8,128)(2,1)}, bf16[2,256,2560]{2,1,0:T(8,128)(2,1)S(1)}, u32[]{:S(2)}, u32[]{:S(2)}) %collective-permute-start.19) | collective-permute-done | bytes 2621472 | tf_op jit(solution)/shard_map/ppermute | solution.py:94
  194.1 8.1 %collective-permute-done.14 = bf16[256,640]{1,0:T(8,128)(2,1)S(1)} collective-permute-done((bf16[256,640]{1,0:T(8,128)(2,1)S(1)}, bf16[256,640]{1,0:T(8,128)(2,1)S(1)}, u32[]{:S(2)}, u32[]{:S(2)}) %collective-permute-start.14) | collective-permute-done | bytes 327712 | tf_op jit(solution)/shard_map/ppermute | solution.py:90
  222.7 9.5 %pad_maximum_fusion = bf16[1024,2560]{1,0:T(8,128)(2,1)} fusion(bf16[256,2560]{1,0:T(8,128)(2,1)} %collective-permute-done.22, bf16[256,2560]{1,0:T(8,128)(2,1)S(1)} %copy-done.69, bf16[256,2560]{1,0:T(8,128)(2,1)S(1)} %copy-done.68, bf16[256,2560]{1,0:T(8,128)(2,1)S(1)} %bitcast.433), kind=kLoop, calls=%fused_computation.28 | loop fusion | flops 20971520 | bytes 10485760 | tf_op jit(solution)/shard_map/concatenate | solution.py:615
  237.6 5.8 pad_maximum_fusion.1
  276.6 5.1 multiply_convert_fusion.5
  311.8 6.2 collective-permute-done.29
  319.5 8.4 %collective-permute-done.31 = bf16[256,640]{1,0:T(8,128)(2,1)S(1)} collective-permute-done((bf16[256,640]{1,0:T(8,128)(2,1)S(1)}, bf16[256,640]{1,0:T(8,128)(2,1)S(1)}, u32[]{:S(2)}, u32[]{:S(2)}) %collective-permute-start.31) | collective-permute-done | bytes 327712 | tf_op jit(solution)/shard_map/ppermute | solution.py:90
  405.8 7.0 collective-permute-done.39
  420.2 7.1 fusion.5
  449.1 5.9 collective-permute-done.47
  462.9 5.2 collective-permute-done.40
  468.1 5.3 collective-permute-done.41
  515.6 6.0 collective-permute-done.56
  544.2 10.2 %collective-permute-done.65 = bf16[640,512]{1,0:T(8,128)(2,1)S(1)} collective-permute-done((bf16[640,512]{1,0:T(8,128)(2,1)S(1)}, bf16[640,512]{1,0:T(8,128)(2,1)S(1)}, u32[]{:S(2)}, u32[]{:S(2)}) %collective-permute-start.65) | collective-permute-done | bytes 655392 | tf_op jit(solution)/shard_map/ppermute | solution.py:90
  586.2 5.1 fusion
  596.5 7.2 fusion.2
  669.1 7.3 collective-permute-done.75
  693.2 11.7 %collective-permute-done.80 = bf16[256,1280]{1,0:T(8,128)(2,1)S(1)} collective-permute-done((bf16[256,1280]{1,0:T(8,128)(2,1)S(1)}, bf16[256,1280]{1,0:T(8,128)(2,1)S(1)}, u32[]{:S(2)}, u32[]{:S(2)}) %collective-permute-start.80) | collective-permute-done | bytes 655392 | tf_op jit(solution)/shard_map/ppermute | solution.py:90
  709.1 11.5 %collective-permute-done.81 = bf16[256,1280]{1,0:T(8,128)(2,1)S(1)} collective-permute-done((bf16[256,1280]{1,0:T(8,128)(2,1)S(1)}, bf16[256,1280]{1,0:T(8,128)(2,1)S(1)}, u32[]{:S(2)}, u32[]{:S(2)}) %collective-permute-start.81) | collective-permute-done | bytes 655392 | tf_op jit(solution)/shard_map/ppermute | solution.py:90
  (933 shorter events, 527.9 us)
Async XLA Ops:
  6.7 44.2 %collective-permute-start = (bf16[128,960]{1,0:T(8,128)(2,1)}, bf16[128,960]{1,0:T(8,128)(2,1)S(1)}, u32[]{:S(2)}, u32[]{:S(2)}) collective-permute-start(bf16[128,960]{1,0:T(8,128)(2,1)} %bitcast_select_fusion.5), channel_id=1, source_target_pairs={{0,64},{64,0},{1,65},{65,1},{2,66},{66,2},{3,67},{67,3},{4,68},{68... | collective-permute-start | bytes 737288 | tf_op jit(solution)/shard_map/ppermute | solution.py:106
  7.6 60.2 %collective-permute-start.15 = (bf16[320,512]{1,0:T(8,128)(2,1)}, bf16[320,512]{1,0:T(8,128)(2,1)}, u32[]{:S(2)}, u32[]{:S(2)}) collective-permute-start(bf16[320,512]{1,0:T(8,128)(2,1)} %select_bitcast_fusion.4), channel_id=1, source_target_pairs={{0,64},{64,0},{1,65},{65,1},{2,66},{66,2},{3,67},{67,3},{4,68},{68... | collective-permute-start | bytes 983048 | tf_op jit(solution)/shard_map/ppermute | solution.py:106
  71.6 42.2 %collective-permute-start.16 = (bf16[2,320,512]{2,1,0:T(8,128)(2,1)S(1)}, bf16[2,320,512]{2,1,0:T(8,128)(2,1)S(1)}, u32[]{:S(2)}, u32[]{:S(2)}) collective-permute-start(bf16[2,320,512]{2,1,0:T(8,128)(2,1)S(1)} %maximum_select_fusion.5), channel_id=1, source_target_pairs={{0,8},{8,0},{16,24},{24,16},{32,40},{40,32},{48,56},{56,48},{1,9},... | collective-permute-start | bytes 1966088 | tf_op jit(solution)/shard_map/ppermute | solution.py:98
  100.7 73.7 %collective-permute-start.20 = (bf16[2,256,2560]{2,1,0:T(8,128)(2,1)}, bf16[2,256,2560]{2,1,0:T(8,128)(2,1)}, u32[]{:S(2)}, u32[]{:S(2)}) collective-permute-start(bf16[2,256,2560]{2,1,0:T(8,128)(2,1)} %bitcast.56), channel_id=1, source_target_pairs={{0,6},{1,7},{2,0},{3,1},{4,2},{5,3},{6,4},{7,5},{8,14},{9,15},{10,... | collective-permute-start | bytes 7864328 | tf_op jit(solution)/shard_map/ppermute | solution.py:94
  103.4 56.6 %collective-permute-start.19 = (bf16[2,256,2560]{2,1,0:T(8,128)(2,1)}, bf16[2,256,2560]{2,1,0:T(8,128)(2,1)S(1)}, u32[]{:S(2)}, u32[]{:S(2)}) collective-permute-start(bf16[2,256,2560]{2,1,0:T(8,128)(2,1)} %bitcast.56), channel_id=1, source_target_pairs={{0,2},{1,3},{2,4},{3,5},{4,6},{5,7},{6,0},{7,1},{8,10},{9,11},{10,... | collective-permute-start | bytes 7864328 | tf_op jit(solution)/shard_map/ppermute | solution.py:94
  111.9 50.5 %collective-permute-start.11 = (bf16[1024,1280]{1,0:T(8,128)(2,1)S(1)}, bf16[1024,1280]{1,0:T(8,128)(2,1)S(1)}, u32[]{:S(2)}, u32[]{:S(2)}) collective-permute-start(bf16[1024,1280]{1,0:T(8,128)(2,1)S(1)} %pad_maximum_fusion.3), channel_id=1, source_target_pairs={{0,64},{64,0},{1,65},{65,1},{2,66},{66,2},{3,67},{67,3},{4,68},{68... | collective-permute-start | bytes 7864328 | tf_op jit(solution)/shard_map/ppermute | solution.py:106
  118.7 167.7 %collective-permute-start.27 = (bf16[1024,1280]{1,0:T(8,128)(2,1)}, bf16[1024,1280]{1,0:T(8,128)(2,1)}, u32[]{:S(2)}, u32[]{:S(2)}) collective-permute-start(bf16[1024,1280]{1,0:T(8,128)(2,1)} %pad_maximum_fusion.5), channel_id=1, source_target_pairs={{0,64},{64,0},{1,65},{65,1},{2,66},{66,2},{3,67},{67,3},{4,68},{68... | collective-permute-start | bytes 7864328 | tf_op jit(solution)/shard_map/ppermute | solution.py:106
  190.8 46.7 %collective-permute-start.34 = (bf16[256,2560]{1,0:T(8,128)(2,1)}, bf16[256,2560]{1,0:T(8,128)(2,1)}, u32[]{:S(2)}, u32[]{:S(2)}) collective-permute-start(bf16[256,2560]{1,0:T(8,128)(2,1)} %broadcast_select_fusion), channel_id=1, source_target_pairs={{0,6},{1,7},{2,0},{3,1},{4,2},{5,3},{6,4},{7,5},{8,14},{9,15},{10,... | collective-permute-start | bytes 3932168 | tf_op jit(solution)/shard_map/ppermute | solution.py:94
  205.4 38.5 %collective-permute-start.17 = (bf16[2,640,512]{2,1,0:T(8,128)(2,1)}, bf16[2,640,512]{2,1,0:T(8,128)(2,1)}, u32[]{:S(2)}, u32[]{:S(2)}) collective-permute-start(bf16[2,640,512]{2,1,0:T(8,128)(2,1)} %bitcast.50), channel_id=1, source_target_pairs={{0,16},{8,24},{16,32},{24,40},{32,48},{40,56},{48,0},{56,8},{1,17}... | collective-permute-start | bytes 3932168 | tf_op jit(solution)/shard_map/ppermute | solution.py:90
  205.4 40.9 %collective-permute-start.18 = (bf16[2,640,512]{2,1,0:T(8,128)(2,1)}, bf16[2,640,512]{2,1,0:T(8,128)(2,1)}, u32[]{:S(2)}, u32[]{:S(2)}) collective-permute-start(bf16[2,640,512]{2,1,0:T(8,128)(2,1)} %bitcast.50), channel_id=1, source_target_pairs={{0,48},{8,56},{16,0},{24,8},{32,16},{40,24},{48,32},{56,40},{1,49}... | collective-permute-start | bytes 3932168 | tf_op jit(solution)/shard_map/ppermute | solution.py:90
  232.2 44.4 %collective-permute-start.23 = (bf16[1024,2560]{1,0:T(8,128)(2,1)}, bf16[1024,2560]{1,0:T(8,128)(2,1)}, u32[]{:S(2)}, u32[]{:S(2)}) collective-permute-start(bf16[1024,2560]{1,0:T(8,128)(2,1)} %pad_maximum_fusion), channel_id=1, source_target_pairs={{0,64},{64,0},{1,65},{65,1},{2,66},{66,2},{3,67},{67,3},{4,68},{68... | collective-permute-start | bytes 15728648 | tf_op jit(solution)/shard_map/ppermute | solution.py:106
  243.3 104.8 %collective-permute-start.35 = (bf16[1024,2560]{1,0:T(8,128)(2,1)}, bf16[1024,2560]{1,0:T(8,128)(2,1)}, u32[]{:S(2)}, u32[]{:S(2)}) collective-permute-start(bf16[1024,2560]{1,0:T(8,128)(2,1)} %pad_maximum_fusion.1), channel_id=1, source_target_pairs={{0,64},{64,0},{1,65},{65,1},{2,66},{66,2},{3,67},{67,3},{4,68},{68... | collective-permute-start | bytes 15728648 | tf_op jit(solution)/shard_map/ppermute | solution.py:106
  309.1 81.6 %collective-permute-start.58 = (bf16[128,3584]{1,0:T(8,128)(2,1)}, bf16[128,3584]{1,0:T(8,128)(2,1)S(1)}, u32[]{:S(2)}, u32[]{:S(2)}) collective-permute-start(bf16[128,3584]{1,0:T(8,128)(2,1)} %pad_maximum_fusion.20), channel_id=1, source_target_pairs={{0,64},{64,0},{1,65},{65,1},{2,66},{66,2},{3,67},{67,3},{4,68},{68... | collective-permute-start | bytes 2752520 | tf_op jit(solution)/shard_map/ppermute | solution.py:106
  356.2 38.1 %collective-permute-start.36 = (bf16[128,3584]{1,0:T(8,128)(2,1)}, bf16[128,3584]{1,0:T(8,128)(2,1)}, u32[]{:S(2)}, u32[]{:S(2)}) collective-permute-start(bf16[128,3584]{1,0:T(8,128)(2,1)} %pad_maximum_fusion.19), channel_id=1, source_target_pairs={{0,64},{64,0},{1,65},{65,1},{2,66},{66,2},{3,67},{67,3},{4,68},{68... | collective-permute-start | bytes 2752520 | tf_op jit(solution)/shard_map/ppermute | solution.py:106
  357.3 34.6 %collective-permute-start.37 = (bf16[128,3072]{1,0:T(8,128)(2,1)}, bf16[128,3072]{1,0:T(8,128)(2,1)}, u32[]{:S(2)}, u32[]{:S(2)}) collective-permute-start(bf16[128,3072]{1,0:T(8,128)(2,1)} %pad_maximum_fusion.21), channel_id=1, source_target_pairs={{0,64},{64,0},{1,65},{65,1},{2,66},{66,2},{3,67},{67,3},{4,68},{68... | collective-permute-start | bytes 2359304 | tf_op jit(solution)/shard_map/ppermute | solution.py:106
  403.8 51.5 %collective-permute-start.42 = (bf16[640,512]{1,0:T(8,128)(2,1)}, bf16[640,512]{1,0:T(8,128)(2,1)}, u32[]{:S(2)}, u32[]{:S(2)}) collective-permute-start(bf16[640,512]{1,0:T(8,128)(2,1)} %convolution_convert_fusion.24), channel_id=1, source_target_pairs={{0,16},{8,24},{16,32},{24,40},{32,48},{40,56},{48,0},{56,8},{1,17}... | collective-permute-start | bytes 1966088 | tf_op jit(solution)/shard_map/ppermute | solution.py:90
  419.6 36.7 %collective-permute-start.44 = (bf16[640,512]{1,0:T(8,128)(2,1)}, bf16[640,512]{1,0:T(8,128)(2,1)}, u32[]{:S(2)}, u32[]{:S(2)}) collective-permute-start(bf16[640,512]{1,0:T(8,128)(2,1)} %fusion.72), channel_id=1, source_target_pairs={{0,48},{8,56},{16,0},{24,8},{32,16},{40,24},{48,32},{56,40},{1,49}... | collective-permute-start | bytes 1966088 | tf_op jit(solution)/shard_map/ppermute | solution.py:90
  455.0 231.6 %collective-permute-start.77 = (bf16[128,2048]{1,0:T(8,128)(2,1)}, bf16[128,2048]{1,0:T(8,128)(2,1)}, u32[]{:S(2)}, u32[]{:S(2)}) collective-permute-start(bf16[128,2048]{1,0:T(8,128)(2,1)} %pad_maximum_fusion.27), channel_id=1, source_target_pairs={{0,64},{64,0},{1,65},{65,1},{2,66},{66,2},{3,67},{67,3},{4,68},{68... | collective-permute-start | bytes 1572872 | tf_op jit(solution)/shard_map/ppermute | solution.py:106
  555.6 61.8 %collective-permute-start.64 = (bf16[640,512]{1,0:T(8,128)(2,1)}, bf16[640,512]{1,0:T(8,128)(2,1)}, u32[]{:S(2)}, u32[]{:S(2)}) collective-permute-start(bf16[640,512]{1,0:T(8,128)(2,1)} %convolution_convert_fusion.20), channel_id=1, source_target_pairs={{0,16},{8,24},{16,32},{24,40},{32,48},{40,56},{48,0},{56,8},{1,17}... | collective-permute-start | bytes 1966088 | tf_op jit(solution)/shard_map/ppermute | solution.py:90
  561.3 57.9 %collective-permute-start.66 = (bf16[640,512]{1,0:T(8,128)(2,1)}, bf16[640,512]{1,0:T(8,128)(2,1)}, u32[]{:S(2)}, u32[]{:S(2)}) collective-permute-start(bf16[640,512]{1,0:T(8,128)(2,1)} %fusion.66), channel_id=1, source_target_pairs={{0,48},{8,56},{16,0},{24,8},{32,16},{40,24},{48,32},{56,40},{1,49}... | collective-permute-start | bytes 1966088 | tf_op jit(solution)/shard_map/ppermute | solution.py:90
  568.4 70.8 %collective-permute-start.62 = (bf16[256,2560]{1,0:T(8,128)(2,1)}, bf16[256,2560]{1,0:T(8,128)(2,1)}, u32[]{:S(2)}, u32[]{:S(2)}) collective-permute-start(bf16[256,2560]{1,0:T(8,128)(2,1)} %fusion.27), channel_id=1, source_target_pairs={{0,2},{1,3},{2,4},{3,5},{4,6},{5,7},{6,0},{7,1},{8,10},{9,11},{10,... | collective-permute-start | bytes 3932168 | tf_op jit(solution)/shard_map/ppermute | solution.py:94
  573.3 65.9 %collective-permute-start.63 = (bf16[256,2560]{1,0:T(8,128)(2,1)}, bf16[256,2560]{1,0:T(8,128)(2,1)}, u32[]{:S(2)}, u32[]{:S(2)}) collective-permute-start(bf16[256,2560]{1,0:T(8,128)(2,1)} %fusion.24), channel_id=1, source_target_pairs={{0,6},{1,7},{2,0},{3,1},{4,2},{5,3},{6,4},{7,5},{8,14},{9,15},{10,... | collective-permute-start | bytes 3932168 | tf_op jit(solution)/shard_map/ppermute | solution.py:94
  633.6 31.9 %collective-permute-start.72 = (bf16[128,3840]{1,0:T(8,128)(2,1)}, bf16[128,3840]{1,0:T(8,128)(2,1)}, u32[]{:S(2)}, u32[]{:S(2)}) collective-permute-start(bf16[128,3840]{1,0:T(8,128)(2,1)} %slice.1132), channel_id=1, source_target_pairs={{0,8},{8,0},{16,24},{24,16},{32,40},{40,32},{48,56},{56,48},{1,9},... | collective-permute-start | bytes 2949128 | tf_op jit(solution)/shard_map/ppermute | solution.py:98
  663.7 99.8 %collective-permute-start.71 = (bf16[128,960]{1,0:T(8,128)(2,1)S(1)}, bf16[128,960]{1,0:T(8,128)(2,1)S(1)}, u32[]{:S(2)}, u32[]{:S(2)}) collective-permute-start(bf16[128,960]{1,0:T(8,128)(2,1)S(1)} %get-tuple-element.56), channel_id=1, source_target_pairs={{0,64},{64,0},{1,65},{65,1},{2,66},{66,2},{3,67},{67,3},{4,68},{68... | collective-permute-start | bytes 737288 | tf_op jit(solution)/shard_map/ppermute | solution.py:106
  (267 other events, 2757.0 us)

commit v8 on v5

--- a/solution.py
+++ b/solution.py
@@ -531,10 +531,9 @@
     )
     waits = ((), ())
     if before:
-        left_rows = gate(left_rows, early)
+        left_rows = gate(left_rows, early, wide)
         early = across_x(place, early)
         piece = across_far(jnp.concatenate([early, before[2]], axis=1))
-        waits = ((early,), (piece,))
         early = all_quarters(place, piece)
     left_rows = jnp.concatenate(
         [left_rows[:, :SPREAD], left_rows[:, SPREAD:], gain_place.astype(BF16)], axis=0
@@ -650,7 +649,7 @@
         first, jnp.stack([ends[0], received]), jnp.stack([received, ends[1]])
     )[None, :, None]
 
-    late = across_x(place, across_y(gate(last, early)))
+    late = across_x(place, across_y(last))
     late = all_quarters(place, across_far(jnp.concatenate([late, wide_first], axis=1)))
     late_first = late[:, :UNIT]
     early_first = jnp.concatenate([early[:, 2 * UNIT : 3 * UNIT], late[:, UNIT:]], axis=1)

time: 779 us -> 761 us (0.977)
  waiting for transfers between devices: 247 us -> 228 us
    ppermute x24, waiting for transfers between devices: 77.3 us -> 50.2 us  [x_step(): lax.ppermute(value, 'dp', [(i, (i + 2 * step) % 8) for i in range(8)])]
    ppermute x41, waiting for transfers between devices: 139 us -> 154 us  [z_step(): lax.ppermute(value, 'fsdp', [(i, (i + 2 * step) % 8) for i in range(8)])]
    ppermute x2, waiting for transfers between devices: 14.2 us -> 4.91 us  [y_far(): return lax.ppermute(value, 'dp', [(i, i ^ 1) for i in range(8)])]
    unnamed x399 -> x393, local copies, waits for them, and re-layouts: 24.7 us -> 24.6 us
  transfers between devices with their start and end apart: 99 -> 99, of which waited for: 41 -> 43; matrix products, arithmetic and copies ran while one was open for 41% -> 42% of each run, Pallas kernels for 0% -> 0%
where the time goes in v8:
time: 761 us; the launch traced here: 747 us
  waiting for transfers between devices  228 us (30%)
  matrix products  163 us (21%)
  other arithmetic  112 us (15%)
  starting transfers between devices  111 us (15%)
  local copies, waits for them, and re-layouts  102 us (13%)
  between operations  30.6 us (4%)
    ppermute x41, waiting for transfers between devices, z_step(): lax.ppermute(value, 'fsdp', [(i, (i + 2 * step) % 8) for i in range(8)])  154 us
    dot_general x24, matrix products, backward_product(): lax.dot_general(grad, weight, (((1,), (1,)), ((), ())), preferred_element...  53.5 us
    ppermute x41, starting transfers between devices, z_step(): lax.ppermute(value, 'fsdp', [(i, (i + 2 * step) % 8) for i in range(8)])  53.5 us
    ppermute x24, waiting for transfers between devices, x_step(): lax.ppermute(value, 'dp', [(i, (i + 2 * step) % 8) for i in range(8)])  50.2 us
    ppermute x24, starting transfers between devices, x_step(): lax.ppermute(value, 'dp', [(i, (i + 2 * step) % 8) for i in range(8)])  35.3 us
    dot_general x16, matrix products, product(): return jnp.dot(left, right, preferred_element_type=F32)  34.9 us
    dot_general x26, matrix products, outer_sum(): lax.dot_general(left, right, (((0,), (0,)), ((), ())), preferred_element_...  31.4 us
    unnamed x393, local copies, waits for them, and re-layouts  24.6 us
  transfers between devices with their start and end apart: 99, of which 43 were waited for; matrix products, arithmetic and copies ran while one was open for 42% of the time, Pallas kernels for 0%

profile of v8, /device:TPU:0, one launch (start us, length us, event | category | flops | bytes accessed | tf_op | source)
XLA Modules:
  0.0 747.4 jit_solution(16663818584247320041)
XLA Ops:
  21.2 8.0 %collective-permute-done.2 = bf16[2,32,2560]{2,1,0:T(8,128)(2,1)S(1)} collective-permute-done((bf16[2,32,2560]{2,1,0:T(8,128)(2,1)S(1)}, bf16[2,32,2560]{2,1,0:T(8,128)(2,1)S(1)}, u32[]{:S(2)}, u32[]{:S(2)}) %collective-permute-start.2) | collective-permute-done | bytes 327712 | tf_op jit(solution)/shard_map/ppermute | solution.py:98
  38.3 8.5 %collective-permute-done.3 = bf16[2,2,32,2560]{3,2,0,1:T(8,128)(2,1)S(1)} collective-permute-done((bf16[2,2,32,2560]{3,2,0,1:T(8,128)(2,1)S(1)}, bf16[2,2,32,2560]{3,2,0,1:T(8,128)(2,1)S(1)}, u32[]{:S(2)}, u32[]{:S(2)}) %collective-permute-start.3) | collective-permute-done | bytes 655392 | tf_op jit(solution)/shard_map/ppermute | solution.py:90
  54.2 8.8 %collective-permute-done.4 = bf16[2,2,32,2560]{3,2,0,1:T(8,128)(2,1)S(1)} collective-permute-done((bf16[2,2,32,2560]{3,2,0,1:T(8,128)(2,1)S(1)}, bf16[2,2,32,2560]{3,2,0,1:T(8,128)(2,1)S(1)}, u32[]{:S(2)}, u32[]{:S(2)}) %collective-permute-start.4) | collective-permute-done | bytes 655392 | tf_op jit(solution)/shard_map/ppermute | solution.py:90
  75.6 20.0 %collective-permute-done.7 = bf16[2,256,1280]{2,1,0:T(8,128)(2,1)S(1)} collective-permute-done((bf16[2,256,1280]{2,1,0:T(8,128)(2,1)S(1)}, bf16[2,256,1280]{2,1,0:T(8,128)(2,1)S(1)}, u32[]{:S(2)}, u32[]{:S(2)}) %collective-permute-start.7) | collective-permute-done | bytes 1310752 | tf_op jit(solution)/shard_map/ppermute | solution.py:90
  100.9 9.9 %collective-permute-done.9 = bf16[256,1280]{1,0:T(8,128)(2,1)S(1)} collective-permute-done((bf16[256,1280]{1,0:T(8,128)(2,1)S(1)}, bf16[256,1280]{1,0:T(8,128)(2,1)S(1)}, u32[]{:S(2)}, u32[]{:S(2)}) %collective-permute-start.9) | collective-permute-done | bytes 655392 | tf_op jit(solution)/shard_map/ppermute | solution.py:90
  117.8 9.2 %collective-permute-done.20 = bf16[2,256,2560]{2,1,0:T(8,128)(2,1)S(1)} collective-permute-done((bf16[2,256,2560]{2,1,0:T(8,128)(2,1)S(1)}, bf16[2,256,2560]{2,1,0:T(8,128)(2,1)S(1)}, u32[]{:S(2)}, u32[]{:S(2)}) %collective-permute-start.20) | collective-permute-done | bytes 2621472 | tf_op jit(solution)/shard_map/ppermute | solution.py:94
  148.7 13.2 %collective-permute-done.22 = bf16[256,2560]{1,0:T(8,128)(2,1)} collective-permute-done((bf16[256,2560]{1,0:T(8,128)(2,1)}, bf16[256,2560]{1,0:T(8,128)(2,1)}, u32[]{:S(2)}, u32[]{:S(2)}) %collective-permute-start.22) | collective-permute-done | bytes 1310752 | tf_op jit(solution)/shard_map/ppermute | solution.py:94
  161.9 6.1 pad_maximum_fusion
  183.8 6.3 collective-permute-done.13
  199.6 6.3 fusion.391
  218.6 5.6 collective-permute-done.16
  281.4 5.5 collective-permute-done.29
  287.5 8.9 %collective-permute-done.31 = bf16[256,640]{1,0:T(8,128)(2,1)S(1)} collective-permute-done((bf16[256,640]{1,0:T(8,128)(2,1)S(1)}, bf16[256,640]{1,0:T(8,128)(2,1)S(1)}, u32[]{:S(2)}, u32[]{:S(2)}) %collective-permute-start.31) | collective-permute-done | bytes 327712 | tf_op jit(solution)/shard_map/ppermute | solution.py:90
  371.9 8.9 %collective-permute-done.39 = bf16[128,2560]{1,0:T(8,128)(2,1)S(1)} collective-permute-done((bf16[128,2560]{1,0:T(8,128)(2,1)S(1)}, bf16[128,2560]{1,0:T(8,128)(2,1)S(1)}, u32[]{:S(2)}, u32[]{:S(2)}) %collective-permute-start.39) | collective-permute-done | bytes 655392 | tf_op jit(solution)/shard_map/ppermute | solution.py:94
  386.4 7.1 fusion.5
  418.3 6.0 collective-permute-done.47
  482.8 5.9 collective-permute-done.56
  511.7 11.2 %collective-permute-done.65 = bf16[640,512]{1,0:T(8,128)(2,1)S(1)} collective-permute-done((bf16[640,512]{1,0:T(8,128)(2,1)S(1)}, bf16[640,512]{1,0:T(8,128)(2,1)S(1)}, u32[]{:S(2)}, u32[]{:S(2)}) %collective-permute-start.65) | collective-permute-done | bytes 655392 | tf_op jit(solution)/shard_map/ppermute | solution.py:90
  537.0 5.2 collective-permute-done.53
  565.4 7.2 fusion.2
  638.2 7.3 collective-permute-done.75
  662.3 11.6 %collective-permute-done.80 = bf16[256,1280]{1,0:T(8,128)(2,1)S(1)} collective-permute-done((bf16[256,1280]{1,0:T(8,128)(2,1)S(1)}, bf16[256,1280]{1,0:T(8,128)(2,1)S(1)}, u32[]{:S(2)}, u32[]{:S(2)}) %collective-permute-start.80) | collective-permute-done | bytes 655392 | tf_op jit(solution)/shard_map/ppermute | solution.py:90
  678.1 11.5 %collective-permute-done.81 = bf16[256,1280]{1,0:T(8,128)(2,1)S(1)} collective-permute-done((bf16[256,1280]{1,0:T(8,128)(2,1)S(1)}, bf16[256,1280]{1,0:T(8,128)(2,1)S(1)}, u32[]{:S(2)}, u32[]{:S(2)}) %collective-permute-start.81) | collective-permute-done | bytes 655392 | tf_op jit(solution)/shard_map/ppermute | solution.py:90
  704.0 5.6 collective-permute-start.96
  (922 shorter events, 513.1 us)
Async XLA Ops:
  7.0 43.5 %collective-permute-start.14 = (bf16[320,512]{1,0:T(8,128)(2,1)}, bf16[320,512]{1,0:T(8,128)(2,1)}, u32[]{:S(2)}, u32[]{:S(2)}) collective-permute-start(bf16[320,512]{1,0:T(8,128)(2,1)} %select_bitcast_fusion.4), channel_id=1, source_target_pairs={{0,64},{64,0},{1,65},{65,1},{2,66},{66,2},{3,67},{67,3},{4,68},{68... | collective-permute-start | bytes 983048 | tf_op jit(solution)/shard_map/ppermute | solution.py:106
  65.0 30.6 %collective-permute-start.7 = (bf16[2,256,1280]{2,1,0:T(8,128)(2,1)S(1)}, bf16[2,256,1280]{2,1,0:T(8,128)(2,1)S(1)}, u32[]{:S(2)}, u32[]{:S(2)}) collective-permute-start(bf16[2,256,1280]{2,1,0:T(8,128)(2,1)S(1)} %bitcast.468), channel_id=1, source_target_pairs={{0,16},{8,24},{16,32},{24,40},{32,48},{40,56},{48,0},{56,8},{1,17}... | collective-permute-start | bytes 3932168 | tf_op jit(solution)/shard_map/ppermute | solution.py:90
  65.2 34.5 %collective-permute-start.15 = (bf16[2,320,512]{2,1,0:T(8,128)(2,1)S(1)}, bf16[2,320,512]{2,1,0:T(8,128)(2,1)S(1)}, u32[]{:S(2)}, u32[]{:S(2)}) collective-permute-start(bf16[2,320,512]{2,1,0:T(8,128)(2,1)S(1)} %maximum_select_fusion.5), channel_id=1, source_target_pairs={{0,8},{8,0},{16,24},{24,16},{32,40},{40,32},{48,56},{56,48},{1,9},... | collective-permute-start | bytes 1966088 | tf_op jit(solution)/shard_map/ppermute | solution.py:98
  66.9 28.9 %collective-permute-start.8 = (bf16[2,256,1280]{2,1,0:T(8,128)(2,1)S(1)}, bf16[2,256,1280]{2,1,0:T(8,128)(2,1)S(1)}, u32[]{:S(2)}, u32[]{:S(2)}) collective-permute-start(bf16[2,256,1280]{2,1,0:T(8,128)(2,1)S(1)} %bitcast.469), channel_id=1, source_target_pairs={{0,48},{8,56},{16,0},{24,8},{32,16},{40,24},{48,32},{56,40},{1,49}... | collective-permute-start | bytes 3932168 | tf_op jit(solution)/shard_map/ppermute | solution.py:90
  71.1 55.9 %collective-permute-start.20 = (bf16[2,256,2560]{2,1,0:T(8,128)(2,1)S(1)}, bf16[2,256,2560]{2,1,0:T(8,128)(2,1)S(1)}, u32[]{:S(2)}, u32[]{:S(2)}) collective-permute-start(bf16[2,256,2560]{2,1,0:T(8,128)(2,1)S(1)} %bitcast.452), channel_id=1, source_target_pairs={{0,6},{1,7},{2,0},{3,1},{4,2},{5,3},{6,4},{7,5},{8,14},{9,15},{10,... | collective-permute-start | bytes 7864328 | tf_op jit(solution)/shard_map/ppermute | solution.py:94
  74.0 58.4 %collective-permute-start.19 = (bf16[2,256,2560]{2,1,0:T(8,128)(2,1)S(1)}, bf16[2,256,2560]{2,1,0:T(8,128)(2,1)S(1)}, u32[]{:S(2)}, u32[]{:S(2)}) collective-permute-start(bf16[2,256,2560]{2,1,0:T(8,128)(2,1)S(1)} %bitcast.453), channel_id=1, source_target_pairs={{0,2},{1,3},{2,4},{3,5},{4,6},{5,7},{6,0},{7,1},{8,10},{9,11},{10,... | collective-permute-start | bytes 7864328 | tf_op jit(solution)/shard_map/ppermute | solution.py:94
  112.9 148.3 %collective-permute-start.27 = (bf16[1024,1280]{1,0:T(8,128)(2,1)}, bf16[1024,1280]{1,0:T(8,128)(2,1)}, u32[]{:S(2)}, u32[]{:S(2)}) collective-permute-start(bf16[1024,1280]{1,0:T(8,128)(2,1)} %pad_maximum_fusion.5), channel_id=1, source_target_pairs={{0,64},{64,0},{1,65},{65,1},{2,66},{66,2},{3,67},{67,3},{4,68},{68... | collective-permute-start | bytes 7864328 | tf_op jit(solution)/shard_map/ppermute | solution.py:106
  128.7 39.5 %collective-permute-start.34 = (bf16[256,2560]{1,0:T(8,128)(2,1)}, bf16[256,2560]{1,0:T(8,128)(2,1)}, u32[]{:S(2)}, u32[]{:S(2)}) collective-permute-start(bf16[256,2560]{1,0:T(8,128)(2,1)} %get-tuple-element.90), channel_id=1, source_target_pairs={{0,6},{1,7},{2,0},{3,1},{4,2},{5,3},{6,4},{7,5},{8,14},{9,15},{10,... | collective-permute-start | bytes 3932168 | tf_op jit(solution)/shard_map/ppermute | solution.py:94
  168.0 83.7 %collective-permute-start.23 = (bf16[1024,2560]{1,0:T(8,128)(2,1)}, bf16[1024,2560]{1,0:T(8,128)(2,1)}, u32[]{:S(2)}, u32[]{:S(2)}) collective-permute-start(bf16[1024,2560]{1,0:T(8,128)(2,1)} %pad_maximum_fusion), channel_id=1, source_target_pairs={{0,64},{64,0},{1,65},{65,1},{2,66},{66,2},{3,67},{67,3},{4,68},{68... | collective-permute-start | bytes 15728648 | tf_op jit(solution)/shard_map/ppermute | solution.py:106
  172.9 143.8 %collective-permute-start.35 = (bf16[1024,2560]{1,0:T(8,128)(2,1)}, bf16[1024,2560]{1,0:T(8,128)(2,1)}, u32[]{:S(2)}, u32[]{:S(2)}) collective-permute-start(bf16[1024,2560]{1,0:T(8,128)(2,1)} %pad_maximum_fusion.1), channel_id=1, source_target_pairs={{0,64},{64,0},{1,65},{65,1},{2,66},{66,2},{3,67},{67,3},{4,68},{68... | collective-permute-start | bytes 15728648 | tf_op jit(solution)/shard_map/ppermute | solution.py:106
  193.1 31.0 %collective-permute-start.16 = (bf16[2,640,512]{2,1,0:T(8,128)(2,1)}, bf16[2,640,512]{2,1,0:T(8,128)(2,1)}, u32[]{:S(2)}, u32[]{:S(2)}) collective-permute-start(bf16[2,640,512]{2,1,0:T(8,128)(2,1)} %bitcast.50), channel_id=1, source_target_pairs={{0,16},{8,24},{16,32},{24,40},{32,48},{40,56},{48,0},{56,8},{1,17}... | collective-permute-start | bytes 3932168 | tf_op jit(solution)/shard_map/ppermute | solution.py:90
  193.1 33.3 %collective-permute-start.17 = (bf16[2,640,512]{2,1,0:T(8,128)(2,1)}, bf16[2,640,512]{2,1,0:T(8,128)(2,1)}, u32[]{:S(2)}, u32[]{:S(2)}) collective-permute-start(bf16[2,640,512]{2,1,0:T(8,128)(2,1)} %bitcast.50), channel_id=1, source_target_pairs={{0,48},{8,56},{16,0},{24,8},{32,16},{40,24},{48,32},{56,40},{1,49}... | collective-permute-start | bytes 3932168 | tf_op jit(solution)/shard_map/ppermute | solution.py:90
  369.9 55.4 %collective-permute-start.42 = (bf16[640,512]{1,0:T(8,128)(2,1)}, bf16[640,512]{1,0:T(8,128)(2,1)}, u32[]{:S(2)}, u32[]{:S(2)}) collective-permute-start(bf16[640,512]{1,0:T(8,128)(2,1)} %convolution_convert_fusion.24), channel_id=1, source_target_pairs={{0,16},{8,24},{16,32},{24,40},{32,48},{40,56},{48,0},{56,8},{1,17}... | collective-permute-start | bytes 1966088 | tf_op jit(solution)/shard_map/ppermute | solution.py:90
  386.1 41.4 %collective-permute-start.44 = (bf16[640,512]{1,0:T(8,128)(2,1)}, bf16[640,512]{1,0:T(8,128)(2,1)}, u32[]{:S(2)}, u32[]{:S(2)}) collective-permute-start(bf16[640,512]{1,0:T(8,128)(2,1)} %fusion.72), channel_id=1, source_target_pairs={{0,48},{8,56},{16,0},{24,8},{32,16},{40,24},{48,32},{56,40},{1,49}... | collective-permute-start | bytes 1966088 | tf_op jit(solution)/shard_map/ppermute | solution.py:90
  405.1 32.0 %collective-permute-start.40 = (bf16[256,2560]{1,0:T(8,128)(2,1)}, bf16[256,2560]{1,0:T(8,128)(2,1)}, u32[]{:S(2)}, u32[]{:S(2)}) collective-permute-start(bf16[256,2560]{1,0:T(8,128)(2,1)} %fusion.36), channel_id=1, source_target_pairs={{0,2},{1,3},{2,4},{3,5},{4,6},{5,7},{6,0},{7,1},{8,10},{9,11},{10,... | collective-permute-start | bytes 3932168 | tf_op jit(solution)/shard_map/ppermute | solution.py:94
  411.3 29.9 %collective-permute-start.41 = (bf16[256,2560]{1,0:T(8,128)(2,1)}, bf16[256,2560]{1,0:T(8,128)(2,1)}, u32[]{:S(2)}, u32[]{:S(2)}) collective-permute-start(bf16[256,2560]{1,0:T(8,128)(2,1)} %fusion.33), channel_id=1, source_target_pairs={{0,6},{1,7},{2,0},{3,1},{4,2},{5,3},{6,4},{7,5},{8,14},{9,15},{10,... | collective-permute-start | bytes 3932168 | tf_op jit(solution)/shard_map/ppermute | solution.py:94
  424.2 231.4 %collective-permute-start.77 = (bf16[128,2048]{1,0:T(8,128)(2,1)}, bf16[128,2048]{1,0:T(8,128)(2,1)}, u32[]{:S(2)}, u32[]{:S(2)}) collective-permute-start(bf16[128,2048]{1,0:T(8,128)(2,1)} %pad_maximum_fusion.27), channel_id=1, source_target_pairs={{0,64},{64,0},{1,65},{65,1},{2,66},{66,2},{3,67},{67,3},{4,68},{68... | collective-permute-start | bytes 1572872 | tf_op jit(solution)/shard_map/ppermute | solution.py:106
  465.7 30.5 %collective-permute-start.59 = (bf16[128,3072]{1,0:T(8,128)(2,1)}, bf16[128,3072]{1,0:T(8,128)(2,1)}, u32[]{:S(2)}, u32[]{:S(2)}) collective-permute-start(bf16[128,3072]{1,0:T(8,128)(2,1)} %pad_maximum_fusion.22), channel_id=1, source_target_pairs={{0,64},{64,0},{1,65},{65,1},{2,66},{66,2},{3,67},{67,3},{4,68},{68... | collective-permute-start | bytes 2359304 | tf_op jit(solution)/shard_map/ppermute | solution.py:106
  524.2 62.2 %collective-permute-start.64 = (bf16[640,512]{1,0:T(8,128)(2,1)}, bf16[640,512]{1,0:T(8,128)(2,1)}, u32[]{:S(2)}, u32[]{:S(2)}) collective-permute-start(bf16[640,512]{1,0:T(8,128)(2,1)} %convolution_convert_fusion.20), channel_id=1, source_target_pairs={{0,16},{8,24},{16,32},{24,40},{32,48},{40,56},{48,0},{56,8},{1,17}... | collective-permute-start | bytes 1966088 | tf_op jit(solution)/shard_map/ppermute | solution.py:90
  529.8 58.3 %collective-permute-start.66 = (bf16[640,512]{1,0:T(8,128)(2,1)}, bf16[640,512]{1,0:T(8,128)(2,1)}, u32[]{:S(2)}, u32[]{:S(2)}) collective-permute-start(bf16[640,512]{1,0:T(8,128)(2,1)} %fusion.66), channel_id=1, source_target_pairs={{0,48},{8,56},{16,0},{24,8},{32,16},{40,24},{48,32},{56,40},{1,49}... | collective-permute-start | bytes 1966088 | tf_op jit(solution)/shard_map/ppermute | solution.py:90
  537.0 70.5 %collective-permute-start.62 = (bf16[256,2560]{1,0:T(8,128)(2,1)}, bf16[256,2560]{1,0:T(8,128)(2,1)}, u32[]{:S(2)}, u32[]{:S(2)}) collective-permute-start(bf16[256,2560]{1,0:T(8,128)(2,1)} %fusion.27), channel_id=1, source_target_pairs={{0,2},{1,3},{2,4},{3,5},{4,6},{5,7},{6,0},{7,1},{8,10},{9,11},{10,... | collective-permute-start | bytes 3932168 | tf_op jit(solution)/shard_map/ppermute | solution.py:94
  542.1 65.3 %collective-permute-start.63 = (bf16[256,2560]{1,0:T(8,128)(2,1)}, bf16[256,2560]{1,0:T(8,128)(2,1)}, u32[]{:S(2)}, u32[]{:S(2)}) collective-permute-start(bf16[256,2560]{1,0:T(8,128)(2,1)} %fusion.24), channel_id=1, source_target_pairs={{0,6},{1,7},{2,0},{3,1},{4,2},{5,3},{6,4},{7,5},{8,14},{9,15},{10,... | collective-permute-start | bytes 3932168 | tf_op jit(solution)/shard_map/ppermute | solution.py:94
  602.7 31.9 %collective-permute-start.72 = (bf16[128,3840]{1,0:T(8,128)(2,1)}, bf16[128,3840]{1,0:T(8,128)(2,1)}, u32[]{:S(2)}, u32[]{:S(2)}) collective-permute-start(bf16[128,3840]{1,0:T(8,128)(2,1)} %slice.1117), channel_id=1, source_target_pairs={{0,8},{8,0},{16,24},{24,16},{32,40},{40,32},{48,56},{56,48},{1,9},... | collective-permute-start | bytes 2949128 | tf_op jit(solution)/shard_map/ppermute | solution.py:98
  632.8 97.1 %collective-permute-start.71 = (bf16[128,960]{1,0:T(8,128)(2,1)S(1)}, bf16[128,960]{1,0:T(8,128)(2,1)S(1)}, u32[]{:S(2)}, u32[]{:S(2)}) collective-permute-start(bf16[128,960]{1,0:T(8,128)(2,1)S(1)} %get-tuple-element.56), channel_id=1, source_target_pairs={{0,64},{64,0},{1,65},{65,1},{2,66},{66,2},{3,67},{67,3},{4,68},{68... | collective-permute-start | bytes 737288 | tf_op jit(solution)/shard_map/ppermute | solution.py:106
  (263 other events, 2552.3 us)
